TPU v7x, 256 devices: a whole 4x4x8 slice. The times are simulated.
256 devices in a mesh: dp: 2 (over x_hi), dap: 128 (over x_lo, z, y, core).
Axes of the slice: x: 4 (x_hi: 2, x_lo: 2; x = x_hi * 2 + x_lo), y: 4, z: 8, core: 2. Of those that a mesh axis runs over, the one named last changes fastest.
Arguments:
- pair: bfloat16 [2, 256, 256, 128], P('dp', 'dap'), may hold values from -6 to 6
- grad_out: bfloat16 [2, 256, 256, 128], P('dp', 'dap'), may hold values from -6 to 6
- w_in: bfloat16 [128, 512], replicated, may hold values from -0.5 to 0.5
- w_gate: bfloat16 [128, 128], replicated, may hold values from -0.5 to 0.5
- w_out: bfloat16 [128, 128], replicated, may hold values from -0.5 to 0.5
- ln_in_gain: float32 [128], replicated, may hold values from 0.1 to 1.9
- ln_in_bias: float32 [128], replicated, may hold values from -2 to 2
- ln_out_gain: float32 [128], replicated, may hold values from 0.1 to 1.9
- ln_out_bias: float32 [128], replicated, may hold values from -2 to 2
Outputs:
- pair_grad: bfloat16 [2, 256, 256, 128], P('dp', 'dap')
- w_in_grad: float32 [128, 512], replicated
- w_gate_grad: float32 [128, 128], replicated
- w_out_grad: float32 [128, 128], replicated
- ln_in_gain_grad: float32 [128], replicated
- ln_in_bias_grad: float32 [128], replicated
- ln_out_gain_grad: float32 [128], replicated
- ln_out_bias_grad: float32 [128], replicated
All inputs are finite; a program needn't handle non-finite values.
Results may differ from a plain program's by a relative error of at most 0.008.
Values may be sent and summed in bfloat16 or wider, within the bound.
No kernel may reach another device: no remote copies, remote signals or barrier semaphores. Data moves between devices by JAX's collectives and lax.ppermute only.
A program may use at most 64 MiB of HBM per device.

v0:
```python
import jax
import jax.numpy as jnp
from jax import lax
from jax.sharding import PartitionSpec as P

EPSILON = 1e-05


def normalize(values, gain, bias, axis):
    center = values - jnp.mean(values, axis=axis, keepdims=True)
    scale_inv = lax.rsqrt(jnp.mean(center * center, axis=axis, keepdims=True) + EPSILON)
    normed_hat = center * scale_inv
    return (normed_hat * gain + bias, normed_hat, scale_inv)


def norm_back(grad_normed, normed_hat, scale_inv, gain, axis):
    scaled = grad_normed * gain
    return scale_inv * (
        scaled
        - jnp.mean(scaled, axis=axis, keepdims=True)
        - normed_hat * jnp.mean(scaled * normed_hat, axis=axis, keepdims=True)
    )


def edge_terms(normed_rows, weights, hidden):
    projected = jnp.einsum(
        "brkc,cf->bfrk", normed_rows, weights, preferred_element_type=jnp.float32
    )
    return (projected[:, :hidden], projected[:, hidden:])


def contract(pieces):
    left_cols, right_cols = pieces
    product = jnp.einsum(
        "bahik,bahjk->bahij", left_cols, right_cols, preferred_element_type=jnp.float32
    ).astype(jnp.bfloat16)
    return (product, left_cols, right_cols)


def contract_back(grads, lefts, rights):
    grad_left = jnp.einsum(
        "bahij,bahjk->bahik", grads, rights, preferred_element_type=jnp.float32
    ).astype(jnp.bfloat16)
    grad_right = jnp.einsum(
        "bahij,bahik->bahjk", grads, lefts, preferred_element_type=jnp.float32
    ).astype(jnp.bfloat16)
    return (grad_left, grad_right)


def contract_pieces(pieces):
    return contract_back(pieces[0], pieces[1], pieces[2])


def on_device(
    pair, grad_out, w_in, w_gate, w_out, ln_in_gain, ln_in_bias, ln_out_gain, ln_out_bias
):
    batch, row_count, full_len, channels = pair.shape
    hidden = w_out.shape[0]
    groups = lax.axis_size("dap")
    share = hidden // groups
    pair_f, pair_hat, pair_scale = normalize(pair.astype(jnp.float32), ln_in_gain, ln_in_bias, 3)
    pair_normed = pair_f.astype(jnp.bfloat16)
    proj_left, gate_left = edge_terms(pair_normed, w_in[:, : 2 * hidden], hidden)
    proj_right, gate_right = edge_terms(pair_normed, w_in[:, 2 * hidden :], hidden)
    sig_left = jax.nn.sigmoid(gate_left)
    sig_right = jax.nn.sigmoid(gate_right)
    left_split = (
        (sig_left * proj_left)
        .astype(jnp.bfloat16)
        .reshape(batch, groups, share, row_count, full_len)
    )
    right_split = (
        (sig_right * proj_right)
        .astype(jnp.bfloat16)
        .reshape(batch, groups, share, row_count, full_len)
    )
    product_cols, left_cols, right_cols = contract(
        (
            lax.all_to_all(left_split, "dap", split_axis=1, concat_axis=3, tiled=True),
            lax.all_to_all(right_split, "dap", split_axis=1, concat_axis=3, tiled=True),
        )
    )
    product_t = lax.all_to_all(
        product_cols, "dap", split_axis=3, concat_axis=1, tiled=True
    ).reshape(batch, hidden, row_count, full_len)
    out_gain_b = ln_out_gain.reshape(1, hidden, 1, 1)
    out_f, out_hat, out_scale = normalize(
        product_t.astype(jnp.float32), out_gain_b, ln_out_bias.reshape(1, hidden, 1, 1), 1
    )
    out_normed = out_f.astype(jnp.bfloat16)
    outlin = jnp.einsum("bhrk,hc->brkc", out_normed, w_out, preferred_element_type=jnp.float32)
    gate = jax.nn.sigmoid(
        jnp.einsum("brkc,cd->brkd", pair_normed, w_gate, preferred_element_type=jnp.float32)
    )
    grad32 = grad_out.astype(jnp.float32)
    grad_lin = (grad32 * gate).astype(jnp.bfloat16)
    grad_gate = (grad32 * outlin * gate * (1.0 - gate)).astype(jnp.bfloat16)
    w_out_part = jnp.einsum(
        "bhrk,brkc->hc", out_normed, grad_lin, preferred_element_type=jnp.float32
    )
    w_gate_part = jnp.einsum(
        "brkc,brkd->cd", pair_normed, grad_gate, preferred_element_type=jnp.float32
    )
    grad_out_normed = jnp.einsum(
        "brkc,hc->bhrk", grad_lin, w_out, preferred_element_type=jnp.float32
    )
    grad_product = norm_back(grad_out_normed, out_hat, out_scale, out_gain_b, 1).astype(
        jnp.bfloat16
    )
    out_gain_part = jnp.sum(grad_out_normed * out_hat, axis=(0, 2, 3))
    out_bias_part = jnp.sum(grad_out_normed, axis=(0, 2, 3))
    head_totals = lax.psum((w_out_part, w_gate_part, out_gain_part, out_bias_part), ("dp", "dap"))
    grad_split = grad_product.reshape(batch, groups, share, row_count, full_len)
    grad_left_cols, grad_right_cols = contract_pieces(
        (
            lax.all_to_all(grad_split, "dap", split_axis=1, concat_axis=3, tiled=True),
            lax.all_to_all(left_split, "dap", split_axis=1, concat_axis=3, tiled=True),
            lax.all_to_all(right_split, "dap", split_axis=1, concat_axis=3, tiled=True),
        )
    )
    grad_left_t, grad_right_t = (
        lax.all_to_all(grad_left_cols, "dap", split_axis=3, concat_axis=1, tiled=True),
        lax.all_to_all(grad_right_cols, "dap", split_axis=3, concat_axis=1, tiled=True),
    )
    left32 = grad_left_t.reshape(batch, hidden, row_count, full_len).astype(jnp.float32)
    right32 = grad_right_t.reshape(batch, hidden, row_count, full_len).astype(jnp.float32)
    grad_projected = jnp.concatenate(
        [
            left32 * sig_left,
            left32 * proj_left * sig_left * (1.0 - sig_left),
            right32 * sig_right,
            right32 * proj_right * sig_right * (1.0 - sig_right),
        ],
        axis=1,
    ).astype(jnp.bfloat16)
    w_in_part = jnp.einsum(
        "brkc,bfrk->cf", pair_normed, grad_projected, preferred_element_type=jnp.float32
    )
    grad_normed = jnp.einsum(
        "bfrk,cf->brkc", grad_projected, w_in, preferred_element_type=jnp.float32
    ) + jnp.einsum("brkd,cd->brkc", grad_gate, w_gate, preferred_element_type=jnp.float32)
    pair_grad = norm_back(grad_normed, pair_hat, pair_scale, ln_in_gain, 3).astype(jnp.bfloat16)
    in_gain_part = jnp.sum(grad_normed * pair_hat, axis=(0, 1, 2))
    in_bias_part = jnp.sum(grad_normed, axis=(0, 1, 2))
    w_in_total, in_gain_total, in_bias_total = lax.psum(
        (w_in_part, in_gain_part, in_bias_part), ("dp", "dap")
    )
    w_out_total, w_gate_total, out_gain_total, out_bias_total = head_totals
    return (
        pair_grad,
        w_in_total,
        w_gate_total,
        w_out_total,
        in_gain_total,
        in_bias_total,
        out_gain_total,
        out_bias_total,
    )


def solution(mesh):
    in_specs = (
        P("dp", "dap", None, None),
        P("dp", "dap", None, None),
        P(),
        P(),
        P(),
        P(),
        P(),
        P(),
        P(),
    )
    out_specs = (P("dp", "dap", None, None), P(), P(), P(), P(), P(), P(), P())
    return jax.shard_map(
        on_device, mesh=mesh, in_specs=in_specs, out_specs=out_specs, check_vma=False
    )
```

profile of v0, /device:TPU:1, one launch (start us, length us, event | category | flops | bytes accessed | tf_op | source)
XLA Modules:
  0.0 394.9 jit_solution(12374260569438579509)
XLA Ops:
  7.2 1.1 convert_reduce_fusion
  8.3 0.2 fusion.25
  8.6 0.6 copy-done.7
  9.2 0.4 convolution_bitcast_fusion
  9.7 0.8 copy.59
  10.5 14.9 %all-to-all-start.1 = ((bf16[1,128,1,2,256]{4,3,2,0,1:T(2,128)(2,1)}), bf16[1,128,1,2,256]{4,3,2,0,1:T(2,128)(2,1)S(1)}, u32[]{:S(2)}, u32[]{:S(2)}) async-start(bf16[1,128,1,2,256]{4,3,2,0,1:T(2,128)(2,1)} %copy.59), calls=%async_computation.1 | async-start | bytes 262144 | tf_op jit(solution)/shard_map/all_to_all | solution.py:80
  25.4 0.4 convolution_bitcast_fusion.1
  25.9 0.8 copy.57
  26.7 11.1 %all-to-all-done.1 = bf16[1,128,1,2,256]{4,3,2,0,1:T(2,128)(2,1)S(1)} async-done(((bf16[1,128,1,2,256]{4,3,2,0,1:T(2,128)(2,1)}), bf16[1,128,1,2,256]{4,3,2,0,1:T(2,128)(2,1)S(1)}, u32[]{:S(2)}, u32[]{:S(2)}) %all-to-all-start.1) | async-done | bytes 131104 | tf_op jit(solution)/shard_map/all_to_all | solution.py:80
  37.8 5.6 %all-to-all-start = ((bf16[1,128,1,2,256]{4,3,2,0,1:T(2,128)(2,1)}), bf16[1,128,1,2,256]{4,3,2,0,1:T(2,128)(2,1)S(1)}, u32[]{:S(2)}, u32[]{:S(2)}) async-start(bf16[1,128,1,2,256]{4,3,2,0,1:T(2,128)(2,1)} %copy.57), calls=%async_computation | async-start | bytes 262144 | tf_op jit(solution)/shard_map/all_to_all | solution.py:79
  43.4 12.5 %all-to-all-done = bf16[1,128,1,2,256]{4,3,2,0,1:T(2,128)(2,1)S(1)} async-done(((bf16[1,128,1,2,256]{4,3,2,0,1:T(2,128)(2,1)}), bf16[1,128,1,2,256]{4,3,2,0,1:T(2,128)(2,1)S(1)}, u32[]{:S(2)}, u32[]{:S(2)}) %all-to-all-start) | async-done | bytes 131104 | tf_op jit(solution)/shard_map/all_to_all | solution.py:79
  56.4 0.5 broadcast.152
  56.9 1.4 reduce.19
  58.3 0.7 reshape.345
  59.1 5.7 %all-to-all-start.2 = ((bf16[128,2,256]{2,1,0:T(2,128)(2,1)}), bf16[128,2,256]{2,1,0:T(2,128)(2,1)S(1)}, u32[]{:S(2)}, u32[]{:S(2)}) async-start(bf16[128,2,256]{2,1,0:T(2,128)(2,1)} %reshape.345), calls=%async_computation.2 | async-start | bytes 262144 | tf_op jit(solution)/shard_map/all_to_all | solution.py:83
  64.8 0.3 fusion.2
  65.1 12.2 %all-to-all-done.2 = bf16[128,2,256]{2,1,0:T(2,128)(2,1)S(1)} async-done(((bf16[128,2,256]{2,1,0:T(2,128)(2,1)}), bf16[128,2,256]{2,1,0:T(2,128)(2,1)S(1)}, u32[]{:S(2)}, u32[]{:S(2)}) %all-to-all-start.2) | async-done | bytes 131104 | tf_op jit(solution)/shard_map/all_to_all | solution.py:83
  77.4 0.7 convert_reduce_fusion.1
  78.1 0.3 reduce_sum.110
  78.4 0.4 multiply_reduce_fusion.1
  79.2 0.7 copy-done.2
  79.9 0.4 fusion.33
  80.3 0.3 fusion.37
  80.7 0.8 copy.62
  81.5 5.9 %all-to-all-start.3 = ((bf16[1,128,1,2,256]{4,3,2,0,1:T(2,128)(2,1)}), bf16[1,128,1,2,256]{4,3,2,0,1:T(2,128)(2,1)S(1)}, u32[]{:S(2)}, u32[]{:S(2)}) async-start(bf16[1,128,1,2,256]{4,3,2,0,1:T(2,128)(2,1)} %copy.62), calls=%async_computation.3 | async-start | bytes 262144 | tf_op jit(solution)/shard_map/all_to_all | solution.py:116
  87.3 0.3 fusion.8
  87.7 12.2 %all-to-all-done.3 = bf16[1,128,1,2,256]{4,3,2,0,1:T(2,128)(2,1)S(1)} async-done(((bf16[1,128,1,2,256]{4,3,2,0,1:T(2,128)(2,1)}), bf16[1,128,1,2,256]{4,3,2,0,1:T(2,128)(2,1)S(1)}, u32[]{:S(2)}, u32[]{:S(2)}) %all-to-all-start.3) | async-done | bytes 131104 | tf_op jit(solution)/shard_map/all_to_all | solution.py:116
  100.3 1.4 reduce.21
  101.8 0.7 reshape.349
  102.5 5.6 %all-to-all-start.4 = ((bf16[128,2,256]{2,1,0:T(2,128)(2,1)}), bf16[128,2,256]{2,1,0:T(2,128)(2,1)S(1)}, u32[]{:S(2)}, u32[]{:S(2)}) async-start(bf16[128,2,256]{2,1,0:T(2,128)(2,1)} %reshape.349), calls=%async_computation.4 | async-start | bytes 262144 | tf_op jit(solution)/shard_map/all_to_all | solution.py:122
  108.0 1.0 convolution_bitcast_fusion.5
  109.6 1.4 reduce.20
  111.0 0.7 reshape.347
  111.7 8.8 %all-to-all-done.4 = bf16[128,2,256]{2,1,0:T(2,128)(2,1)S(1)} async-done(((bf16[128,2,256]{2,1,0:T(2,128)(2,1)}), bf16[128,2,256]{2,1,0:T(2,128)(2,1)S(1)}, u32[]{:S(2)}, u32[]{:S(2)}) %all-to-all-start.4) | async-done | bytes 131104 | tf_op jit(solution)/shard_map/all_to_all | solution.py:122
  120.6 5.6 %all-to-all-start.5 = ((bf16[128,2,256]{2,1,0:T(2,128)(2,1)}), bf16[128,2,256]{2,1,0:T(2,128)(2,1)S(1)}, u32[]{:S(2)}, u32[]{:S(2)}) async-start(bf16[128,2,256]{2,1,0:T(2,128)(2,1)} %reshape.347), calls=%async_computation.5 | async-start | bytes 262144 | tf_op jit(solution)/shard_map/all_to_all | solution.py:123
  126.2 1.0 convolution_bitcast_fusion.6
  127.4 0.3 convert.24
  127.8 10.9 %all-to-all-done.5 = bf16[128,2,256]{2,1,0:T(2,128)(2,1)S(1)} async-done(((bf16[128,2,256]{2,1,0:T(2,128)(2,1)}), bf16[128,2,256]{2,1,0:T(2,128)(2,1)S(1)}, u32[]{:S(2)}, u32[]{:S(2)}) %all-to-all-start.5) | async-done | bytes 131104 | tf_op jit(solution)/shard_map/all_to_all | solution.py:123
  138.8 0.3 convert.25
  139.2 1.2 convolution_bitcast_fusion.2
  140.4 0.3 fusion.44
  140.7 0.3 fusion.24
  141.3 73.9 %all-reduce = (f32[128]{0:T(128)}, f32[128]{0:T(128)}, f32[128]{0:T(128)}, f32[128]{0:T(128)}) all-reduce(f32[128]{0:T(128)S(1)} %get-tuple-element.10, f32[128]{0:T(128)S(1)} %get-tuple-element.13, f32[128]{0:T(128)S(1)} %get-tuple-element.8, f32[128]{0:T(128)S(1)} %reduce_sum.119), channel_id=1, replica_groups=mesh['dp'=2,'dap'=128] {'dp','dap'}, use_global_device_ids=true, to_apply=%region_12.0 | all-reduce | flops 512 | bytes 4096 | tf_op jit(solution)/shard_map/psum | solution.py:145
  215.2 1.0 fusion.23
  216.2 168.7 %all-reduce.4.cloned.1.call-done = (f32[128,512]{1,0:T(8,128)}, f32[128,128]{1,0:T(8,128)}, f32[128,128]{1,0:T(8,128)}) async-done(((f32[128,512]{1,0:T(8,128)}, f32[128,128]{1,0:T(8,128)}, f32[128,128]{1,0:T(8,128)}), (f32[128,512]{1,0:T(8,128)}, f32[128,128]{1,0:T(8,128)}, f32[128,128]{1,0:T(8,128)})) %all-reduce.4.cloned.1.call-update) | async-done | bytes 393232 | tf_op jit(solution)/shard_map/psum | solution.py:145
  384.8 1.7 copy.110
  386.5 0.6 copy.111
  387.4 0.6 copy.112
  (50 shorter events, 3.1 us)
Async XLA Ops:
  7.2 72.0 %copy-start = (bf16[128,128]{1,0:T(8,128)(2,1)S(1)}, bf16[128,128]{1,0:T(8,128)(2,1)}, u32[]{:S(2)}) copy-start(bf16[128,128]{1,0:T(8,128)(2,1)} %param.13) | copy-start | bytes 98308
  7.2 1.1 copy-start.1
  7.2 1.4 copy-start.3
  8.5 0.7 copy-start.7
  8.6 0.7 copy-start.10
  10.5 27.3 %all-to-all-start.1 = ((bf16[1,128,1,2,256]{4,3,2,0,1:T(2,128)(2,1)}), bf16[1,128,1,2,256]{4,3,2,0,1:T(2,128)(2,1)S(1)}, u32[]{:S(2)}, u32[]{:S(2)}) async-start(bf16[1,128,1,2,256]{4,3,2,0,1:T(2,128)(2,1)} %copy.59), calls=%async_computation.1 | async-start | bytes 262144 | tf_op jit(solution)/shard_map/all_to_all | solution.py:80
  37.8 18.1 %all-to-all-start = ((bf16[1,128,1,2,256]{4,3,2,0,1:T(2,128)(2,1)}), bf16[1,128,1,2,256]{4,3,2,0,1:T(2,128)(2,1)S(1)}, u32[]{:S(2)}, u32[]{:S(2)}) async-start(bf16[1,128,1,2,256]{4,3,2,0,1:T(2,128)(2,1)} %copy.57), calls=%async_computation | async-start | bytes 262144 | tf_op jit(solution)/shard_map/all_to_all | solution.py:79
  59.1 5.7 %copy-start.6 = (bf16[128,128]{1,0:T(8,128)(2,1)S(1)}, bf16[128,128]{1,0:T(8,128)(2,1)}, u32[]{:S(2)}) copy-start(bf16[128,128]{1,0:T(8,128)(2,1)} %param.12) | copy-start | bytes 98308
  59.1 18.2 %all-to-all-start.2 = ((bf16[128,2,256]{2,1,0:T(2,128)(2,1)}), bf16[128,2,256]{2,1,0:T(2,128)(2,1)S(1)}, u32[]{:S(2)}, u32[]{:S(2)}) async-start(bf16[128,2,256]{2,1,0:T(2,128)(2,1)} %reshape.345), calls=%async_computation.2 | async-start | bytes 262144 | tf_op jit(solution)/shard_map/all_to_all | solution.py:83
  79.0 0.9 copy-start.2
  79.0 0.9 copy-start.8
  81.5 5.9 %copy-start.9 = (f32[128]{0:T(128)S(1)}, f32[128]{0:T(128)}, u32[]{:S(2)}) copy-start(f32[128]{0:T(128)} %param.17) | copy-start | bytes 1540
  81.5 18.4 %all-to-all-start.3 = ((bf16[1,128,1,2,256]{4,3,2,0,1:T(2,128)(2,1)}), bf16[1,128,1,2,256]{4,3,2,0,1:T(2,128)(2,1)S(1)}, u32[]{:S(2)}, u32[]{:S(2)}) async-start(bf16[1,128,1,2,256]{4,3,2,0,1:T(2,128)(2,1)} %copy.62), calls=%async_computation.3 | async-start | bytes 262144 | tf_op jit(solution)/shard_map/all_to_all | solution.py:116
  102.5 18.1 %all-to-all-start.4 = ((bf16[128,2,256]{2,1,0:T(2,128)(2,1)}), bf16[128,2,256]{2,1,0:T(2,128)(2,1)S(1)}, u32[]{:S(2)}, u32[]{:S(2)}) async-start(bf16[128,2,256]{2,1,0:T(2,128)(2,1)} %reshape.349), calls=%async_computation.4 | async-start | bytes 262144 | tf_op jit(solution)/shard_map/all_to_all | solution.py:122
  120.6 18.1 %all-to-all-start.5 = ((bf16[128,2,256]{2,1,0:T(2,128)(2,1)}), bf16[128,2,256]{2,1,0:T(2,128)(2,1)S(1)}, u32[]{:S(2)}, u32[]{:S(2)}) async-start(bf16[128,2,256]{2,1,0:T(2,128)(2,1)} %reshape.347), calls=%async_computation.5 | async-start | bytes 262144 | tf_op jit(solution)/shard_map/all_to_all | solution.py:123
  126.1 258.7 %all-reduce.4.cloned.1.call-start = ((), (), s32[]{:S(2)}) async-start(), calls=%async_computation.6 | async-start | bytes 786432 | tf_op jit(solution)/shard_map/psum | solution.py:145
  384.8 1.7 copy-start.5
  386.5 0.9 copy-start.4
Sparse Core Ops, SparseCore 0:
  141.4 243.3 all-reduce.3
where the time goes:
time: 396 us; the launch traced here: 395 us
  waiting for transfers between devices  236 us (60%)
  blocking collectives  73.9 us (19%)
  starting transfers between devices  43.2 us (11%)
  between operations  14.4 us (4%)
  local copies, waits for them, and re-layouts  11.1 us (3%)
  other arithmetic  9.51 us (2%)
  matrix products  6.42 us (2%)
    psum x1, waiting for transfers between devices, on_device(): lax.psum((w_in_part, in_gain_part, in_bias_part), ('dp', 'dap'))  169 us
    psum x1, blocking collectives, on_device(): lax.psum((w_in_part, in_gain_part, in_bias_part), ('dp', 'dap'))  73.9 us
    all_to_all x1, starting transfers between devices, on_device(): lax.all_to_all(right_split, 'dap', split_axis=1, concat_axis=3, tiled=True)  14.9 us
    all_to_all x1, waiting for transfers between devices, on_device(): lax.all_to_all(left_split, 'dap', split_axis=1, concat_axis=3, tiled=True)  12.5 us
    all_to_all x1, waiting for transfers between devices, on_device(): lax.all_to_all(grad_split, 'dap', split_axis=1, concat_axis=3, tiled=True)  12.2 us
    all_to_all x1, waiting for transfers between devices, on_device(): lax.all_to_all(product_cols, 'dap', split_axis=3, concat_axis=1, tiled=True)  12.2 us
    all_to_all x1, waiting for transfers between devices, on_device(): lax.all_to_all(right_split, 'dap', split_axis=1, concat_axis=3, tiled=True)  11.1 us
    all_to_all x1, waiting for transfers between devices, on_device(): lax.all_to_all(grad_right_cols, 'dap', split_axis=3, concat_axis=1, tiled...  10.9 us
  transfers between devices with their start and end apart: 7, of which 7 were waited for; matrix products, arithmetic and copies ran while one was open for 2% of the time, Pallas kernels for 0%

commit v1 on v0

--- a/solution.py
+++ b/solution.py
@@ -1,9 +1,11 @@
 import jax
 import jax.numpy as jnp
 from jax import lax
-from jax.sharding import PartitionSpec as P
+from jax.sharding import Mesh, PartitionSpec as P
 
 EPSILON = 1e-05
+DAP = ("x", "z", "y", "c")
+PEERS = ("X", "x", "z", "y")
 
 
 def normalize(values, gain, bias, axis):
@@ -29,26 +31,31 @@
     return (projected[:, :hidden], projected[:, hidden:])
 
 
-def contract(pieces):
-    left_cols, right_cols = pieces
-    product = jnp.einsum(
-        "bahik,bahjk->bahij", left_cols, right_cols, preferred_element_type=jnp.float32
-    ).astype(jnp.bfloat16)
-    return (product, left_cols, right_cols)
-
-
-def contract_back(grads, lefts, rights):
-    grad_left = jnp.einsum(
-        "bahij,bahjk->bahik", grads, rights, preferred_element_type=jnp.float32
-    ).astype(jnp.bfloat16)
-    grad_right = jnp.einsum(
-        "bahij,bahik->bahjk", grads, lefts, preferred_element_type=jnp.float32
-    ).astype(jnp.bfloat16)
-    return (grad_left, grad_right)
-
-
-def contract_pieces(pieces):
-    return contract_back(pieces[0], pieces[1], pieces[2])
+def total_over_devices(matrices, vectors):
+    core = lax.axis_index("c")
+    swap = [(0, 1), (1, 0)]
+    rows, width = matrices.shape
+    half = rows // 2
+    peers = lax.axis_size(PEERS)
+    parts = matrices.reshape(2, peers, half * width // peers // 128, 128)
+    vec = vectors.reshape(2, peers, 1, vectors.size // 2 // peers)
+    vec = jnp.pad(vec, ((0, 0), (0, 0), (0, 0), (0, 128 - vec.shape[-1])))
+    parts = jnp.concatenate([parts, vec], axis=2)
+    keep = jnp.where(core == 0, parts[0], parts[1])
+    give = jnp.where(core == 0, parts[1], parts[0])
+    keep = keep + lax.ppermute(give, "c", swap)
+    share = lax.all_to_all(keep, PEERS, 0, 0, tiled=True)
+    share = jnp.sum(share, axis=0, keepdims=True)
+    mine = lax.all_to_all(
+        jnp.broadcast_to(share, keep.shape), PEERS, 0, 0, tiled=True
+    )
+    other = lax.ppermute(mine, "c", swap)
+    low = jnp.where(core == 0, mine, other)
+    high = jnp.where(core == 0, other, mine)
+    both = jnp.stack([low, high])
+    total = both[:, :, :-1].reshape(rows, width)
+    vec_total = both[:, :, -1, : vectors.size // 2 // peers].reshape(vectors.shape)
+    return total, vec_total
 
 
 def on_device(
@@ -56,7 +63,7 @@
 ):
     batch, row_count, full_len, channels = pair.shape
     hidden = w_out.shape[0]
-    groups = lax.axis_size("dap")
+    groups = lax.axis_size(DAP)
     share = hidden // groups
     pair_f, pair_hat, pair_scale = normalize(pair.astype(jnp.float32), ln_in_gain, ln_in_bias, 3)
     pair_normed = pair_f.astype(jnp.bfloat16)
@@ -74,14 +81,15 @@
         .astype(jnp.bfloat16)
         .reshape(batch, groups, share, row_count, full_len)
     )
-    product_cols, left_cols, right_cols = contract(
-        (
-            lax.all_to_all(left_split, "dap", split_axis=1, concat_axis=3, tiled=True),
-            lax.all_to_all(right_split, "dap", split_axis=1, concat_axis=3, tiled=True),
-        )
-    )
+    edges = jnp.stack([left_split[0, :, 0], right_split[0, :, 0]], axis=1)
+    edge_cols = lax.all_to_all(edges, DAP, 0, 0, tiled=True)
+    left_cols = edge_cols[:, 0].reshape(full_len, full_len)
+    right_cols = edge_cols[:, 1].reshape(full_len, full_len)
+    product_cols = jnp.einsum(
+        "ik,jk->ij", left_cols, right_cols, preferred_element_type=jnp.float32
+    ).astype(jnp.bfloat16)
     product_t = lax.all_to_all(
-        product_cols, "dap", split_axis=3, concat_axis=1, tiled=True
+        product_cols.reshape(groups, row_count, full_len), DAP, 0, 0, tiled=True
     ).reshape(batch, hidden, row_count, full_len)
     out_gain_b = ln_out_gain.reshape(1, hidden, 1, 1)
     out_f, out_hat, out_scale = normalize(
@@ -109,19 +117,25 @@
     )
     out_gain_part = jnp.sum(grad_out_normed * out_hat, axis=(0, 2, 3))
     out_bias_part = jnp.sum(grad_out_normed, axis=(0, 2, 3))
-    head_totals = lax.psum((w_out_part, w_gate_part, out_gain_part, out_bias_part), ("dp", "dap"))
-    grad_split = grad_product.reshape(batch, groups, share, row_count, full_len)
-    grad_left_cols, grad_right_cols = contract_pieces(
-        (
-            lax.all_to_all(grad_split, "dap", split_axis=1, concat_axis=3, tiled=True),
-            lax.all_to_all(left_split, "dap", split_axis=1, concat_axis=3, tiled=True),
-            lax.all_to_all(right_split, "dap", split_axis=1, concat_axis=3, tiled=True),
-        )
+    grad_cols = lax.all_to_all(
+        grad_product.reshape(groups, row_count, full_len), DAP, 0, 0, tiled=True
+    ).reshape(full_len, full_len)
+    grad_left_cols = jnp.einsum(
+        "ij,jk->ik", grad_cols, right_cols, preferred_element_type=jnp.float32
+    ).astype(jnp.bfloat16)
+    grad_right_cols = jnp.einsum(
+        "ij,ik->jk", grad_cols, left_cols, preferred_element_type=jnp.float32
+    ).astype(jnp.bfloat16)
+    grad_edge_cols = jnp.stack(
+        [
+            grad_left_cols.reshape(groups, row_count, full_len),
+            grad_right_cols.reshape(groups, row_count, full_len),
+        ],
+        axis=1,
     )
-    grad_left_t, grad_right_t = (
-        lax.all_to_all(grad_left_cols, "dap", split_axis=3, concat_axis=1, tiled=True),
-        lax.all_to_all(grad_right_cols, "dap", split_axis=3, concat_axis=1, tiled=True),
-    )
+    grad_edges = lax.all_to_all(grad_edge_cols, DAP, 0, 0, tiled=True)
+    grad_left_t = grad_edges[:, 0]
+    grad_right_t = grad_edges[:, 1]
     left32 = grad_left_t.reshape(batch, hidden, row_count, full_len).astype(jnp.float32)
     right32 = grad_right_t.reshape(batch, hidden, row_count, full_len).astype(jnp.float32)
     grad_projected = jnp.concatenate(
@@ -142,10 +156,14 @@
     pair_grad = norm_back(grad_normed, pair_hat, pair_scale, ln_in_gain, 3).astype(jnp.bfloat16)
     in_gain_part = jnp.sum(grad_normed * pair_hat, axis=(0, 1, 2))
     in_bias_part = jnp.sum(grad_normed, axis=(0, 1, 2))
-    w_in_total, in_gain_total, in_bias_total = lax.psum(
-        (w_in_part, in_gain_part, in_bias_part), ("dp", "dap")
+    matrices, vectors = total_over_devices(
+        jnp.concatenate([w_in_part, w_gate_part, w_out_part], axis=1),
+        jnp.stack([in_gain_part, in_bias_part, out_gain_part, out_bias_part]),
     )
-    w_out_total, w_gate_total, out_gain_total, out_bias_total = head_totals
+    w_in_total = matrices[:, : 4 * hidden]
+    w_gate_total = matrices[:, 4 * hidden : 4 * hidden + channels]
+    w_out_total = matrices[:, 4 * hidden + channels :]
+    in_gain_total, in_bias_total, out_gain_total, out_bias_total = vectors
     return (
         pair_grad,
         w_in_total,
@@ -159,9 +177,11 @@
 
 
 def solution(mesh):
+    fine = Mesh(mesh.devices.reshape(2, 2, 8, 4, 2), ("X", "x", "z", "y", "c"))
+    cells = P("X", DAP, None, None)
     in_specs = (
-        P("dp", "dap", None, None),
-        P("dp", "dap", None, None),
+        cells,
+        cells,
         P(),
         P(),
         P(),
@@ -170,7 +190,7 @@
         P(),
         P(),
     )
-    out_specs = (P("dp", "dap", None, None), P(), P(), P(), P(), P(), P(), P())
+    out_specs = (cells, P(), P(), P(), P(), P(), P(), P())
     return jax.shard_map(
-        on_device, mesh=mesh, in_specs=in_specs, out_specs=out_specs, check_vma=False
+        on_device, mesh=fine, in_specs=in_specs, out_specs=out_specs, check_vma=False
     )

time: 396 us -> 147 us (0.37)
  waiting for transfers between devices: 236 us -> 38.9 us
  starting transfers between devices: 43.2 us -> 22.4 us
  between operations: 14.4 us -> 1.06 us
  blocking collectives: 73.9 us -> 66.8 us
  other arithmetic: 9.51 us -> 5.39 us
    psum x1 -> x0, waiting for transfers between devices: 169 us -> none  [on_device(): lax.psum((w_in_part, in_gain_part, in_bias_part), ('dp', 'dap'))]
    psum x1 -> x0, blocking collectives: 73.9 us -> none  [on_device(): lax.psum((w_in_part, in_gain_part, in_bias_part), ('dp', 'dap'))]
    all_to_all x0 -> x3, blocking collectives: none -> 66.8 us  [the longest x1 29.8 us: on_device(): edge_cols = lax.all_to_all(edges, DAP, 0, 0, tiled=True)]
    all_to_all x6 -> x3, waiting for transfers between devices: 67.7 us -> 37.5 us  [the longest x1 13.4 us: on_device(): grad_edges = lax.all_to_all(grad_edge_cols, DAP, 0, 0, tiled=True)]
    all_to_all x6 -> x3, starting transfers between devices: 43.1 us -> 18.2 us  [the longest x1 6.96 us: total_over_devices(): lax.all_to_all(jnp.broadcast_to(share, keep.shape), PEERS, 0, 0, tiled=True)]
    unnamed x32 -> x18, local copies, waits for them, and re-layouts: 7.55 us -> 1.88 us
    unnamed x3 -> x0, other arithmetic: 4.22 us -> none
    ppermute x0 -> x2, starting transfers between devices: none -> 4.15 us  [the longest x1 3.68 us: total_over_devices(): other = lax.ppermute(mine, 'c', swap)]
  transfers between devices with their start and end apart: 7 -> 5, of which waited for: 7 -> 5; matrix products, arithmetic and copies ran while one was open for 2% -> 2% of each run, Pallas kernels for 0% -> 0%
where the time goes in v1:
time: 147 us
  blocking collectives  66.8 us (45%)
  waiting for transfers between devices  38.9 us (26%)
  starting transfers between devices  22.4 us (15%)
  local copies, waits for them, and re-layouts  8.03 us (5%)
  other arithmetic  5.39 us (4%)
  matrix products  4.48 us (3%)
    all_to_all x1, blocking collectives, on_device(): edge_cols = lax.all_to_all(edges, DAP, 0, 0, tiled=True)  29.8 us
    all_to_all x1, blocking collectives, total_over_devices(): share = lax.all_to_all(keep, PEERS, 0, 0, tiled=True)  19.5 us
    all_to_all x1, blocking collectives, on_device(): lax.all_to_all(grad_product.reshape(groups, row_count, full_len), DAP, 0,...  17.4 us
    all_to_all x1, waiting for transfers between devices, on_device(): grad_edges = lax.all_to_all(grad_edge_cols, DAP, 0, 0, tiled=True)  13.4 us
    all_to_all x1, waiting for transfers between devices, on_device(): lax.all_to_all(product_cols.reshape(groups, row_count, full_len), DAP, 0,...  12.2 us
    all_to_all x1, waiting for transfers between devices, total_over_devices(): lax.all_to_all(jnp.broadcast_to(share, keep.shape), PEERS, 0, 0, tiled=True)  11.9 us
    all_to_all x1, starting transfers between devices, total_over_devices(): lax.all_to_all(jnp.broadcast_to(share, keep.shape), PEERS, 0, 0, tiled=True)  6.96 us
    all_to_all x1, starting transfers between devices, on_device(): lax.all_to_all(product_cols.reshape(groups, row_count, full_len), DAP, 0,...  5.69 us
  transfers between devices with their start and end apart: 5, of which 5 were waited for; matrix products, arithmetic and copies ran while one was open for 2% of the time, Pallas kernels for 0%

profile of v1, /device:TPU:1, one launch (start us, length us, event | category | flops | bytes accessed | tf_op | source)
XLA Modules:
  0.0 147.0 jit_solution(585652083076847348)
XLA Ops:
  0.7 1.1 convert_reduce_fusion.1
  1.8 0.2 fusion.35
  2.1 0.6 copy-done.5
  2.7 0.4 convolution_bitcast_fusion
  3.1 0.4 convolution_bitcast_fusion.1
  3.7 0.3 copy.48
  4.0 29.8 %all_to_all.30 = bf16[128,2,2,256]{3,2,1,0:T(2,128)(2,1)S(1)} all-to-all(bf16[128,2,2,256]{3,2,1,0:T(2,128)(2,1)S(1)} %copy.48), channel_id=1, replica_groups=mesh['X'=2,'x'=2,'z'=8,'y'=4,'c'=2] {'x','z','y','c'}, dimensions={0} | all-to-all | bytes 524288 | tf_op jit(solution)/shard_map/all_to_all | solution.py:85
  33.8 0.2 fusion.86
  34.1 0.2 convolution_convert_fusion.2
  34.3 0.7 reshape.247
  35.0 5.7 %all-to-all-start.1 = ((bf16[128,2,256]{2,1,0:T(2,128)(2,1)}), bf16[128,2,256]{2,1,0:T(2,128)(2,1)S(1)}, u32[]{:S(2)}, u32[]{:S(2)}) async-start(bf16[128,2,256]{2,1,0:T(2,128)(2,1)} %reshape.247), calls=%async_computation.1 | async-start | bytes 262144 | tf_op jit(solution)/shard_map/all_to_all | solution.py:91
  40.7 0.3 fusion.2
  41.1 12.2 %all-to-all-done.1 = bf16[128,2,256]{2,1,0:T(2,128)(2,1)S(1)} async-done(((bf16[128,2,256]{2,1,0:T(2,128)(2,1)}), bf16[128,2,256]{2,1,0:T(2,128)(2,1)S(1)}, u32[]{:S(2)}, u32[]{:S(2)}) %all-to-all-start.1) | async-done | bytes 131104 | tf_op jit(solution)/shard_map/all_to_all | solution.py:91
  53.5 0.3 fusion.27
  53.8 0.5 copy-done.2
  54.5 0.4 fusion.26
  54.9 0.3 fusion.23
  55.4 17.4 %all_to_all.31 = bf16[128,2,256]{2,1,0:T(2,128)(2,1)S(1)} all-to-all(bf16[128,2,256]{2,1,0:T(2,128)(2,1)S(1)} %copy.50), channel_id=1, replica_groups=mesh['X'=2,'x'=2,'z'=8,'y'=4,'c'=2] {'x','z','y','c'}, dimensions={0} | all-to-all | bytes 262144 | tf_op jit(solution)/shard_map/all_to_all | solution.py:120
  72.9 0.2 convolution_convert_fusion
  73.1 0.2 convolution_convert_fusion.1
  73.4 0.4 pad_maximum_fusion.3
  73.8 0.9 copy.51
  74.7 5.6 %all-to-all-start.3 = ((bf16[128,2,2,256]{3,2,1,0:T(2,128)(2,1)}), bf16[128,2,2,256]{3,2,1,0:T(2,128)(2,1)S(1)}, u32[]{:S(2)}, u32[]{:S(2)}) async-start(bf16[128,2,2,256]{3,2,1,0:T(2,128)(2,1)} %copy.51), calls=%async_computation.3 | async-start | bytes 524288 | tf_op jit(solution)/shard_map/all_to_all | solution.py:136
  80.4 0.6 copy-done.8
  80.9 0.3 fusion.7
  81.3 0.4 convolution_bitcast_fusion.5
  81.7 0.4 convolution_bitcast_fusion.4
  82.1 13.4 %all-to-all-done.3 = bf16[128,2,2,256]{3,2,1,0:T(2,128)(2,1)S(1)} async-done(((bf16[128,2,2,256]{3,2,1,0:T(2,128)(2,1)}), bf16[128,2,2,256]{3,2,1,0:T(2,128)(2,1)S(1)}, u32[]{:S(2)}, u32[]{:S(2)}) %all-to-all-start.3) | async-done | bytes 262176 | tf_op jit(solution)/shard_map/all_to_all | solution.py:136
  95.5 0.2 fusion.85
  96.0 0.5 convolution_bitcast_fusion.2
  96.5 0.3 fusion.61
  96.8 0.3 fusion.34
  97.5 0.2 reshape.251
  97.7 0.3 select_maximum_fusion
  98.1 0.5 collective-permute-start
  98.6 1.2 collective-permute-done
  99.9 19.5 %all_to_all.32 = f32[128,4,128]{2,1,0:T(4,128)S(1)} all-to-all(f32[128,4,128]{2,1,0:T(4,128)S(1)} %bitcast_add_fusion), channel_id=1, replica_groups=mesh['X'=2,'x'=2,'z'=8,'y'=4,'c'=2] {'X','x','z','y'}, dimensions={0} | all-to-all | bytes 524288 | tf_op jit(solution)/shard_map/all_to_all | solution.py:47
  119.5 0.7 broadcast_in_dim.2
  120.3 7.0 %all-to-all-start.5 = ((f32[128,4,128]{2,1,0:T(4,128)}), f32[128,4,128]{2,1,0:T(4,128)S(1)}, u32[]{:S(2)}, u32[]{:S(2)}) async-start(f32[128,4,128]{2,1,0:T(4,128)} %broadcast_in_dim.2), calls=%async_computation.5 | async-start | bytes 524288 | tf_op jit(solution)/shard_map/all_to_all | solution.py:49
  127.3 11.9 %all-to-all-done.5 = f32[128,4,128]{2,1,0:T(4,128)S(1)} async-done(((f32[128,4,128]{2,1,0:T(4,128)}), f32[128,4,128]{2,1,0:T(4,128)S(1)}, u32[]{:S(2)}, u32[]{:S(2)}) %all-to-all-start.5) | async-done | bytes 262176 | tf_op jit(solution)/shard_map/all_to_all | solution.py:49
  139.2 3.7 %collective-permute-start.1 = (f32[128,4,128]{2,1,0:T(4,128)S(1)}, f32[128,4,128]{2,1,0:T(4,128)S(1)}, u32[]{:S(2)}, u32[]{:S(2)}) collective-permute-start(f32[128,4,128]{2,1,0:T(4,128)S(1)} %all-to-all-done.5), channel_id=1, source_target_pairs={{0,1},{1,0},{2,3},{3,2},{4,5},{5,4},{6,7},{7,6},{8,9},{9,8},{10,11... | collective-permute-start | bytes 786440 | tf_op jit(solution)/shard_map/ppermute | solution.py:52
  142.9 1.0 fusion.33
  143.9 0.2 collective-permute-done.1
  144.1 0.4 fusion.60
  144.7 0.2 reshape.253
  144.9 0.7 fusion.84
  145.6 0.7 slice.82
  146.4 0.5 slice_bitcast_fusion
  (46 shorter events, 2.4 us)
Async XLA Ops:
  0.6 53.2 %copy-start = (bf16[128,128]{1,0:T(8,128)(2,1)S(1)}, bf16[128,128]{1,0:T(8,128)(2,1)}, u32[]{:S(2)}) copy-start(bf16[128,128]{1,0:T(8,128)(2,1)} %param.13) | copy-start | bytes 98308
  0.6 1.1 copy-start.1
  0.7 1.4 copy-start.3
  2.0 0.7 copy-start.5
  2.0 0.7 copy-start.7
  35.0 5.7 %copy-start.4 = (bf16[128,128]{1,0:T(8,128)(2,1)S(1)}, bf16[128,128]{1,0:T(8,128)(2,1)}, u32[]{:S(2)}) copy-start(bf16[128,128]{1,0:T(8,128)(2,1)} %param.12) | copy-start | bytes 98308
  35.0 18.2 %all-to-all-start.1 = ((bf16[128,2,256]{2,1,0:T(2,128)(2,1)}), bf16[128,2,256]{2,1,0:T(2,128)(2,1)S(1)}, u32[]{:S(2)}, u32[]{:S(2)}) async-start(bf16[128,2,256]{2,1,0:T(2,128)(2,1)} %reshape.247), calls=%async_computation.1 | async-start | bytes 262144 | tf_op jit(solution)/shard_map/all_to_all | solution.py:91
  53.4 0.9 copy-start.2
  53.8 0.7 copy-start.6
  74.7 20.8 %all-to-all-start.3 = ((bf16[128,2,2,256]{3,2,1,0:T(2,128)(2,1)}), bf16[128,2,2,256]{3,2,1,0:T(2,128)(2,1)S(1)}, u32[]{:S(2)}, u32[]{:S(2)}) async-start(bf16[128,2,2,256]{3,2,1,0:T(2,128)(2,1)} %copy.51), calls=%async_computation.3 | async-start | bytes 524288 | tf_op jit(solution)/shard_map/all_to_all | solution.py:136
  80.3 0.7 copy-start.8
  98.1 1.6 %collective-permute-start = (f32[128,4,128]{2,1,0:T(4,128)S(1)}, f32[128,4,128]{2,1,0:T(4,128)S(1)}, u32[]{:S(2)}, u32[]{:S(2)}) collective-permute-start(f32[128,4,128]{2,1,0:T(4,128)S(1)} %select_bitcast_fusion.2), channel_id=1, source_target_pairs={{0,1},{1,0},{2,3},{3,2},{4,5},{5,4},{6,7},{7,6},{8,9},{9,8},{10,11... | collective-permute-start | bytes 786440 | tf_op jit(solution)/shard_map/ppermute | solution.py:46
  120.3 18.9 %all-to-all-start.5 = ((f32[128,4,128]{2,1,0:T(4,128)}), f32[128,4,128]{2,1,0:T(4,128)S(1)}, u32[]{:S(2)}, u32[]{:S(2)}) async-start(f32[128,4,128]{2,1,0:T(4,128)} %broadcast_in_dim.2), calls=%async_computation.5 | async-start | bytes 524288 | tf_op jit(solution)/shard_map/all_to_all | solution.py:49
  139.2 4.8 %collective-permute-start.1 = (f32[128,4,128]{2,1,0:T(4,128)S(1)}, f32[128,4,128]{2,1,0:T(4,128)S(1)}, u32[]{:S(2)}, u32[]{:S(2)}) collective-permute-start(f32[128,4,128]{2,1,0:T(4,128)S(1)} %all-to-all-done.5), channel_id=1, source_target_pairs={{0,1},{1,0},{2,3},{3,2},{4,5},{5,4},{6,7},{7,6},{8,9},{9,8},{10,11... | collective-permute-start | bytes 786440 | tf_op jit(solution)/shard_map/ppermute | solution.py:52

commit v2 on v0

v2 whole, which is shorter than its diff:
```python
import functools

import jax
import jax.numpy as jnp
from jax import lax
from jax.experimental import pallas as pl
from jax.experimental.pallas import tpu as pltpu
from jax.sharding import Mesh, PartitionSpec as P

EPSILON = 1e-05
CHIPS = ("x", "z", "y")
PEERS = ("X", "x", "z", "y")
SWAP = [(0, 1), (1, 0)]
LANES = 128
F32 = jnp.float32
BF16 = jnp.bfloat16


def call(body, outs, scratch=(), work=0):
    def run(*operands):
        return pl.pallas_call(
            body,
            out_shape=[jax.ShapeDtypeStruct(shape, dtype) for shape, dtype in outs],
            in_specs=[pl.BlockSpec(memory_space=pltpu.VMEM)] * len(operands),
            out_specs=[pl.BlockSpec(memory_space=pltpu.VMEM)] * len(outs),
            scratch_shapes=[pltpu.VMEM(shape, F32) for shape in scratch],
            compiler_params=pltpu.CompilerParams(vmem_limit_bytes=24 * 1024 * 1024),
            cost_estimate=pl.CostEstimate(
                flops=work, bytes_accessed=1 << 20, transcendentals=0
            ),
        )(*operands)

    return run


def dot_nt(a, b):
    return lax.dot_general(a, b, (((1,), (1,)), ((), ())), preferred_element_type=F32)


def dot_nn(a, b):
    return lax.dot_general(a, b, (((1,), (0,)), ((), ())), preferred_element_type=F32)


def sigmoid(x):
    return jax.nn.sigmoid(x)


def every(start, count, stride):
    return pl.ds(start, count, stride=stride)


def front(pair_ref, w_in_ref, gain_ref, bias_ref, edges_ref, normed_ref, w_in_t_ref, rows):
    cells, channels = pair_ref.shape
    values = pair_ref[...].astype(F32)
    center = values - jnp.mean(values, axis=1, keepdims=True)
    scale = lax.rsqrt(jnp.mean(center * center, axis=1, keepdims=True) + EPSILON)
    normed = (center * scale * gain_ref[...] + bias_ref[...]).astype(BF16)
    normed_ref[...] = normed
    w_in_t = jnp.transpose(w_in_ref[...].astype(F32)).astype(BF16)
    w_in_t_ref[...] = w_in_t
    hidden = w_in_t.shape[0] // 4
    for side in range(2):
        proj = dot_nt(w_in_t[2 * side * hidden : (2 * side + 1) * hidden], normed)
        gate = dot_nt(w_in_t[(2 * side + 1) * hidden : (2 * side + 2) * hidden], normed)
        value = sigmoid(gate) * proj
        for u in range(4):
            rows[every(4 * side + u, hidden, 8), :] = value[:, u * LANES : (u + 1) * LANES]
    edges_ref[...] = rows[...].astype(BF16)


def beside_front(
    normed_ref, pair_ref, grad_ref, w_in_t_ref, w_gate_ref, w_out_ref, gain_ref,
    normed_t_ref, hat_t_ref, scale_ref, factors_ref, grad_t_ref, gate_t_ref, grad_lin_ref,
    grad_out_normed_ref, scaled_ref, mean_ref,
):
    hidden = w_out_ref.shape[0]
    normed = normed_ref[...]
    normed_t_ref[...] = jnp.transpose(normed.astype(F32)).astype(BF16)
    values = jnp.transpose(pair_ref[...].astype(F32))
    center = values - jnp.mean(values, axis=0, keepdims=True)
    scale = lax.rsqrt(jnp.mean(center * center, axis=0, keepdims=True) + EPSILON)
    hat_t_ref[...] = center * scale
    scale_ref[...] = jnp.broadcast_to(scale, scale_ref.shape)
    grad_t = jnp.transpose(grad_ref[...].astype(F32))
    grad_t_ref[...] = grad_t
    w_gate_t = jnp.transpose(w_gate_ref[...].astype(F32)).astype(BF16)
    gate = sigmoid(dot_nt(w_gate_t, normed))
    gate_t_ref[...] = gate
    grad_lin = (grad_t * gate).astype(BF16)
    grad_lin_ref[...] = grad_lin
    grad_out_normed = dot_nn(w_out_ref[...], grad_lin)
    grad_out_normed_ref[...] = grad_out_normed
    scaled = grad_out_normed * gain_ref[...]
    scaled_ref[...] = scaled
    mean_ref[...] = jnp.broadcast_to(jnp.mean(scaled, axis=0, keepdims=True), mean_ref.shape)
    for side in range(2):
        at = 2 * side * hidden
        proj = dot_nt(w_in_t_ref[at : at + hidden, :], normed)
        sig = sigmoid(dot_nt(w_in_t_ref[at + hidden : at + 2 * hidden, :], normed))
        factors_ref[at : at + hidden, :] = sig
        factors_ref[at + hidden : at + 2 * hidden, :] = proj * sig * (1.0 - sig)


def contract(own_ref, other_ref, product_ref, left_ref, right_ref, own, other, natural, rows):
    core = lax.axis_index("c")
    own[...] = own_ref[...].astype(F32)
    other[...] = other_ref[...].astype(F32)
    chips = own.shape[0] // 16
    for ch in range(2):
        halves = []
        for kh in range(2):
            halves.append(
                jnp.concatenate([own[every(ch * 8 + 2 * r + kh, chips, 16), :] for r in range(2)], axis=0)
            )
            for r in range(2):
                at = every(ch * 8 + 4 + 2 * r + kh, chips, 16)
                mine, theirs = own[at, :], other[at, :]
                base = kh * 4 * chips + r
                natural[every(base, chips, 4), :] = jnp.where(core == 0, mine, theirs)
                natural[every(base + 2, chips, 4), :] = jnp.where(core == 0, theirs, mine)
        left = jnp.concatenate(halves, axis=1).astype(BF16)
        right = jnp.concatenate([natural[: 4 * chips, :], natural[4 * chips :, :]], axis=1).astype(BF16)
        left_ref[ch] = left
        right_ref[ch] = right
        product = dot_nt(left, right)
        for r in range(2):
            for jh in range(2):
                rows[every(ch * 4 + 2 * r + jh, chips, 8), :] = product[
                    r * chips : (r + 1) * chips, jh * LANES : (jh + 1) * LANES
                ]
    product_ref[...] = rows[...].astype(BF16)


def out_norm(values):
    center = values - jnp.mean(values, axis=0, keepdims=True)
    scale = lax.rsqrt(jnp.mean(center * center, axis=0, keepdims=True) + EPSILON)
    return center * scale, scale


def middle(product_ref, scaled_ref, mean_ref, grad_ref, rows, grads):
    hidden = scaled_ref.shape[0]
    rows[...] = product_ref[...].astype(F32)
    for u in range(4):
        hat, scale = out_norm(rows[every(u, hidden, 4), :])
        at = slice(u * LANES, (u + 1) * LANES)
        scaled = scaled_ref[:, at]
        both = jnp.mean(scaled * hat, axis=0, keepdims=True)
        grads[every(u, hidden, 4), :] = scale * (scaled - mean_ref[:1, at] - hat * both)
    grad_ref[...] = grads[...].astype(BF16)


def beside_middle(
    product_ref, grad_out_normed_ref, grad_lin_ref, grad_t_ref, gate_t_ref, normed_t_ref,
    w_out_ref, w_gate_ref, gain_ref, bias_ref, w_out_part_ref, w_gate_part_ref, vectors_ref, gate_term_ref,
    rows,
):
    hidden = w_out_ref.shape[0]
    rows[...] = product_ref[...].astype(F32)
    hats, normed = [], []
    for u in range(4):
        hat, _ = out_norm(rows[every(u, hidden, 4), :])
        hats.append(hat)
        normed.append((hat * gain_ref[...] + bias_ref[...]).astype(BF16))
    hat = jnp.concatenate(hats, axis=1)
    out_normed = jnp.concatenate(normed, axis=1)
    w_out_t = jnp.transpose(w_out_ref[...].astype(F32)).astype(BF16)
    outlin = dot_nn(w_out_t, out_normed)
    gate = gate_t_ref[...]
    grad_gate = (grad_t_ref[...] * outlin * gate * (1.0 - gate)).astype(BF16)
    w_out_part_ref[...] = dot_nt(out_normed, grad_lin_ref[...])
    w_gate_part_ref[...] = dot_nt(normed_t_ref[...], grad_gate)
    gate_term_ref[...] = dot_nn(w_gate_ref[...], grad_gate)
    grad_out_normed = grad_out_normed_ref[...]
    vectors_ref[...] = columns(
        jnp.sum(grad_out_normed * hat, axis=1, keepdims=True),
        jnp.sum(grad_out_normed, axis=1, keepdims=True),
    )


def columns(first, second):
    lane = lax.broadcasted_iota(jnp.int32, (first.shape[0], LANES), 1)
    return jnp.where(lane == 0, first, jnp.where(lane == 1, second, 0.0))


def contract_back(grad_ref, left_ref, right_ref, grad_left_ref, keep_ref, give_ref, rows, natural):
    core = lax.axis_index("c")
    rows[...] = grad_ref[...].astype(F32)
    chips = rows.shape[0] // 8
    pieces = []
    for ch in range(2):
        halves = []
        for jh in range(2):
            halves.append(
                jnp.concatenate([rows[every(ch * 4 + 2 * r + jh, chips, 8), :] for r in range(2)], axis=0)
            )
        grad = jnp.concatenate(halves, axis=1)
        grad_t = jnp.transpose(grad).astype(BF16)
        grad_right = dot_nn(grad_t, left_ref[ch])
        natural[: 4 * chips, :] = grad_right[:, :LANES]
        natural[4 * chips :, :] = grad_right[:, LANES:]
        for r in range(2):
            for kh in range(2):
                base = kh * 4 * chips + r
                low = natural[every(base, chips, 4), :]
                high = natural[every(base + 2, chips, 4), :]
                at = every(ch * 4 + 2 * r + kh, chips, 8)
                keep_ref[at, :] = jnp.where(core == 0, low, high)
                give_ref[at, :] = jnp.where(core == 0, high, low)
        pieces.append(dot_nn(grad.astype(BF16), right_ref[ch]))
    for ch in range(2):
        for r in range(2):
            for kh in range(2):
                rows[every(ch * 4 + 2 * r + kh, chips, 8), :] = pieces[ch][
                    r * chips : (r + 1) * chips, kh * LANES : (kh + 1) * LANES
                ]
    grad_left_ref[...] = rows[...]


def join(grad_left_ref, keep_ref, got_ref, edges_ref):
    grad_left = grad_left_ref[...].reshape(-1, 8, LANES)
    grad_right = (keep_ref[...] + got_ref[...]).reshape(-1, 8, LANES)
    both = jnp.concatenate([grad_left, grad_right], axis=1)
    edges_ref[...] = both.reshape(-1, LANES).astype(BF16)


def rear(
    edges_ref, factors_ref, normed_t_ref, hat_t_ref, w_in_ref, gate_term_ref, w_out_part_ref, w_gate_part_ref,
    vectors_ref, keep_ref, give_ref, grad_normed_ref, lefts, rights, low, high,
):
    core = lax.axis_index("c")
    hidden = w_in_ref.shape[1] // 4
    edges = edges_ref[...].astype(F32).reshape(-1, 16, LANES)
    lefts[...] = edges[:, :8, :].reshape(-1, LANES)
    rights[...] = edges[:, 8:, :].reshape(-1, LANES)
    parts = []
    for u in range(4):
        at = slice(u * LANES, (u + 1) * LANES)
        left = lefts[every(u, hidden, 4), :]
        right = rights[every(u, hidden, 4), :]
        parts.append(
            jnp.concatenate(
                [
                    left * factors_ref[:hidden, at],
                    left * factors_ref[hidden : 2 * hidden, at],
                    right * factors_ref[2 * hidden : 3 * hidden, at],
                    right * factors_ref[3 * hidden :, at],
                ],
                axis=0,
            ).astype(BF16)
        )
    grad_projected = jnp.concatenate(parts, axis=1)
    w_in_part = dot_nt(normed_t_ref[...], grad_projected)
    grad_normed = dot_nn(w_in_ref[...], grad_projected) + gate_term_ref[...]
    grad_normed_ref[...] = grad_normed
    channels = w_in_part.shape[0]
    for t in range(3):
        low[every(t, channels, 4), :] = w_in_part[:, t * LANES : (t + 1) * LANES]
    low[every(3, channels, 4), :] = columns(
        jnp.sum(grad_normed * hat_t_ref[...], axis=1, keepdims=True),
        jnp.sum(grad_normed, axis=1, keepdims=True),
    )
    high[every(0, channels, 4), :] = w_in_part[:, 3 * LANES :]
    high[every(1, channels, 4), :] = w_gate_part_ref[...]
    high[every(2, channels, 4), :] = w_out_part_ref[...]
    high[every(3, channels, 4), :] = vectors_ref[...]
    keep_ref[...] = jnp.where(core == 0, low[...], high[...])
    give_ref[...] = jnp.where(core == 0, high[...], low[...])


def beside_rear(grad_normed_ref, hat_t_ref, scale_ref, gain_ref, pair_grad_ref):
    hat = hat_t_ref[...]
    scaled = grad_normed_ref[...] * gain_ref[...]
    grad = scale_ref[:1, :] * (
        scaled
        - jnp.mean(scaled, axis=0, keepdims=True)
        - hat * jnp.mean(scaled * hat, axis=0, keepdims=True)
    )
    pair_grad_ref[...] = jnp.transpose(grad).astype(BF16)


def add(keep_ref, got_ref, sum_ref):
    sum_ref[...] = keep_ref[...] + got_ref[...]


def reduce_share(parts_ref, share_ref):
    total = jnp.sum(parts_ref[...].reshape(-1, 8, LANES), axis=0)
    total = total[:4] + total[4:]
    both = jnp.concatenate([total, total], axis=0)
    share_ref[...] = (
        jnp.broadcast_to(both[None], (share_ref.shape[0] // 8, 8, LANES))
        .reshape(share_ref.shape)
        .astype(BF16)
    )


def finish(own_ref, other_ref, w_in_ref, w_gate_ref, w_out_ref, vectors_ref, low, high):
    core = lax.axis_index("c")
    own, other = own_ref[...].astype(F32), other_ref[...].astype(F32)
    low[...] = jnp.where(core == 0, own, other)
    high[...] = jnp.where(core == 0, other, own)
    channels = w_in_ref.shape[0]
    for t in range(3):
        w_in_ref[:, t * LANES : (t + 1) * LANES] = low[every(t, channels, 4), :]
    w_in_ref[:, 3 * LANES :] = high[every(0, channels, 4), :]
    w_gate_ref[...] = high[every(1, channels, 4), :]
    w_out_ref[...] = high[every(2, channels, 4), :]
    inner = jnp.transpose(low[every(3, channels, 4), :])
    outer = jnp.transpose(high[every(3, channels, 4), :])
    vectors_ref[...] = jnp.concatenate([inner[:2], outer[:2], inner[:2], outer[:2]], axis=0)


def on_device(
    pair, grad_out, w_in, w_gate, w_out, ln_in_gain, ln_in_bias, ln_out_gain, ln_out_bias
):
    shape = pair.shape
    channels = shape[3]
    hidden = w_out.shape[0]
    cells = shape[1] * shape[2]
    full_len = shape[2]
    pair2 = pair.reshape(cells, channels)
    grad2 = grad_out.reshape(cells, channels)
    in_gain_row, in_bias_row = ln_in_gain.reshape(1, -1), ln_in_bias.reshape(1, -1)
    in_gain_col = ln_in_gain.reshape(-1, 1)
    out_gain_col, out_bias_col = ln_out_gain.reshape(-1, 1), ln_out_bias.reshape(-1, 1)
    grid = (hidden, cells)
    quarter = (4 * hidden, LANES)
    whole = (8 * hidden, LANES)
    flat = lambda axes: lambda a: lax.all_to_all(a, axes, 0, 0, tiled=True)
    to_chips, to_peers = flat(CHIPS), flat(PEERS)
    swap = lambda a: lax.ppermute(a, "c", SWAP)

    edges, normed, w_in_t = call(
        front, [(whole, BF16), ((cells, channels), BF16), ((4 * hidden, channels), BF16)], [whole]
    )(pair2, w_in, in_gain_row, in_bias_row)
    own = to_chips(edges)
    normed_t, hat_t, scale, factors, grad_t, gate_t, grad_lin, grad_out_normed, scaled, mean = call(
        beside_front,
        [
            (grid, BF16), (grid, F32), ((8, cells), F32), ((4 * hidden, cells), F32), (grid, F32), (grid, F32),
            (grid, BF16), (grid, F32), (grid, F32), ((8, cells), F32),
        ],
        work=1 << 28,
    )(normed, pair2, grad2, w_in_t, w_gate, w_out, out_gain_col)
    other = swap(own)
    product, left, right = call(
        contract,
        [(quarter, BF16), ((2, full_len // 2, full_len), BF16), ((2, full_len, full_len), BF16)],
        [whole, whole, quarter, quarter],
    )(own, other)
    product = to_chips(product)
    (grad_product,) = call(middle, [(quarter, BF16)], [quarter, quarter])(product, scaled, mean)
    grad_cols = to_chips(grad_product)
    w_out_part, w_gate_part, vectors, gate_term = call(
        beside_middle,
        [((hidden, channels), F32), ((channels, channels), F32), ((hidden, LANES), F32), (grid, F32)],
        [quarter],
        work=1 << 28,
    )(product, grad_out_normed, grad_lin, grad_t, gate_t, normed_t, w_out, w_gate, out_gain_col, out_bias_col)
    grad_left, keep, give = call(contract_back, [(quarter, F32)] * 3, [quarter, quarter])(
        grad_cols, left, right
    )
    (grad_edges,) = call(join, [(whole, BF16)])(grad_left, keep, swap(give))
    grad_edges = to_chips(grad_edges)
    keep, give, grad_normed = call(
        rear, [(quarter, F32), (quarter, F32), (grid, F32)], [quarter] * 4
    )(grad_edges, factors, normed_t, hat_t, w_in, gate_term, w_out_part, w_gate_part, vectors)
    (parts,) = call(add, [(quarter, F32)])(keep, swap(give))
    parts = to_peers(parts)
    (pair_grad,) = call(beside_rear, [((cells, channels), BF16)], work=1 << 28)(
        grad_normed, hat_t, scale, in_gain_col
    )
    (share,) = call(reduce_share, [(quarter, BF16)])(parts)
    mine = to_peers(share)
    w_in_total, w_gate_total, w_out_total, vectors = call(
        finish,
        [(w_in.shape, F32), (w_gate.shape, F32), (w_out.shape, F32), ((8, LANES), F32)],
        [quarter, quarter],
    )(mine, swap(mine))
    return (
        pair_grad.reshape(shape),
        w_in_total,
        w_gate_total,
        w_out_total,
        vectors[0],
        vectors[1],
        vectors[2],
        vectors[3],
    )


def solution(mesh):
    fine = Mesh(mesh.devices.reshape(2, 2, 8, 4, 2), ("X", "x", "z", "y", "c"))
    cells = P("X", ("x", "z", "y", "c"), None, None)
    in_specs = (cells, cells, P(), P(), P(), P(), P(), P(), P())
    out_specs = (cells, P(), P(), P(), P(), P(), P(), P())
    return jax.shard_map(
        on_device, mesh=fine, in_specs=in_specs, out_specs=out_specs, check_vma=False
    )
```

time: 396 us -> 134 us (0.34)
  waiting for transfers between devices: 236 us -> 19 us
  starting transfers between devices: 43.2 us -> 20.9 us
  between operations: 14.4 us -> 0.8 us
  other arithmetic: 9.51 us -> 0 us
  Pallas kernels: 0 us -> 6.49 us
  matrix products: 6.42 us -> 0 us
  blocking collectives: 73.9 us -> 78.2 us
    psum x1 -> x0, waiting for transfers between devices: 169 us -> none  [on_device(): lax.psum((w_in_part, in_gain_part, in_bias_part), ('dp', 'dap'))]
    all_to_all x0 -> x4, blocking collectives: none -> 78.2 us  [on_device(): flat = lambda axes: lambda a: lax.all_to_all(a, axes, 0, 0, tiled=True)]
    psum x1 -> x0, blocking collectives: 73.9 us -> none  [on_device(): lax.psum((w_in_part, in_gain_part, in_bias_part), ('dp', 'dap'))]
    all_to_all x6 -> x2, waiting for transfers between devices: 67.7 us -> 15.5 us  [on_device(): flat = lambda axes: lambda a: lax.all_to_all(a, axes, 0, 0, tiled=True)]
    all_to_all x6 -> x2, starting transfers between devices: 43.1 us -> 9.51 us  [on_device(): flat = lambda axes: lambda a: lax.all_to_all(a, axes, 0, 0, tiled=True)]
    ppermute x0 -> x4, starting transfers between devices: none -> 11.4 us  [on_device(): swap = lambda a: lax.ppermute(a, 'c', SWAP)]
    pallas_call x0 -> x12, Pallas kernels: none -> 6.49 us  [run(): pl.pallas_call(body, out_shape=[jax.ShapeDtypeStruct(shape, dtype) for sh...]
    dot_general x13 -> x0, matrix products: 6.42 us -> none  [the longest x1 1.23 us: on_device(): jnp.einsum('brkc,bfrk->cf', pair_normed, grad_projected, preferred_elemen...]
  transfers between devices with their start and end apart: 7 -> 6, of which waited for: 7 -> 5; matrix products, arithmetic and copies ran while one was open for 2% -> 0% of each run, Pallas kernels for 0% -> 1%
where the time goes in v2:
time: 134 us
  blocking collectives  78.2 us (58%)
  starting transfers between devices  20.9 us (16%)
  waiting for transfers between devices  19 us (14%)
  local copies, waits for them, and re-layouts  8.35 us (6%)
  Pallas kernels  6.49 us (5%)
    all_to_all x4, blocking collectives, on_device(): flat = lambda axes: lambda a: lax.all_to_all(a, axes, 0, 0, tiled=True)  78.2 us
    all_to_all x2, waiting for transfers between devices, on_device(): flat = lambda axes: lambda a: lax.all_to_all(a, axes, 0, 0, tiled=True)  15.5 us
    ppermute x4, starting transfers between devices, on_device(): swap = lambda a: lax.ppermute(a, 'c', SWAP)  11.4 us
    all_to_all x2, starting transfers between devices, on_device(): flat = lambda axes: lambda a: lax.all_to_all(a, axes, 0, 0, tiled=True)  9.51 us
    unnamed x38, local copies, waits for them, and re-layouts  7.49 us
    pallas_call x12, Pallas kernels, run(): pl.pallas_call(body, out_shape=[jax.ShapeDtypeStruct(shape, dtype) for sh...  6.49 us
    ppermute x4, waiting for transfers between devices, on_device(): swap = lambda a: lax.ppermute(a, 'c', SWAP)  3.49 us
  transfers between devices with their start and end apart: 6, of which 5 were waited for; matrix products, arithmetic and copies ran while one was open for 0% of the time, Pallas kernels for 1%

profile of v2, /device:TPU:1, one launch (start us, length us, event | category | flops | bytes accessed | tf_op | source)
XLA Modules:
  0.0 133.8 jit_solution(3173641922034631641)
XLA Ops:
  0.7 0.6 copy-done.8
  1.3 0.0 copy-done.9
  1.3 0.9 copy-done
  2.2 0.9 copy-done.2
  3.1 0.6 shard_map.152
  3.7 0.0 copy-start.11
  3.7 24.2 %all_to_all.66 = bf16[64,16,128]{2,1,0:T(8,128)(2,1)S(1)} all-to-all(bf16[64,16,128]{2,1,0:T(8,128)(2,1)S(1)} %bitcast.40), channel_id=1, replica_groups=mesh['X'=2,'x'=2,'z'=8,'y'=4,'c'=2] {'x','z','y'}, dimensions={0} | all-to-all | bytes 524288 | tf_op jit(solution)/shard_map/all_to_all | solution.py:328
  27.9 0.0 copy-done.11
  27.9 3.4 %collective-permute-start = (bf16[1024,128]{1,0:T(8,128)(2,1)S(1)}, bf16[1024,128]{1,0:T(8,128)(2,1)S(1)}, u32[]{:S(2)}, u32[]{:S(2)}) collective-permute-start(bf16[1024,128]{1,0:T(8,128)(2,1)S(1)} %bitcast.32), channel_id=1, source_target_pairs={{0,1},{1,0},{2,3},{3,2},{4,5},{5,4},{6,7},{7,6},{8,9},{9,8},{10,11... | collective-permute-start | bytes 786440 | tf_op jit(solution)/shard_map/ppermute | solution.py:330
  31.3 1.2 collective-permute-done.other_ref
  32.5 1.1 shard_map.153
  33.6 4.8 %all-to-all-start.1 = ((bf16[64,8,128]{2,1,0:T(8,128)(2,1)}), bf16[64,8,128]{2,1,0:T(8,128)(2,1)S(1)}, u32[]{:S(2)}, u32[]{:S(2)}) async-start(bf16[64,8,128]{2,1,0:T(8,128)(2,1)} %bitcast.5), calls=%async_computation.1 | async-start | bytes 262144 | tf_op jit(solution)/shard_map/all_to_all | solution.py:328
  38.4 0.0 copy-start.17
  38.4 0.6 copy-done.17
  39.0 0.1 copy.17.gain_ref
  39.2 0.6 copy-done.6
  39.8 0.0 copy-done.7
  39.8 0.9 copy-done.12
  40.7 0.9 copy-done.14
  41.6 0.6 shard_map.154
  42.2 0.6 copy-done.4
  42.9 5.5 %all-to-all-done.1 = bf16[64,8,128]{2,1,0:T(8,128)(2,1)S(1)} async-done(((bf16[64,8,128]{2,1,0:T(8,128)(2,1)}), bf16[64,8,128]{2,1,0:T(8,128)(2,1)S(1)}, u32[]{:S(2)}, u32[]{:S(2)}) %all-to-all-start.1) | async-done | bytes 131104 | tf_op jit(solution)/shard_map/all_to_all | solution.py:328
  48.3 0.2 shard_map.155
  48.5 15.5 %all_to_all.67 = bf16[64,8,128]{2,1,0:T(8,128)(2,1)S(1)} all-to-all(bf16[64,8,128]{2,1,0:T(8,128)(2,1)S(1)} %bitcast.39), channel_id=1, replica_groups=mesh['X'=2,'x'=2,'z'=8,'y'=4,'c'=2] {'x','z','y'}, dimensions={0} | all-to-all | bytes 262144 | tf_op jit(solution)/shard_map/all_to_all | solution.py:328
  64.0 0.4 shard_map.156
  64.4 2.3 %collective-permute-start.1 = (f32[512,128]{1,0:T(8,128)S(1)}, f32[512,128]{1,0:T(8,128)S(1)}, u32[]{:S(2)}, u32[]{:S(2)}) collective-permute-start(f32[512,128]{1,0:T(8,128)S(1)} %get-tuple-element.48), channel_id=1, source_target_pairs={{0,1},{1,0},{2,3},{3,2},{4,5},{5,4},{6,7},{7,6},{8,9},{9,8},{10,11... | collective-permute-start | bytes 786440 | tf_op jit(solution)/shard_map/ppermute | solution.py:330
  66.7 1.2 collective-permute-done.1.got_ref
  67.8 0.7 shard_map.157
  68.6 4.8 %all-to-all-start.3 = ((bf16[64,16,128]{2,1,0:T(8,128)(2,1)}), bf16[64,16,128]{2,1,0:T(8,128)(2,1)S(1)}, u32[]{:S(2)}, u32[]{:S(2)}) async-start(bf16[64,16,128]{2,1,0:T(8,128)(2,1)} %bitcast.11), calls=%async_computation.3 | async-start | bytes 524288 | tf_op jit(solution)/shard_map/all_to_all | solution.py:328
  73.3 0.0 copy-start.18
  73.4 0.6 copy-done.18
  74.0 0.1 copy.19.bias_ref
  74.1 0.0 copy-start.1
  74.1 0.5 shard_map.158
  74.7 10.0 %all-to-all-done.3 = bf16[64,16,128]{2,1,0:T(8,128)(2,1)S(1)} async-done(((bf16[64,16,128]{2,1,0:T(8,128)(2,1)}), bf16[64,16,128]{2,1,0:T(8,128)(2,1)S(1)}, u32[]{:S(2)}, u32[]{:S(2)}) %all-to-all-start.3) | async-done | bytes 262176 | tf_op jit(solution)/shard_map/all_to_all | solution.py:328
  84.7 0.6 shard_map.159
  85.3 2.7 %collective-permute-start.2 = (f32[512,128]{1,0:T(8,128)S(1)}, f32[512,128]{1,0:T(8,128)S(1)}, u32[]{:S(2)}, u32[]{:S(2)}) collective-permute-start(f32[512,128]{1,0:T(8,128)S(1)} %get-tuple-element.63), channel_id=1, source_target_pairs={{0,1},{1,0},{2,3},{3,2},{4,5},{5,4},{6,7},{7,6},{8,9},{9,8},{10,11... | collective-permute-start | bytes 786440 | tf_op jit(solution)/shard_map/ppermute | solution.py:330
  88.0 1.2 collective-permute-done.2.got_ref
  89.2 20.8 %all_to_all.68 = f32[128,4,128]{2,1,0:T(4,128)S(1)} all-to-all(f32[128,4,128]{2,1,0:T(4,128)S(1)} %bitcast.31), channel_id=1, replica_groups=mesh['X'=2,'x'=2,'z'=8,'y'=4,'c'=2] {'X','x','z','y'}, dimensions={0} | all-to-all | bytes 524288 | tf_op jit(solution)/shard_map/all_to_all | solution.py:328
  110.0 0.1 shard_map.162
  110.1 17.8 %all_to_all.69 = bf16[128,4,128]{2,1,0:T(4,128)(2,1)S(1)} all-to-all(bf16[128,4,128]{2,1,0:T(4,128)(2,1)S(1)} %bitcast.35), channel_id=1, replica_groups=mesh['X'=2,'x'=2,'z'=8,'y'=4,'c'=2] {'X','x','z','y'}, dimensions={0} | all-to-all | bytes 262144 | tf_op jit(solution)/shard_map/all_to_all | solution.py:328
  127.9 3.0 %collective-permute-start.3 = (bf16[512,128]{1,0:T(8,128)(2,1)S(1)}, bf16[512,128]{1,0:T(8,128)(2,1)S(1)}, u32[]{:S(2)}, u32[]{:S(2)}) collective-permute-start(bf16[512,128]{1,0:T(8,128)(2,1)S(1)} %bitcast.36), channel_id=1, source_target_pairs={{0,1},{1,0},{2,3},{3,2},{4,5},{5,4},{6,7},{7,6},{8,9},{9,8},{10,11... | collective-permute-start | bytes 393224 | tf_op jit(solution)/shard_map/ppermute | solution.py:330
  130.9 0.1 copy.20.gain_ref
  131.0 0.6 copy-done.16
  131.6 0.9 shard_map.160
  132.5 0.0 collective-permute-done.3.other_ref
  132.5 0.8 shard_map.163
  133.3 0.5 slice_bitcast_fusion
  (22 shorter events, 0.1 us)
Async XLA Ops:
  0.6 0.7 copy-start.8
  0.6 0.7 copy-start.9
  1.3 0.9 copy-start
  2.2 0.9 copy-start.2
  3.7 24.2 %copy-start.11 = (bf16[512,128]{1,0:T(8,128)(2,1)}, bf16[512,128]{1,0:T(8,128)(2,1)S(1)}, u32[]{:S(2)}) copy-start(bf16[512,128]{1,0:T(8,128)(2,1)S(1)} %get-tuple-element.40.normed_ref) | copy-start | bytes 393220
  3.7 24.2 %copy-start.13 = (bf16[512,128]{1,0:T(8,128)(2,1)}, bf16[512,128]{1,0:T(8,128)(2,1)S(1)}, u32[]{:S(2)}) copy-start(bf16[512,128]{1,0:T(8,128)(2,1)S(1)} %get-tuple-element.41.w_in_t_ref) | copy-start | bytes 393220
  27.9 4.6 %collective-permute-start = (bf16[1024,128]{1,0:T(8,128)(2,1)S(1)}, bf16[1024,128]{1,0:T(8,128)(2,1)S(1)}, u32[]{:S(2)}, u32[]{:S(2)}) collective-permute-start(bf16[1024,128]{1,0:T(8,128)(2,1)S(1)} %bitcast.32), channel_id=1, source_target_pairs={{0,1},{1,0},{2,3},{3,2},{4,5},{5,4},{6,7},{7,6},{8,9},{9,8},{10,11... | collective-permute-start | bytes 786440 | tf_op jit(solution)/shard_map/ppermute | solution.py:330
  33.6 5.5 %copy-start.3 = (bf16[1,2,256,128]{3,2,1,0:T(8,128)(2,1)S(1)}, bf16[1,2,256,128]{3,2,1,0:T(8,128)(2,1)}, u32[]{:S(2)}) copy-start(bf16[1,2,256,128]{3,2,1,0:T(8,128)(2,1)} %param.9) | copy-start | bytes 393220
  33.6 5.5 %copy-start.10 = (bf16[1,2,256,128]{3,2,1,0:T(8,128)(2,1)S(1)}, bf16[1,2,256,128]{3,2,1,0:T(8,128)(2,1)}, u32[]{:S(2)}) copy-start(bf16[1,2,256,128]{3,2,1,0:T(8,128)(2,1)} %param.10) | copy-start | bytes 393220
  33.6 14.7 %all-to-all-start.1 = ((bf16[64,8,128]{2,1,0:T(8,128)(2,1)}), bf16[64,8,128]{2,1,0:T(8,128)(2,1)S(1)}, u32[]{:S(2)}, u32[]{:S(2)}) async-start(bf16[64,8,128]{2,1,0:T(8,128)(2,1)} %bitcast.5), calls=%async_computation.1 | async-start | bytes 262144 | tf_op jit(solution)/shard_map/all_to_all | solution.py:328
  38.4 0.7 copy-start.17
  39.0 0.8 copy-start.6
  39.0 0.8 copy-start.7
  39.8 0.9 copy-start.12
  40.7 0.9 copy-start.14
  42.2 0.6 copy-start.4
  42.9 5.7 %copy-start.15 = (f32[8,512]{1,0:T(8,128)}, f32[8,512]{1,0:T(8,128)S(1)}, u32[]{:S(2)}) copy-start(f32[8,512]{1,0:T(8,128)S(1)} %get-tuple-element.61.scale_ref) | copy-start | bytes 49156
  64.4 3.4 %collective-permute-start.1 = (f32[512,128]{1,0:T(8,128)S(1)}, f32[512,128]{1,0:T(8,128)S(1)}, u32[]{:S(2)}, u32[]{:S(2)}) collective-permute-start(f32[512,128]{1,0:T(8,128)S(1)} %get-tuple-element.48), channel_id=1, source_target_pairs={{0,1},{1,0},{2,3},{3,2},{4,5},{5,4},{6,7},{7,6},{8,9},{9,8},{10,11... | collective-permute-start | bytes 786440 | tf_op jit(solution)/shard_map/ppermute | solution.py:330
  68.6 5.5 %copy-start.5 = (bf16[128,512]{1,0:T(8,128)(2,1)S(1)}, bf16[128,512]{1,0:T(8,128)(2,1)}, u32[]{:S(2)}) copy-start(bf16[128,512]{1,0:T(8,128)(2,1)} %copy-done.4) | copy-start | bytes 393220
  68.6 16.1 %all-to-all-start.3 = ((bf16[64,16,128]{2,1,0:T(8,128)(2,1)}), bf16[64,16,128]{2,1,0:T(8,128)(2,1)S(1)}, u32[]{:S(2)}, u32[]{:S(2)}) async-start(bf16[64,16,128]{2,1,0:T(8,128)(2,1)} %bitcast.11), calls=%async_computation.3 | async-start | bytes 524288 | tf_op jit(solution)/shard_map/all_to_all | solution.py:328
  73.3 0.7 copy-start.18
  74.1 10.6 %copy-start.1 = (bf16[128,512]{1,0:T(8,128)(2,1)S(1)}, bf16[128,512]{1,0:T(8,128)(2,1)}, u32[]{:S(2)}) copy-start(bf16[128,512]{1,0:T(8,128)(2,1)} %w_in_ref.3) | copy-start | bytes 393220
  85.3 3.9 %collective-permute-start.2 = (f32[512,128]{1,0:T(8,128)S(1)}, f32[512,128]{1,0:T(8,128)S(1)}, u32[]{:S(2)}, u32[]{:S(2)}) collective-permute-start(f32[512,128]{1,0:T(8,128)S(1)} %get-tuple-element.63), channel_id=1, source_target_pairs={{0,1},{1,0},{2,3},{3,2},{4,5},{5,4},{6,7},{7,6},{8,9},{9,8},{10,11... | collective-permute-start | bytes 786440 | tf_op jit(solution)/shard_map/ppermute | solution.py:330
  127.9 4.6 %collective-permute-start.3 = (bf16[512,128]{1,0:T(8,128)(2,1)S(1)}, bf16[512,128]{1,0:T(8,128)(2,1)S(1)}, u32[]{:S(2)}, u32[]{:S(2)}) collective-permute-start(bf16[512,128]{1,0:T(8,128)(2,1)S(1)} %bitcast.36), channel_id=1, source_target_pairs={{0,1},{1,0},{2,3},{3,2},{4,5},{5,4},{6,7},{7,6},{8,9},{9,8},{10,11... | collective-permute-start | bytes 393224 | tf_op jit(solution)/shard_map/ppermute | solution.py:330
  130.9 0.7 copy-start.16

commit v3 on v2

--- a/solution.py
+++ b/solution.py
@@ -16,15 +16,16 @@
 BF16 = jnp.bfloat16
 
 
-def call(body, outs, scratch=(), work=0):
+def call(body, outs, scratch=(), work=0, far=0):
     def run(*operands):
         return pl.pallas_call(
             body,
             out_shape=[jax.ShapeDtypeStruct(shape, dtype) for shape, dtype in outs],
-            in_specs=[pl.BlockSpec(memory_space=pltpu.VMEM)] * len(operands),
+            in_specs=[pl.BlockSpec(memory_space=pltpu.HBM)] * far
+            + [pl.BlockSpec(memory_space=pltpu.VMEM)] * (len(operands) - far),
             out_specs=[pl.BlockSpec(memory_space=pltpu.VMEM)] * len(outs),
-            scratch_shapes=[pltpu.VMEM(shape, F32) for shape in scratch],
-            compiler_params=pltpu.CompilerParams(vmem_limit_bytes=24 * 1024 * 1024),
+            scratch_shapes=[pltpu.VMEM(s, F32) if isinstance(s, tuple) else s for s in scratch],
+            compiler_params=pltpu.CompilerParams(vmem_limit_bytes=8 * 1024 * 1024),
             cost_estimate=pl.CostEstimate(
                 flops=work, bytes_accessed=1 << 20, transcendentals=0
             ),
@@ -49,8 +50,24 @@
     return pl.ds(start, count, stride=stride)
 
 
-def front(pair_ref, w_in_ref, gain_ref, bias_ref, edges_ref, normed_ref, w_in_t_ref, rows):
-    cells, channels = pair_ref.shape
+def column(row):
+    return jnp.transpose(jnp.broadcast_to(row, (LANES, row.shape[1])))[:, :1]
+
+
+def front(
+    pair_far, w_in_far, gain_far, bias_far, edges_ref, normed_ref, w_in_t_ref,
+    rows, pair_ref, w_in_ref, gain_ref, bias_ref, arrived,
+):
+    copies = [
+        pltpu.make_async_copy(source, target, arrived.at[n])
+        for n, (source, target) in enumerate(
+            [(pair_far, pair_ref), (gain_far, gain_ref), (bias_far, bias_ref), (w_in_far, w_in_ref)]
+        )
+    ]
+    for copy in copies:
+        copy.start()
+    for copy in copies:
+        copy.wait()
     values = pair_ref[...].astype(F32)
     center = values - jnp.mean(values, axis=1, keepdims=True)
     scale = lax.rsqrt(jnp.mean(center * center, axis=1, keepdims=True) + EPSILON)
@@ -90,7 +107,7 @@
     grad_lin_ref[...] = grad_lin
     grad_out_normed = dot_nn(w_out_ref[...], grad_lin)
     grad_out_normed_ref[...] = grad_out_normed
-    scaled = grad_out_normed * gain_ref[...]
+    scaled = grad_out_normed * column(gain_ref[...])
     scaled_ref[...] = scaled
     mean_ref[...] = jnp.broadcast_to(jnp.mean(scaled, axis=0, keepdims=True), mean_ref.shape)
     for side in range(2):
@@ -157,10 +174,11 @@
     hidden = w_out_ref.shape[0]
     rows[...] = product_ref[...].astype(F32)
     hats, normed = [], []
+    gain, bias = column(gain_ref[...]), column(bias_ref[...])
     for u in range(4):
         hat, _ = out_norm(rows[every(u, hidden, 4), :])
         hats.append(hat)
-        normed.append((hat * gain_ref[...] + bias_ref[...]).astype(BF16))
+        normed.append((hat * gain + bias).astype(BF16))
     hat = jnp.concatenate(hats, axis=1)
     out_normed = jnp.concatenate(normed, axis=1)
     w_out_t = jnp.transpose(w_out_ref[...].astype(F32)).astype(BF16)
@@ -177,9 +195,13 @@
     )
 
 
-def columns(first, second):
-    lane = lax.broadcasted_iota(jnp.int32, (first.shape[0], LANES), 1)
-    return jnp.where(lane == 0, first, jnp.where(lane == 1, second, 0.0))
+def columns(*sums):
+    lane = lax.broadcasted_iota(jnp.int32, (sums[0].shape[0], LANES), 1)
+    high = [value.astype(BF16).astype(F32) for value in sums]
+    out = jnp.zeros(lane.shape, F32)
+    for n, value in enumerate(high + [value - top for value, top in zip(sums, high)]):
+        out = jnp.where(lane == n, value, out)
+    return out
 
 
 def contract_back(grad_ref, left_ref, right_ref, grad_left_ref, keep_ref, give_ref, rows, natural):
@@ -269,7 +291,7 @@
 
 def beside_rear(grad_normed_ref, hat_t_ref, scale_ref, gain_ref, pair_grad_ref):
     hat = hat_t_ref[...]
-    scaled = grad_normed_ref[...] * gain_ref[...]
+    scaled = grad_normed_ref[...] * column(gain_ref[...])
     grad = scale_ref[:1, :] * (
         scaled
         - jnp.mean(scaled, axis=0, keepdims=True)
@@ -278,14 +300,23 @@
     pair_grad_ref[...] = jnp.transpose(grad).astype(BF16)
 
 
+def split_vectors(values):
+    lane = lax.broadcasted_iota(jnp.int32, values.shape, values.ndim - 1)
+    row = lax.broadcasted_iota(jnp.int32, values.shape, values.ndim - 2)
+    total = values + pltpu.roll(values, LANES - 2, values.ndim - 1)
+    high = total.astype(BF16).astype(F32)
+    low = pltpu.roll(total - high, 2, values.ndim - 1)
+    return jnp.where(row % 4 == 3, jnp.where(lane < 2, high, jnp.where(lane < 4, low, 0.0)), values)
+
+
 def add(keep_ref, got_ref, sum_ref):
-    sum_ref[...] = keep_ref[...] + got_ref[...]
+    sum_ref[...] = split_vectors(keep_ref[...] + got_ref[...]).astype(BF16)
 
 
 def reduce_share(parts_ref, share_ref):
-    total = jnp.sum(parts_ref[...].reshape(-1, 8, LANES), axis=0)
+    total = jnp.sum(parts_ref[...].astype(F32).reshape(-1, 8, LANES), axis=0)
     total = total[:4] + total[4:]
-    both = jnp.concatenate([total, total], axis=0)
+    both = split_vectors(jnp.concatenate([total, total], axis=0))
     share_ref[...] = (
         jnp.broadcast_to(both[None], (share_ref.shape[0] // 8, 8, LANES))
         .reshape(share_ref.shape)
@@ -293,7 +324,9 @@
     )
 
 
-def finish(own_ref, other_ref, w_in_ref, w_gate_ref, w_out_ref, vectors_ref, low, high):
+def finish(
+    own_ref, other_ref, w_in_ref, w_gate_ref, w_out_ref, in_gain_ref, in_bias_ref, out_gain_ref, out_bias_ref, low, high
+):
     core = lax.axis_index("c")
     own, other = own_ref[...].astype(F32), other_ref[...].astype(F32)
     low[...] = jnp.where(core == 0, own, other)
@@ -306,7 +339,9 @@
     w_out_ref[...] = high[every(2, channels, 4), :]
     inner = jnp.transpose(low[every(3, channels, 4), :])
     outer = jnp.transpose(high[every(3, channels, 4), :])
-    vectors_ref[...] = jnp.concatenate([inner[:2], outer[:2], inner[:2], outer[:2]], axis=0)
+    inner, outer = inner[:2] + inner[2:4], outer[:2] + outer[2:4]
+    in_gain_ref[...], in_bias_ref[...] = inner[:1], inner[1:2]
+    out_gain_ref[...], out_bias_ref[...] = outer[:1], outer[1:2]
 
 
 def on_device(
@@ -320,8 +355,7 @@
     pair2 = pair.reshape(cells, channels)
     grad2 = grad_out.reshape(cells, channels)
     in_gain_row, in_bias_row = ln_in_gain.reshape(1, -1), ln_in_bias.reshape(1, -1)
-    in_gain_col = ln_in_gain.reshape(-1, 1)
-    out_gain_col, out_bias_col = ln_out_gain.reshape(-1, 1), ln_out_bias.reshape(-1, 1)
+    out_gain_row, out_bias_row = ln_out_gain.reshape(1, -1), ln_out_bias.reshape(1, -1)
     grid = (hidden, cells)
     quarter = (4 * hidden, LANES)
     whole = (8 * hidden, LANES)
@@ -330,9 +364,15 @@
     swap = lambda a: lax.ppermute(a, "c", SWAP)
 
     edges, normed, w_in_t = call(
-        front, [(whole, BF16), ((cells, channels), BF16), ((4 * hidden, channels), BF16)], [whole]
+        front, [(whole, BF16), ((cells, channels), BF16), ((4 * hidden, channels), BF16)],
+        [
+            whole, pltpu.VMEM((cells, channels), BF16), pltpu.VMEM(w_in.shape, BF16), (1, channels), (1, channels),
+            pltpu.SemaphoreType.DMA((4,)),
+        ],
+        far=4,
     )(pair2, w_in, in_gain_row, in_bias_row)
-    own = to_chips(edges)
+    own, normed = lax.optimization_barrier((to_chips(edges), normed))
+    other = swap(own)
     normed_t, hat_t, scale, factors, grad_t, gate_t, grad_lin, grad_out_normed, scaled, mean = call(
         beside_front,
         [
@@ -340,8 +380,8 @@
             (grid, BF16), (grid, F32), (grid, F32), ((8, cells), F32),
         ],
         work=1 << 28,
-    )(normed, pair2, grad2, w_in_t, w_gate, w_out, out_gain_col)
-    other = swap(own)
+    )(normed, pair2, grad2, w_in_t, w_gate, w_out, out_gain_row)
+    other, normed_t = lax.optimization_barrier((other, normed_t))
     product, left, right = call(
         contract,
         [(quarter, BF16), ((2, full_len // 2, full_len), BF16), ((2, full_len, full_len), BF16)],
@@ -350,30 +390,35 @@
     product = to_chips(product)
     (grad_product,) = call(middle, [(quarter, BF16)], [quarter, quarter])(product, scaled, mean)
     grad_cols = to_chips(grad_product)
+    grad_left, keep, give = call(contract_back, [(quarter, F32)] * 3, [quarter, quarter])(
+        grad_cols, left, right
+    )
+    give, product = lax.optimization_barrier((give, product))
+    got = swap(give)
     w_out_part, w_gate_part, vectors, gate_term = call(
         beside_middle,
         [((hidden, channels), F32), ((channels, channels), F32), ((hidden, LANES), F32), (grid, F32)],
         [quarter],
         work=1 << 28,
-    )(product, grad_out_normed, grad_lin, grad_t, gate_t, normed_t, w_out, w_gate, out_gain_col, out_bias_col)
-    grad_left, keep, give = call(contract_back, [(quarter, F32)] * 3, [quarter, quarter])(
-        grad_cols, left, right
-    )
-    (grad_edges,) = call(join, [(whole, BF16)])(grad_left, keep, swap(give))
+    )(product, grad_out_normed, grad_lin, grad_t, gate_t, normed_t, w_out, w_gate, out_gain_row, out_bias_row)
+    got, vectors = lax.optimization_barrier((got, vectors))
+    (grad_edges,) = call(join, [(whole, BF16)])(grad_left, keep, got)
     grad_edges = to_chips(grad_edges)
     keep, give, grad_normed = call(
         rear, [(quarter, F32), (quarter, F32), (grid, F32)], [quarter] * 4
     )(grad_edges, factors, normed_t, hat_t, w_in, gate_term, w_out_part, w_gate_part, vectors)
-    (parts,) = call(add, [(quarter, F32)])(keep, swap(give))
+    got = swap(give)
+    (pair_grad,) = call(beside_rear, [((cells, channels), BF16)], work=1 << 28)(
+        grad_normed, hat_t, scale, in_gain_row
+    )
+    got, pair_grad = lax.optimization_barrier((got, pair_grad))
+    (parts,) = call(add, [(quarter, BF16)])(keep, got)
     parts = to_peers(parts)
-    (pair_grad,) = call(beside_rear, [((cells, channels), BF16)], work=1 << 28)(
-        grad_normed, hat_t, scale, in_gain_col
-    )
     (share,) = call(reduce_share, [(quarter, BF16)])(parts)
     mine = to_peers(share)
-    w_in_total, w_gate_total, w_out_total, vectors = call(
+    w_in_total, w_gate_total, w_out_total, *vectors = call(
         finish,
-        [(w_in.shape, F32), (w_gate.shape, F32), (w_out.shape, F32), ((8, LANES), F32)],
+        [(w_in.shape, F32), (w_gate.shape, F32), (w_out.shape, F32)] + [((1, LANES), F32)] * 4,
         [quarter, quarter],
     )(mine, swap(mine))
     return (
@@ -381,10 +426,7 @@
         w_in_total,
         w_gate_total,
         w_out_total,
-        vectors[0],
-        vectors[1],
-        vectors[2],
-        vectors[3],
+        *(vector.reshape(-1) for vector in vectors),
     )
 
 

time: 134 us -> 128 us (0.955)
  blocking collectives: 78.2 us -> 104 us
  waiting for transfers between devices: 19 us -> 1.2 us
  starting transfers between devices: 20.9 us -> 11.7 us
  local copies, waits for them, and re-layouts: 8.35 us -> 3.79 us
    all_to_all x4 -> x6, blocking collectives: 78.2 us -> 104 us  [on_device(): flat = lambda axes: lambda a: lax.all_to_all(a, axes, 0, 0, tiled=True)]
    all_to_all x2 -> x0, waiting for transfers between devices: 15.5 us -> none  [on_device(): flat = lambda axes: lambda a: lax.all_to_all(a, axes, 0, 0, tiled=True)]
    all_to_all x2 -> x0, starting transfers between devices: 9.51 us -> none  [on_device(): flat = lambda axes: lambda a: lax.all_to_all(a, axes, 0, 0, tiled=True)]
    unnamed x38 -> x20, local copies, waits for them, and re-layouts: 7.49 us -> 3.79 us
    ppermute x4, waiting for transfers between devices: 3.49 us -> 1.2 us  [on_device(): swap = lambda a: lax.ppermute(a, 'c', SWAP)]
  transfers between devices with their start and end apart: 6 -> 4, of which waited for: 5 -> 2; matrix products, arithmetic and copies ran while one was open for 0% -> 0% of each run, Pallas kernels for 1% -> 2%
where the time goes in v3:
time: 128 us
  blocking collectives  104 us (81%)
  starting transfers between devices  11.7 us (9%)
  Pallas kernels  5.99 us (5%)
  local copies, waits for them, and re-layouts  3.79 us (3%)
    all_to_all x6, blocking collectives, on_device(): flat = lambda axes: lambda a: lax.all_to_all(a, axes, 0, 0, tiled=True)  104 us
    ppermute x4, starting transfers between devices, on_device(): swap = lambda a: lax.ppermute(a, 'c', SWAP)  11.7 us
    pallas_call x12, Pallas kernels, run(): pl.pallas_call(body, out_shape=[jax.ShapeDtypeStruct(shape, dtype) for sh...  5.99 us
    unnamed x20, local copies, waits for them, and re-layouts  3.79 us
  transfers between devices with their start and end apart: 4, of which 2 were waited for; matrix products, arithmetic and copies ran while one was open for 0% of the time, Pallas kernels for 2%

profile of v3, /device:TPU:1, one launch (start us, length us, event | category | flops | bytes accessed | tf_op | source)
XLA Modules:
  0.0 127.9 jit_solution(6483322059816311040)
XLA Ops:
  0.6 0.0 copy-start.5
  0.6 0.0 copy-start.8
  0.7 0.6 copy-done.5
  1.3 0.0 copy-done.8
  1.3 0.0 copy-start
  1.3 0.9 copy-done
  2.2 0.0 copy-start.2
  2.2 0.9 copy-done.2
  3.1 0.9 shard_map.152
  4.0 0.0 copy-start.3
  4.0 0.0 copy-start.4
  4.1 0.0 copy-start.9
  4.1 24.3 %all_to_all.67 = bf16[64,16,128]{2,1,0:T(8,128)(2,1)S(1)} all-to-all(bf16[64,16,128]{2,1,0:T(8,128)(2,1)S(1)} %bitcast.36), channel_id=1, replica_groups=mesh['X'=2,'x'=2,'z'=8,'y'=4,'c'=2] {'x','z','y'}, dimensions={0} | all-to-all | bytes 524288 | tf_op jit(solution)/shard_map/all_to_all | solution.py:362
  28.4 3.4 %collective-permute-start = (bf16[1024,128]{1,0:T(8,128)(2,1)S(1)}, bf16[1024,128]{1,0:T(8,128)(2,1)S(1)}, u32[]{:S(2)}, u32[]{:S(2)}) collective-permute-start(bf16[1024,128]{1,0:T(8,128)(2,1)S(1)} %bitcast.26), channel_id=1, source_target_pairs={{0,1},{1,0},{2,3},{3,2},{4,5},{5,4},{6,7},{7,6},{8,9},{9,8},{10,11... | collective-permute-start | bytes 786440 | tf_op jit(solution)/shard_map/ppermute | solution.py:364
  31.8 0.0 copy-start.6
  31.8 0.0 copy-done.3
  31.8 0.0 copy-done.4
  31.8 0.0 copy-done.9
  31.8 0.6 copy-done.6
  32.5 0.6 shard_map.153
  33.0 0.0 collective-permute-done.other_ref
  33.0 0.5 shard_map.154
  33.5 14.3 %all_to_all.68 = bf16[64,8,128]{2,1,0:T(8,128)(2,1)S(1)} all-to-all(bf16[64,8,128]{2,1,0:T(8,128)(2,1)S(1)} %bitcast.39), channel_id=1, replica_groups=mesh['X'=2,'x'=2,'z'=8,'y'=4,'c'=2] {'x','z','y'}, dimensions={0} | all-to-all | bytes 262144 | tf_op jit(solution)/shard_map/all_to_all | solution.py:362
  47.8 0.2 shard_map.155
  48.0 14.7 %all_to_all.69 = bf16[64,8,128]{2,1,0:T(8,128)(2,1)S(1)} all-to-all(bf16[64,8,128]{2,1,0:T(8,128)(2,1)S(1)} %bitcast.35), channel_id=1, replica_groups=mesh['X'=2,'x'=2,'z'=8,'y'=4,'c'=2] {'x','z','y'}, dimensions={0} | all-to-all | bytes 262144 | tf_op jit(solution)/shard_map/all_to_all | solution.py:362
  62.7 0.4 shard_map.156
  63.1 2.6 %collective-permute-start.1 = (f32[512,128]{1,0:T(8,128)S(1)}, f32[512,128]{1,0:T(8,128)S(1)}, u32[]{:S(2)}, u32[]{:S(2)}) collective-permute-start(f32[512,128]{1,0:T(8,128)S(1)} %get-tuple-element.66), channel_id=1, source_target_pairs={{0,1},{1,0},{2,3},{3,2},{4,5},{5,4},{6,7},{7,6},{8,9},{9,8},{10,11... | collective-permute-start | bytes 786440 | tf_op jit(solution)/shard_map/ppermute | solution.py:364
  65.7 0.0 copy-start.7
  65.7 0.7 copy-done.7
  66.4 0.6 shard_map.157
  67.0 0.0 collective-permute-done.1.got_ref
  67.0 0.1 shard_map.158
  67.0 0.0 copy-start.1
  67.0 15.3 %all_to_all.70 = bf16[64,16,128]{2,1,0:T(8,128)(2,1)S(1)} all-to-all(bf16[64,16,128]{2,1,0:T(8,128)(2,1)S(1)} %bitcast.28), channel_id=1, replica_groups=mesh['X'=2,'x'=2,'z'=8,'y'=4,'c'=2] {'x','z','y'}, dimensions={0} | all-to-all | bytes 524288 | tf_op jit(solution)/shard_map/all_to_all | solution.py:362
  82.4 0.0 copy-done.1
  82.4 0.6 shard_map.159
  82.9 2.7 %collective-permute-start.2 = (f32[512,128]{1,0:T(8,128)S(1)}, f32[512,128]{1,0:T(8,128)S(1)}, u32[]{:S(2)}, u32[]{:S(2)}) collective-permute-start(f32[512,128]{1,0:T(8,128)S(1)} %get-tuple-element.81), channel_id=1, source_target_pairs={{0,1},{1,0},{2,3},{3,2},{4,5},{5,4},{6,7},{7,6},{8,9},{9,8},{10,11... | collective-permute-start | bytes 786440 | tf_op jit(solution)/shard_map/ppermute | solution.py:364
  85.6 1.0 shard_map.160
  86.5 0.2 collective-permute-done.2.got_ref
  86.8 0.2 shard_map.161
  87.0 18.9 %all_to_all.71 = bf16[128,4,128]{2,1,0:T(4,128)(2,1)S(1)} all-to-all(bf16[128,4,128]{2,1,0:T(4,128)(2,1)S(1)} %bitcast.29), channel_id=1, replica_groups=mesh['X'=2,'x'=2,'z'=8,'y'=4,'c'=2] {'X','x','z','y'}, dimensions={0} | all-to-all | bytes 262144 | tf_op jit(solution)/shard_map/all_to_all | solution.py:362
  105.9 0.2 shard_map.162
  106.1 17.0 %all_to_all.72 = bf16[128,4,128]{2,1,0:T(4,128)(2,1)S(1)} all-to-all(bf16[128,4,128]{2,1,0:T(4,128)(2,1)S(1)} %bitcast.33), channel_id=1, replica_groups=mesh['X'=2,'x'=2,'z'=8,'y'=4,'c'=2] {'X','x','z','y'}, dimensions={0} | all-to-all | bytes 262144 | tf_op jit(solution)/shard_map/all_to_all | solution.py:362
  123.1 3.0 %collective-permute-start.3 = (bf16[512,128]{1,0:T(8,128)(2,1)S(1)}, bf16[512,128]{1,0:T(8,128)(2,1)S(1)}, u32[]{:S(2)}, u32[]{:S(2)}) collective-permute-start(bf16[512,128]{1,0:T(8,128)(2,1)S(1)} %bitcast.30), channel_id=1, source_target_pairs={{0,1},{1,0},{2,3},{3,2},{4,5},{5,4},{6,7},{7,6},{8,9},{9,8},{10,11... | collective-permute-start | bytes 393224 | tf_op jit(solution)/shard_map/ppermute | solution.py:364
  126.1 1.0 collective-permute-done.3.other_ref
  127.1 0.8 shard_map.163
Async XLA Ops:
  0.6 0.7 copy-start.5
  0.6 0.7 copy-start.8
  1.3 0.9 copy-start
  2.2 0.9 copy-start.2
  4.0 27.8 %copy-start.3 = (bf16[128,128]{1,0:T(8,128)(2,1)S(1)}, bf16[128,128]{1,0:T(8,128)(2,1)}, u32[]{:S(2)}) copy-start(bf16[128,128]{1,0:T(8,128)(2,1)} %w_gate_ref.3) | copy-start | bytes 98308
  4.0 27.8 %copy-start.4 = (bf16[128,128]{1,0:T(8,128)(2,1)S(1)}, bf16[128,128]{1,0:T(8,128)(2,1)}, u32[]{:S(2)}) copy-start(bf16[128,128]{1,0:T(8,128)(2,1)} %w_out_ref.3) | copy-start | bytes 98308
  4.1 27.7 %copy-start.9 = (bf16[1,2,256,128]{3,2,1,0:T(8,128)(2,1)S(1)}, bf16[1,2,256,128]{3,2,1,0:T(8,128)(2,1)}, u32[]{:S(2)}) copy-start(bf16[1,2,256,128]{3,2,1,0:T(8,128)(2,1)} %param.10) | copy-start | bytes 393220
  28.4 4.7 %collective-permute-start = (bf16[1024,128]{1,0:T(8,128)(2,1)S(1)}, bf16[1024,128]{1,0:T(8,128)(2,1)S(1)}, u32[]{:S(2)}, u32[]{:S(2)}) collective-permute-start(bf16[1024,128]{1,0:T(8,128)(2,1)S(1)} %bitcast.26), channel_id=1, source_target_pairs={{0,1},{1,0},{2,3},{3,2},{4,5},{5,4},{6,7},{7,6},{8,9},{9,8},{10,11... | collective-permute-start | bytes 786440 | tf_op jit(solution)/shard_map/ppermute | solution.py:364
  31.8 0.7 copy-start.6
  63.1 3.9 %collective-permute-start.1 = (f32[512,128]{1,0:T(8,128)S(1)}, f32[512,128]{1,0:T(8,128)S(1)}, u32[]{:S(2)}, u32[]{:S(2)}) collective-permute-start(f32[512,128]{1,0:T(8,128)S(1)} %get-tuple-element.66), channel_id=1, source_target_pairs={{0,1},{1,0},{2,3},{3,2},{4,5},{5,4},{6,7},{7,6},{8,9},{9,8},{10,11... | collective-permute-start | bytes 786440 | tf_op jit(solution)/shard_map/ppermute | solution.py:364
  65.7 0.7 copy-start.7
  67.0 15.3 %copy-start.1 = (bf16[128,512]{1,0:T(8,128)(2,1)S(1)}, bf16[128,512]{1,0:T(8,128)(2,1)}, u32[]{:S(2)}) copy-start(bf16[128,512]{1,0:T(8,128)(2,1)} %w_in_ref.1) | copy-start | bytes 393220
  82.9 3.8 %collective-permute-start.2 = (f32[512,128]{1,0:T(8,128)S(1)}, f32[512,128]{1,0:T(8,128)S(1)}, u32[]{:S(2)}, u32[]{:S(2)}) collective-permute-start(f32[512,128]{1,0:T(8,128)S(1)} %get-tuple-element.81), channel_id=1, source_target_pairs={{0,1},{1,0},{2,3},{3,2},{4,5},{5,4},{6,7},{7,6},{8,9},{9,8},{10,11... | collective-permute-start | bytes 786440 | tf_op jit(solution)/shard_map/ppermute | solution.py:364
  123.1 4.0 %collective-permute-start.3 = (bf16[512,128]{1,0:T(8,128)(2,1)S(1)}, bf16[512,128]{1,0:T(8,128)(2,1)S(1)}, u32[]{:S(2)}, u32[]{:S(2)}) collective-permute-start(bf16[512,128]{1,0:T(8,128)(2,1)S(1)} %bitcast.30), channel_id=1, source_target_pairs={{0,1},{1,0},{2,3},{3,2},{4,5},{5,4},{6,7},{7,6},{8,9},{9,8},{10,11... | collective-permute-start | bytes 393224 | tf_op jit(solution)/shard_map/ppermute | solution.py:364

commit v4 on v3

--- a/solution.py
+++ b/solution.py
@@ -55,7 +55,7 @@
 
 
 def front(
-    pair_far, w_in_far, gain_far, bias_far, edges_ref, normed_ref, w_in_t_ref,
+    pair_far, gain_far, bias_far, w_in_far, edges_ref, normed_ref, w_in_t_ref,
     rows, pair_ref, w_in_ref, gain_ref, bias_ref, arrived,
 ):
     copies = [
@@ -66,13 +66,14 @@
     ]
     for copy in copies:
         copy.start()
-    for copy in copies:
+    for copy in copies[:3]:
         copy.wait()
     values = pair_ref[...].astype(F32)
     center = values - jnp.mean(values, axis=1, keepdims=True)
     scale = lax.rsqrt(jnp.mean(center * center, axis=1, keepdims=True) + EPSILON)
     normed = (center * scale * gain_ref[...] + bias_ref[...]).astype(BF16)
     normed_ref[...] = normed
+    copies[3].wait()
     w_in_t = jnp.transpose(w_in_ref[...].astype(F32)).astype(BF16)
     w_in_t_ref[...] = w_in_t
     hidden = w_in_t.shape[0] // 4
@@ -314,11 +315,9 @@
 
 
 def reduce_share(parts_ref, share_ref):
-    total = jnp.sum(parts_ref[...].astype(F32).reshape(-1, 8, LANES), axis=0)
-    total = total[:4] + total[4:]
-    both = split_vectors(jnp.concatenate([total, total], axis=0))
+    total = split_vectors(jnp.sum(parts_ref[...].astype(F32).reshape(-1, 8, LANES), axis=0))
     share_ref[...] = (
-        jnp.broadcast_to(both[None], (share_ref.shape[0] // 8, 8, LANES))
+        jnp.broadcast_to(total[None], (share_ref.shape[0] // 8, 8, LANES))
         .reshape(share_ref.shape)
         .astype(BF16)
     )
@@ -328,7 +327,8 @@
     own_ref, other_ref, w_in_ref, w_gate_ref, w_out_ref, in_gain_ref, in_bias_ref, out_gain_ref, out_bias_ref, low, high
 ):
     core = lax.axis_index("c")
-    own, other = own_ref[...].astype(F32), other_ref[...].astype(F32)
+    own = jnp.sum(own_ref[...].astype(F32).reshape(2, *low.shape), axis=0)
+    other = jnp.sum(other_ref[...].astype(F32).reshape(2, *low.shape), axis=0)
     low[...] = jnp.where(core == 0, own, other)
     high[...] = jnp.where(core == 0, other, own)
     channels = w_in_ref.shape[0]
@@ -359,8 +359,9 @@
     grid = (hidden, cells)
     quarter = (4 * hidden, LANES)
     whole = (8 * hidden, LANES)
-    flat = lambda axes: lambda a: lax.all_to_all(a, axes, 0, 0, tiled=True)
-    to_chips, to_peers = flat(CHIPS), flat(PEERS)
+    to_chips = lambda a: lax.all_to_all(a, CHIPS, 0, 0, tiled=True)
+    to_peers = lambda a: lax.all_to_all(a, PEERS, 0, 0, tiled=True)
+    stay = lambda a: pltpu.with_memory_space_constraint(a, pltpu.HBM)
     swap = lambda a: lax.ppermute(a, "c", SWAP)
 
     edges, normed, w_in_t = call(
@@ -370,7 +371,7 @@
             pltpu.SemaphoreType.DMA((4,)),
         ],
         far=4,
-    )(pair2, w_in, in_gain_row, in_bias_row)
+    )(stay(pair2), stay(in_gain_row), stay(in_bias_row), stay(w_in))
     own, normed = lax.optimization_barrier((to_chips(edges), normed))
     other = swap(own)
     normed_t, hat_t, scale, factors, grad_t, gate_t, grad_lin, grad_out_normed, scaled, mean = call(
@@ -413,8 +414,7 @@
     )
     got, pair_grad = lax.optimization_barrier((got, pair_grad))
     (parts,) = call(add, [(quarter, BF16)])(keep, got)
-    parts = to_peers(parts)
-    (share,) = call(reduce_share, [(quarter, BF16)])(parts)
+    (share,) = call(reduce_share, [(whole, BF16)])(to_chips(parts))
     mine = to_peers(share)
     w_in_total, w_gate_total, w_out_total, *vectors = call(
         finish,

time: 128 us -> 126 us (0.984)
  local copies, waits for them, and re-layouts: 3.79 us -> 1.98 us
    unnamed x20 -> x16, local copies, waits for them, and re-layouts: 3.79 us -> 1.98 us
    all_to_all x6, blocking collectives: 104 us -> 103 us  [the longest x5 83.1 us: on_device(): to_chips = lambda a: lax.all_to_all(a, CHIPS, 0, 0, tiled=True)]
  transfers between devices with their start and end apart: 4 -> 4, of which waited for: 2 -> 1; matrix products, arithmetic and copies ran while one was open for 0% -> 0% of each run, Pallas kernels for 2% -> 2%
where the time goes in v4:
time: 126 us
  blocking collectives  103 us (82%)
  starting transfers between devices  12.4 us (10%)
  Pallas kernels  6.69 us (5%)
  local copies, waits for them, and re-layouts  1.98 us (2%)
    all_to_all x5, blocking collectives, on_device(): to_chips = lambda a: lax.all_to_all(a, CHIPS, 0, 0, tiled=True)  83.1 us
    all_to_all x1, blocking collectives, on_device(): to_peers = lambda a: lax.all_to_all(a, PEERS, 0, 0, tiled=True)  19.8 us
    ppermute x4, starting transfers between devices, on_device(): swap = lambda a: lax.ppermute(a, 'c', SWAP)  12.4 us
    pallas_call x12, Pallas kernels, run(): pl.pallas_call(body, out_shape=[jax.ShapeDtypeStruct(shape, dtype) for sh...  6.69 us
  transfers between devices with their start and end apart: 4, of which 1 were waited for; matrix products, arithmetic and copies ran while one was open for 0% of the time, Pallas kernels for 2%

profile of v4, /device:TPU:1, one launch (start us, length us, event | category | flops | bytes accessed | tf_op | source)
XLA Modules:
  0.0 125.9 jit_solution(11212452453724818288)
XLA Ops:
  0.6 1.6 %shard_map.152 = (bf16[1024,128]{1,0:T(8,128)(2,1)S(1)}, bf16[512,128]{1,0:T(8,128)(2,1)S(1)}, bf16[512,128]{1,0:T(8,128)(2,1)S(1)}) custom-call(bf16[512,128]{1,0:T(8,128)(2,1)} %bitcast.37, f32[1,128]{1,0:T(1,128)} %bitcast.43, f32[1,128]{1,0:T(1,128)} %bitcast.46, bf16[128,512]{1,0:T(8,128)(2,1)} %w_in_ref.1), custom_call_target="tpu_custom_call" | custom-call | bytes 1048576 | tf_op jit(solution)/shard_map/pallas_call | solution.py:21
  2.2 0.0 copy-start.1
  2.2 0.0 copy-start.2
  2.2 0.0 copy-start.3
  2.3 0.0 copy-start.7
  2.3 24.3 %all_to_all.67 = bf16[64,16,128]{2,1,0:T(8,128)(2,1)S(1)} all-to-all(bf16[64,16,128]{2,1,0:T(8,128)(2,1)S(1)} %bitcast.36), channel_id=1, replica_groups=mesh['X'=2,'x'=2,'z'=8,'y'=4,'c'=2] {'x','z','y'}, dimensions={0} | all-to-all | bytes 524288 | tf_op jit(solution)/shard_map/all_to_all | solution.py:362
  26.6 3.4 %collective-permute-start = (bf16[1024,128]{1,0:T(8,128)(2,1)S(1)}, bf16[1024,128]{1,0:T(8,128)(2,1)S(1)}, u32[]{:S(2)}, u32[]{:S(2)}) collective-permute-start(bf16[1024,128]{1,0:T(8,128)(2,1)S(1)} %bitcast.26), channel_id=1, source_target_pairs={{0,1},{1,0},{2,3},{3,2},{4,5},{5,4},{6,7},{7,6},{8,9},{9,8},{10,11... | collective-permute-start | bytes 786440 | tf_op jit(solution)/shard_map/ppermute | solution.py:365
  30.0 0.0 copy-start.4
  30.0 0.0 copy-done.1
  30.0 0.0 copy-done.2
  30.0 0.0 copy-done.3
  30.0 0.0 copy-done.7
  30.0 0.6 copy-done.4
  30.6 0.6 shard_map.153
  31.2 0.0 collective-permute-done.other_ref
  31.2 0.5 shard_map.154
  31.7 14.3 %all_to_all.68 = bf16[64,8,128]{2,1,0:T(8,128)(2,1)S(1)} all-to-all(bf16[64,8,128]{2,1,0:T(8,128)(2,1)S(1)} %bitcast.39), channel_id=1, replica_groups=mesh['X'=2,'x'=2,'z'=8,'y'=4,'c'=2] {'x','z','y'}, dimensions={0} | all-to-all | bytes 262144 | tf_op jit(solution)/shard_map/all_to_all | solution.py:362
  46.0 0.2 shard_map.155
  46.2 14.7 %all_to_all.69 = bf16[64,8,128]{2,1,0:T(8,128)(2,1)S(1)} all-to-all(bf16[64,8,128]{2,1,0:T(8,128)(2,1)S(1)} %bitcast.35), channel_id=1, replica_groups=mesh['X'=2,'x'=2,'z'=8,'y'=4,'c'=2] {'x','z','y'}, dimensions={0} | all-to-all | bytes 262144 | tf_op jit(solution)/shard_map/all_to_all | solution.py:362
  60.9 0.4 shard_map.156
  61.3 2.6 %collective-permute-start.1 = (f32[512,128]{1,0:T(8,128)S(1)}, f32[512,128]{1,0:T(8,128)S(1)}, u32[]{:S(2)}, u32[]{:S(2)}) collective-permute-start(f32[512,128]{1,0:T(8,128)S(1)} %get-tuple-element.66), channel_id=1, source_target_pairs={{0,1},{1,0},{2,3},{3,2},{4,5},{5,4},{6,7},{7,6},{8,9},{9,8},{10,11... | collective-permute-start | bytes 786440 | tf_op jit(solution)/shard_map/ppermute | solution.py:365
  63.9 0.0 copy-start.5
  63.9 0.7 copy-done.5
  64.6 0.6 shard_map.157
  65.2 0.0 collective-permute-done.1.got_ref
  65.2 0.1 shard_map.158
  65.2 0.0 copy-start
  65.2 15.3 %all_to_all.70 = bf16[64,16,128]{2,1,0:T(8,128)(2,1)S(1)} all-to-all(bf16[64,16,128]{2,1,0:T(8,128)(2,1)S(1)} %bitcast.31), channel_id=1, replica_groups=mesh['X'=2,'x'=2,'z'=8,'y'=4,'c'=2] {'x','z','y'}, dimensions={0} | all-to-all | bytes 524288 | tf_op jit(solution)/shard_map/all_to_all | solution.py:362
  80.6 0.0 copy-done
  80.6 0.6 shard_map.159
  81.1 2.6 %collective-permute-start.2 = (f32[512,128]{1,0:T(8,128)S(1)}, f32[512,128]{1,0:T(8,128)S(1)}, u32[]{:S(2)}, u32[]{:S(2)}) collective-permute-start(f32[512,128]{1,0:T(8,128)S(1)} %get-tuple-element.81), channel_id=1, source_target_pairs={{0,1},{1,0},{2,3},{3,2},{4,5},{5,4},{6,7},{7,6},{8,9},{9,8},{10,11... | collective-permute-start | bytes 786440 | tf_op jit(solution)/shard_map/ppermute | solution.py:365
  83.8 0.0 copy-start.6
  83.8 0.7 copy-done.6
  84.4 0.9 shard_map.160
  85.4 0.0 collective-permute-done.2.got_ref
  85.4 0.2 shard_map.161
  85.6 14.6 %all_to_all.71 = bf16[64,8,128]{2,1,0:T(8,128)(2,1)S(1)} all-to-all(bf16[64,8,128]{2,1,0:T(8,128)(2,1)S(1)} %bitcast.32), channel_id=1, replica_groups=mesh['X'=2,'x'=2,'z'=8,'y'=4,'c'=2] {'x','z','y'}, dimensions={0} | all-to-all | bytes 262144 | tf_op jit(solution)/shard_map/all_to_all | solution.py:362
  100.2 0.2 shard_map.162
  100.4 19.8 %all_to_all.72 = bf16[128,8,128]{2,1,0:T(8,128)(2,1)S(1)} all-to-all(bf16[128,8,128]{2,1,0:T(8,128)(2,1)S(1)} %bitcast.30), channel_id=1, replica_groups=mesh['X'=2,'x'=2,'z'=8,'y'=4,'c'=2] {'X','x','z','y'}, dimensions={0} | all-to-all | bytes 524288 | tf_op jit(solution)/shard_map/all_to_all | solution.py:363
  120.2 3.7 %collective-permute-start.3 = (bf16[1024,128]{1,0:T(8,128)(2,1)S(1)}, bf16[1024,128]{1,0:T(8,128)(2,1)S(1)}, u32[]{:S(2)}, u32[]{:S(2)}) collective-permute-start(bf16[1024,128]{1,0:T(8,128)(2,1)S(1)} %bitcast.28), channel_id=1, source_target_pairs={{0,1},{1,0},{2,3},{3,2},{4,5},{5,4},{6,7},{7,6},{8,9},{9,8},{10,11... | collective-permute-start | bytes 786440 | tf_op jit(solution)/shard_map/ppermute | solution.py:365
  123.9 1.2 collective-permute-done.3.other_ref
  125.1 0.8 shard_map.163
Async XLA Ops:
  2.2 27.8 %copy-start.1 = (bf16[1,2,256,128]{3,2,1,0:T(8,128)(2,1)S(1)}, bf16[1,2,256,128]{3,2,1,0:T(8,128)(2,1)}, u32[]{:S(2)}) copy-start(bf16[1,2,256,128]{3,2,1,0:T(8,128)(2,1)} %param.9) | copy-start | bytes 393220
  2.2 27.8 %copy-start.2 = (bf16[128,128]{1,0:T(8,128)(2,1)S(1)}, bf16[128,128]{1,0:T(8,128)(2,1)}, u32[]{:S(2)}) copy-start(bf16[128,128]{1,0:T(8,128)(2,1)} %w_gate_ref.3) | copy-start | bytes 98308
  2.2 27.8 %copy-start.3 = (bf16[128,128]{1,0:T(8,128)(2,1)S(1)}, bf16[128,128]{1,0:T(8,128)(2,1)}, u32[]{:S(2)}) copy-start(bf16[128,128]{1,0:T(8,128)(2,1)} %w_out_ref.3) | copy-start | bytes 98308
  2.3 27.8 %copy-start.7 = (bf16[1,2,256,128]{3,2,1,0:T(8,128)(2,1)S(1)}, bf16[1,2,256,128]{3,2,1,0:T(8,128)(2,1)}, u32[]{:S(2)}) copy-start(bf16[1,2,256,128]{3,2,1,0:T(8,128)(2,1)} %param.10) | copy-start | bytes 393220
  26.6 4.7 %collective-permute-start = (bf16[1024,128]{1,0:T(8,128)(2,1)S(1)}, bf16[1024,128]{1,0:T(8,128)(2,1)S(1)}, u32[]{:S(2)}, u32[]{:S(2)}) collective-permute-start(bf16[1024,128]{1,0:T(8,128)(2,1)S(1)} %bitcast.26), channel_id=1, source_target_pairs={{0,1},{1,0},{2,3},{3,2},{4,5},{5,4},{6,7},{7,6},{8,9},{9,8},{10,11... | collective-permute-start | bytes 786440 | tf_op jit(solution)/shard_map/ppermute | solution.py:365
  30.0 0.7 copy-start.4
  61.3 3.9 %collective-permute-start.1 = (f32[512,128]{1,0:T(8,128)S(1)}, f32[512,128]{1,0:T(8,128)S(1)}, u32[]{:S(2)}, u32[]{:S(2)}) collective-permute-start(f32[512,128]{1,0:T(8,128)S(1)} %get-tuple-element.66), channel_id=1, source_target_pairs={{0,1},{1,0},{2,3},{3,2},{4,5},{5,4},{6,7},{7,6},{8,9},{9,8},{10,11... | collective-permute-start | bytes 786440 | tf_op jit(solution)/shard_map/ppermute | solution.py:365
  63.9 0.7 copy-start.5
  65.2 15.3 %copy-start = (bf16[128,512]{1,0:T(8,128)(2,1)S(1)}, bf16[128,512]{1,0:T(8,128)(2,1)}, u32[]{:S(2)}) copy-start(bf16[128,512]{1,0:T(8,128)(2,1)} %w_in_ref.1) | copy-start | bytes 393220
  81.1 4.2 %collective-permute-start.2 = (f32[512,128]{1,0:T(8,128)S(1)}, f32[512,128]{1,0:T(8,128)S(1)}, u32[]{:S(2)}, u32[]{:S(2)}) collective-permute-start(f32[512,128]{1,0:T(8,128)S(1)} %get-tuple-element.81), channel_id=1, source_target_pairs={{0,1},{1,0},{2,3},{3,2},{4,5},{5,4},{6,7},{7,6},{8,9},{9,8},{10,11... | collective-permute-start | bytes 786440 | tf_op jit(solution)/shard_map/ppermute | solution.py:365
  83.8 0.7 copy-start.6
  120.2 4.8 %collective-permute-start.3 = (bf16[1024,128]{1,0:T(8,128)(2,1)S(1)}, bf16[1024,128]{1,0:T(8,128)(2,1)S(1)}, u32[]{:S(2)}, u32[]{:S(2)}) collective-permute-start(bf16[1024,128]{1,0:T(8,128)(2,1)S(1)} %bitcast.28), channel_id=1, source_target_pairs={{0,1},{1,0},{2,3},{3,2},{4,5},{5,4},{6,7},{7,6},{8,9},{9,8},{10,11... | collective-permute-start | bytes 786440 | tf_op jit(solution)/shard_map/ppermute | solution.py:365

commit v5 on v4

--- a/solution.py
+++ b/solution.py
@@ -9,7 +9,6 @@
 
 EPSILON = 1e-05
 CHIPS = ("x", "z", "y")
-PEERS = ("X", "x", "z", "y")
 SWAP = [(0, 1), (1, 0)]
 LANES = 128
 F32 = jnp.float32
@@ -315,10 +314,14 @@
 
 
 def reduce_share(parts_ref, share_ref):
-    total = split_vectors(jnp.sum(parts_ref[...].astype(F32).reshape(-1, 8, LANES), axis=0))
-    share_ref[...] = (
-        jnp.broadcast_to(total[None], (share_ref.shape[0] // 8, 8, LANES))
-        .reshape(share_ref.shape)
+    share_ref[...] = jnp.sum(parts_ref[...].astype(F32).reshape(-1, 8, LANES), axis=0)
+
+
+def spread(share_ref, got_ref, copies_ref):
+    total = split_vectors(share_ref[...] + got_ref[...])
+    copies_ref[...] = (
+        jnp.broadcast_to(total[None], (copies_ref.shape[0] // 8, 8, LANES))
+        .reshape(copies_ref.shape)
         .astype(BF16)
     )
 
@@ -327,8 +330,7 @@
     own_ref, other_ref, w_in_ref, w_gate_ref, w_out_ref, in_gain_ref, in_bias_ref, out_gain_ref, out_bias_ref, low, high
 ):
     core = lax.axis_index("c")
-    own = jnp.sum(own_ref[...].astype(F32).reshape(2, *low.shape), axis=0)
-    other = jnp.sum(other_ref[...].astype(F32).reshape(2, *low.shape), axis=0)
+    own, other = own_ref[...].astype(F32), other_ref[...].astype(F32)
     low[...] = jnp.where(core == 0, own, other)
     high[...] = jnp.where(core == 0, other, own)
     channels = w_in_ref.shape[0]
@@ -360,7 +362,6 @@
     quarter = (4 * hidden, LANES)
     whole = (8 * hidden, LANES)
     to_chips = lambda a: lax.all_to_all(a, CHIPS, 0, 0, tiled=True)
-    to_peers = lambda a: lax.all_to_all(a, PEERS, 0, 0, tiled=True)
     stay = lambda a: pltpu.with_memory_space_constraint(a, pltpu.HBM)
     swap = lambda a: lax.ppermute(a, "c", SWAP)
 
@@ -414,8 +415,9 @@
     )
     got, pair_grad = lax.optimization_barrier((got, pair_grad))
     (parts,) = call(add, [(quarter, BF16)])(keep, got)
-    (share,) = call(reduce_share, [(whole, BF16)])(to_chips(parts))
-    mine = to_peers(share)
+    (share,) = call(reduce_share, [((8, LANES), F32)])(to_chips(parts))
+    (copies,) = call(spread, [(quarter, BF16)])(share, lax.ppermute(share, "X", SWAP))
+    mine = to_chips(copies)
     w_in_total, w_gate_total, w_out_total, *vectors = call(
         finish,
         [(w_in.shape, F32), (w_gate.shape, F32), (w_out.shape, F32)] + [((1, LANES), F32)] * 4,

time: 126 us -> 125 us (level)
  blocking collectives: 103 us -> 97.7 us
  starting transfers between devices: 12.4 us -> 15 us
  waiting for transfers between devices: 1.17 us -> 2.5 us
    all_to_all x1 -> x0, blocking collectives: 19.8 us -> none  [on_device(): to_peers = lambda a: lax.all_to_all(a, PEERS, 0, 0, tiled=True)]
    all_to_all x5 -> x6, blocking collectives: 83.1 us -> 97.7 us  [on_device(): to_chips = lambda a: lax.all_to_all(a, CHIPS, 0, 0, tiled=True)]
    ppermute x0 -> x1, starting transfers between devices: none -> 2.53 us  [on_device(): lax.ppermute(share, 'X', SWAP)]
    ppermute x0 -> x1, waiting for transfers between devices: none -> 1.51 us  [on_device(): lax.ppermute(share, 'X', SWAP)]
    pallas_call x12 -> x13, Pallas kernels: 6.69 us -> 6.66 us  [run(): pl.pallas_call(body, out_shape=[jax.ShapeDtypeStruct(shape, dtype) for sh...]
  transfers between devices with their start and end apart: 4 -> 5, of which waited for: 1 -> 2; matrix products, arithmetic and copies ran while one was open for 0% -> 0% of each run, Pallas kernels for 2% -> 2%
where the time goes in v5:
time: 125 us
  blocking collectives  97.7 us (78%)
  starting transfers between devices  15 us (12%)
  Pallas kernels  6.66 us (5%)
  waiting for transfers between devices  2.5 us (2%)
  local copies, waits for them, and re-layouts  1.98 us (2%)
    all_to_all x6, blocking collectives, on_device(): to_chips = lambda a: lax.all_to_all(a, CHIPS, 0, 0, tiled=True)  97.7 us
    ppermute x4, starting transfers between devices, on_device(): swap = lambda a: lax.ppermute(a, 'c', SWAP)  12.4 us
    pallas_call x13, Pallas kernels, run(): pl.pallas_call(body, out_shape=[jax.ShapeDtypeStruct(shape, dtype) for sh...  6.66 us
    ppermute x1, starting transfers between devices, on_device(): lax.ppermute(share, 'X', SWAP)  2.53 us
  transfers between devices with their start and end apart: 5, of which 2 were waited for; matrix products, arithmetic and copies ran while one was open for 0% of the time, Pallas kernels for 2%

profile of v5, /device:TPU:1, one launch (start us, length us, event | category | flops | bytes accessed | tf_op | source)
XLA Modules:
  0.0 124.6 jit_solution(6718523421203058736)
XLA Ops:
  0.6 1.6 %shard_map.152 = (bf16[1024,128]{1,0:T(8,128)(2,1)S(1)}, bf16[512,128]{1,0:T(8,128)(2,1)S(1)}, bf16[512,128]{1,0:T(8,128)(2,1)S(1)}) custom-call(bf16[512,128]{1,0:T(8,128)(2,1)} %bitcast.37, f32[1,128]{1,0:T(1,128)} %bitcast.43, f32[1,128]{1,0:T(1,128)} %bitcast.46, bf16[128,512]{1,0:T(8,128)(2,1)} %w_in_ref.1), custom_call_target="tpu_custom_call" | custom-call | bytes 1048576 | tf_op jit(solution)/shard_map/pallas_call | solution.py:20
  2.2 0.0 copy-start.1
  2.2 0.0 copy-start.2
  2.2 0.0 copy-start.3
  2.3 0.0 copy-start.7
  2.3 24.3 %all_to_all.67 = bf16[64,16,128]{2,1,0:T(8,128)(2,1)S(1)} all-to-all(bf16[64,16,128]{2,1,0:T(8,128)(2,1)S(1)} %bitcast.36), channel_id=1, replica_groups=mesh['X'=2,'x'=2,'z'=8,'y'=4,'c'=2] {'x','z','y'}, dimensions={0} | all-to-all | bytes 524288 | tf_op jit(solution)/shard_map/all_to_all | solution.py:364
  26.6 3.4 %collective-permute-start = (bf16[1024,128]{1,0:T(8,128)(2,1)S(1)}, bf16[1024,128]{1,0:T(8,128)(2,1)S(1)}, u32[]{:S(2)}, u32[]{:S(2)}) collective-permute-start(bf16[1024,128]{1,0:T(8,128)(2,1)S(1)} %bitcast.26), channel_id=1, source_target_pairs={{0,1},{1,0},{2,3},{3,2},{4,5},{5,4},{6,7},{7,6},{8,9},{9,8},{10,11... | collective-permute-start | bytes 786440 | tf_op jit(solution)/shard_map/ppermute | solution.py:366
  30.0 0.0 copy-start.4
  30.0 0.0 copy-done.1
  30.0 0.0 copy-done.2
  30.0 0.0 copy-done.3
  30.0 0.0 copy-done.7
  30.0 0.6 copy-done.4
  30.6 0.6 shard_map.153
  31.2 0.0 collective-permute-done.other_ref
  31.2 0.5 shard_map.154
  31.7 14.3 %all_to_all.68 = bf16[64,8,128]{2,1,0:T(8,128)(2,1)S(1)} all-to-all(bf16[64,8,128]{2,1,0:T(8,128)(2,1)S(1)} %bitcast.39), channel_id=1, replica_groups=mesh['X'=2,'x'=2,'z'=8,'y'=4,'c'=2] {'x','z','y'}, dimensions={0} | all-to-all | bytes 262144 | tf_op jit(solution)/shard_map/all_to_all | solution.py:364
  46.0 0.2 shard_map.155
  46.2 14.7 %all_to_all.69 = bf16[64,8,128]{2,1,0:T(8,128)(2,1)S(1)} all-to-all(bf16[64,8,128]{2,1,0:T(8,128)(2,1)S(1)} %bitcast.35), channel_id=1, replica_groups=mesh['X'=2,'x'=2,'z'=8,'y'=4,'c'=2] {'x','z','y'}, dimensions={0} | all-to-all | bytes 262144 | tf_op jit(solution)/shard_map/all_to_all | solution.py:364
  60.9 0.4 shard_map.156
  61.3 2.6 %collective-permute-start.1 = (f32[512,128]{1,0:T(8,128)S(1)}, f32[512,128]{1,0:T(8,128)S(1)}, u32[]{:S(2)}, u32[]{:S(2)}) collective-permute-start(f32[512,128]{1,0:T(8,128)S(1)} %get-tuple-element.66), channel_id=1, source_target_pairs={{0,1},{1,0},{2,3},{3,2},{4,5},{5,4},{6,7},{7,6},{8,9},{9,8},{10,11... | collective-permute-start | bytes 786440 | tf_op jit(solution)/shard_map/ppermute | solution.py:366
  63.9 0.0 copy-start.5
  63.9 0.7 copy-done.5
  64.6 0.6 shard_map.157
  65.2 0.0 collective-permute-done.1.got_ref
  65.2 0.1 shard_map.158
  65.2 0.0 copy-start
  65.2 15.3 %all_to_all.70 = bf16[64,16,128]{2,1,0:T(8,128)(2,1)S(1)} all-to-all(bf16[64,16,128]{2,1,0:T(8,128)(2,1)S(1)} %bitcast.28), channel_id=1, replica_groups=mesh['X'=2,'x'=2,'z'=8,'y'=4,'c'=2] {'x','z','y'}, dimensions={0} | all-to-all | bytes 524288 | tf_op jit(solution)/shard_map/all_to_all | solution.py:364
  80.6 0.0 copy-done
  80.6 0.6 shard_map.159
  81.1 2.6 %collective-permute-start.2 = (f32[512,128]{1,0:T(8,128)S(1)}, f32[512,128]{1,0:T(8,128)S(1)}, u32[]{:S(2)}, u32[]{:S(2)}) collective-permute-start(f32[512,128]{1,0:T(8,128)S(1)} %get-tuple-element.81), channel_id=1, source_target_pairs={{0,1},{1,0},{2,3},{3,2},{4,5},{5,4},{6,7},{7,6},{8,9},{9,8},{10,11... | collective-permute-start | bytes 786440 | tf_op jit(solution)/shard_map/ppermute | solution.py:366
  83.8 0.0 copy-start.6
  83.8 0.7 copy-done.6
  84.4 0.9 shard_map.160
  85.4 0.0 collective-permute-done.2.got_ref
  85.4 0.2 shard_map.161
  85.6 14.6 %all_to_all.71 = bf16[64,8,128]{2,1,0:T(8,128)(2,1)S(1)} all-to-all(bf16[64,8,128]{2,1,0:T(8,128)(2,1)S(1)} %bitcast.29), channel_id=1, replica_groups=mesh['X'=2,'x'=2,'z'=8,'y'=4,'c'=2] {'x','z','y'}, dimensions={0} | all-to-all | bytes 262144 | tf_op jit(solution)/shard_map/all_to_all | solution.py:364
  100.2 0.1 shard_map.162.share_ref
  100.2 2.5 %collective-permute-start.3 = (f32[8,128]{1,0:T(8,128)S(1)}, f32[8,128]{1,0:T(8,128)S(1)}, u32[]{:S(2)}, u32[]{:S(2)}) collective-permute-start(f32[8,128]{1,0:T(8,128)S(1)} %shard_map.162.share_ref), channel_id=1, source_target_pairs={{0,128},{128,0},{1,129},{129,1},{2,130},{130,2},{3,131},{131,3},{4... | collective-permute-start | bytes 12296 | tf_op jit(solution)/shard_map/ppermute | solution.py:419
  102.8 1.5 %collective-permute-done.3.got_ref = f32[8,128]{1,0:T(8,128)S(1)} collective-permute-done((f32[8,128]{1,0:T(8,128)S(1)}, f32[8,128]{1,0:T(8,128)S(1)}, u32[]{:S(2)}, u32[]{:S(2)}) %collective-permute-start.3) | collective-permute-done | bytes 4128 | tf_op jit(solution)/shard_map/ppermute | solution.py:419
  104.3 0.2 shard_map.163
  104.4 14.6 %all_to_all.72 = bf16[64,8,128]{2,1,0:T(8,128)(2,1)S(1)} all-to-all(bf16[64,8,128]{2,1,0:T(8,128)(2,1)S(1)} %bitcast.32), channel_id=1, replica_groups=mesh['X'=2,'x'=2,'z'=8,'y'=4,'c'=2] {'x','z','y'}, dimensions={0} | all-to-all | bytes 262144 | tf_op jit(solution)/shard_map/all_to_all | solution.py:364
  119.0 3.8 %collective-permute-start.4 = (bf16[512,128]{1,0:T(8,128)(2,1)S(1)}, bf16[512,128]{1,0:T(8,128)(2,1)S(1)}, u32[]{:S(2)}, u32[]{:S(2)}) collective-permute-start(bf16[512,128]{1,0:T(8,128)(2,1)S(1)} %bitcast.30), channel_id=1, source_target_pairs={{0,1},{1,0},{2,3},{3,2},{4,5},{5,4},{6,7},{7,6},{8,9},{9,8},{10,11... | collective-permute-start | bytes 393224 | tf_op jit(solution)/shard_map/ppermute | solution.py:366
  122.8 1.0 collective-permute-done.4.other_ref
  123.8 0.8 shard_map.164
Async XLA Ops:
  2.2 27.8 %copy-start.1 = (bf16[1,2,256,128]{3,2,1,0:T(8,128)(2,1)S(1)}, bf16[1,2,256,128]{3,2,1,0:T(8,128)(2,1)}, u32[]{:S(2)}) copy-start(bf16[1,2,256,128]{3,2,1,0:T(8,128)(2,1)} %param.9) | copy-start | bytes 393220
  2.2 27.8 %copy-start.2 = (bf16[128,128]{1,0:T(8,128)(2,1)S(1)}, bf16[128,128]{1,0:T(8,128)(2,1)}, u32[]{:S(2)}) copy-start(bf16[128,128]{1,0:T(8,128)(2,1)} %w_gate_ref.3) | copy-start | bytes 98308
  2.2 27.8 %copy-start.3 = (bf16[128,128]{1,0:T(8,128)(2,1)S(1)}, bf16[128,128]{1,0:T(8,128)(2,1)}, u32[]{:S(2)}) copy-start(bf16[128,128]{1,0:T(8,128)(2,1)} %w_out_ref.3) | copy-start | bytes 98308
  2.3 27.8 %copy-start.7 = (bf16[1,2,256,128]{3,2,1,0:T(8,128)(2,1)S(1)}, bf16[1,2,256,128]{3,2,1,0:T(8,128)(2,1)}, u32[]{:S(2)}) copy-start(bf16[1,2,256,128]{3,2,1,0:T(8,128)(2,1)} %param.10) | copy-start | bytes 393220
  26.6 4.7 %collective-permute-start = (bf16[1024,128]{1,0:T(8,128)(2,1)S(1)}, bf16[1024,128]{1,0:T(8,128)(2,1)S(1)}, u32[]{:S(2)}, u32[]{:S(2)}) collective-permute-start(bf16[1024,128]{1,0:T(8,128)(2,1)S(1)} %bitcast.26), channel_id=1, source_target_pairs={{0,1},{1,0},{2,3},{3,2},{4,5},{5,4},{6,7},{7,6},{8,9},{9,8},{10,11... | collective-permute-start | bytes 786440 | tf_op jit(solution)/shard_map/ppermute | solution.py:366
  30.0 0.7 copy-start.4
  61.3 3.9 %collective-permute-start.1 = (f32[512,128]{1,0:T(8,128)S(1)}, f32[512,128]{1,0:T(8,128)S(1)}, u32[]{:S(2)}, u32[]{:S(2)}) collective-permute-start(f32[512,128]{1,0:T(8,128)S(1)} %get-tuple-element.66), channel_id=1, source_target_pairs={{0,1},{1,0},{2,3},{3,2},{4,5},{5,4},{6,7},{7,6},{8,9},{9,8},{10,11... | collective-permute-start | bytes 786440 | tf_op jit(solution)/shard_map/ppermute | solution.py:366
  63.9 0.7 copy-start.5
  65.2 15.3 %copy-start = (bf16[128,512]{1,0:T(8,128)(2,1)S(1)}, bf16[128,512]{1,0:T(8,128)(2,1)}, u32[]{:S(2)}) copy-start(bf16[128,512]{1,0:T(8,128)(2,1)} %w_in_ref.1) | copy-start | bytes 393220
  81.1 4.2 %collective-permute-start.2 = (f32[512,128]{1,0:T(8,128)S(1)}, f32[512,128]{1,0:T(8,128)S(1)}, u32[]{:S(2)}, u32[]{:S(2)}) collective-permute-start(f32[512,128]{1,0:T(8,128)S(1)} %get-tuple-element.81), channel_id=1, source_target_pairs={{0,1},{1,0},{2,3},{3,2},{4,5},{5,4},{6,7},{7,6},{8,9},{9,8},{10,11... | collective-permute-start | bytes 786440 | tf_op jit(solution)/shard_map/ppermute | solution.py:366
  83.8 0.7 copy-start.6
  100.2 4.0 %collective-permute-start.3 = (f32[8,128]{1,0:T(8,128)S(1)}, f32[8,128]{1,0:T(8,128)S(1)}, u32[]{:S(2)}, u32[]{:S(2)}) collective-permute-start(f32[8,128]{1,0:T(8,128)S(1)} %shard_map.162.share_ref), channel_id=1, source_target_pairs={{0,128},{128,0},{1,129},{129,1},{2,130},{130,2},{3,131},{131,3},{4... | collective-permute-start | bytes 12296 | tf_op jit(solution)/shard_map/ppermute | solution.py:419
  119.0 4.7 %collective-permute-start.4 = (bf16[512,128]{1,0:T(8,128)(2,1)S(1)}, bf16[512,128]{1,0:T(8,128)(2,1)S(1)}, u32[]{:S(2)}, u32[]{:S(2)}) collective-permute-start(bf16[512,128]{1,0:T(8,128)(2,1)S(1)} %bitcast.30), channel_id=1, source_target_pairs={{0,1},{1,0},{2,3},{3,2},{4,5},{5,4},{6,7},{7,6},{8,9},{9,8},{10,11... | collective-permute-start | bytes 393224 | tf_op jit(solution)/shard_map/ppermute | solution.py:366

commit v6 on v5

--- a/solution.py
+++ b/solution.py
@@ -43,6 +43,10 @@
 
 def sigmoid(x):
     return jax.nn.sigmoid(x)
+
+
+def first_half():
+    return lax.axis_index("c") == lax.axis_index("X")
 
 
 def every(start, count, stride):
@@ -249,7 +253,7 @@
     edges_ref, factors_ref, normed_t_ref, hat_t_ref, w_in_ref, gate_term_ref, w_out_part_ref, w_gate_part_ref,
     vectors_ref, keep_ref, give_ref, grad_normed_ref, lefts, rights, low, high,
 ):
-    core = lax.axis_index("c")
+    first = first_half()
     hidden = w_in_ref.shape[1] // 4
     edges = edges_ref[...].astype(F32).reshape(-1, 16, LANES)
     lefts[...] = edges[:, :8, :].reshape(-1, LANES)
@@ -285,8 +289,8 @@
     high[every(1, channels, 4), :] = w_gate_part_ref[...]
     high[every(2, channels, 4), :] = w_out_part_ref[...]
     high[every(3, channels, 4), :] = vectors_ref[...]
-    keep_ref[...] = jnp.where(core == 0, low[...], high[...])
-    give_ref[...] = jnp.where(core == 0, high[...], low[...])
+    keep_ref[...] = jnp.where(first, low[...], high[...])
+    give_ref[...] = jnp.where(first, high[...], low[...])
 
 
 def beside_rear(grad_normed_ref, hat_t_ref, scale_ref, gain_ref, pair_grad_ref):
@@ -300,39 +304,40 @@
     pair_grad_ref[...] = jnp.transpose(grad).astype(BF16)
 
 
-def split_vectors(values):
-    lane = lax.broadcasted_iota(jnp.int32, values.shape, values.ndim - 1)
-    row = lax.broadcasted_iota(jnp.int32, values.shape, values.ndim - 2)
-    total = values + pltpu.roll(values, LANES - 2, values.ndim - 1)
-    high = total.astype(BF16).astype(F32)
-    low = pltpu.roll(total - high, 2, values.ndim - 1)
-    return jnp.where(row % 4 == 3, jnp.where(lane < 2, high, jnp.where(lane < 4, low, 0.0)), values)
-
-
-def add(keep_ref, got_ref, sum_ref):
-    sum_ref[...] = split_vectors(keep_ref[...] + got_ref[...]).astype(BF16)
+def split_vectors(sums, count):
+    at = every(3, count, 4)
+    values = sums[at, :]
+    sums[at, :] = columns(values[:, :1] + values[:, 2:3], values[:, 1:2] + values[:, 3:4])
+
+
+def add(keep_ref, got_ref, sum_ref, sums):
+    sums[...] = keep_ref[...] + got_ref[...]
+    split_vectors(sums, sums.shape[0] // 4)
+    sum_ref[...] = sums[...].astype(BF16)
 
 
 def reduce_share(parts_ref, share_ref):
     share_ref[...] = jnp.sum(parts_ref[...].astype(F32).reshape(-1, 8, LANES), axis=0)
 
 
-def spread(share_ref, got_ref, copies_ref):
-    total = split_vectors(share_ref[...] + got_ref[...])
+def spread(share_ref, got_ref, copies_ref, sums):
+    sums[...] = share_ref[...] + got_ref[...]
+    split_vectors(sums, 2)
     copies_ref[...] = (
-        jnp.broadcast_to(total[None], (copies_ref.shape[0] // 8, 8, LANES))
+        jnp.broadcast_to(sums[...][None], (copies_ref.shape[0] // 8, 8, LANES))
         .reshape(copies_ref.shape)
         .astype(BF16)
     )
 
 
 def finish(
-    own_ref, other_ref, w_in_ref, w_gate_ref, w_out_ref, in_gain_ref, in_bias_ref, out_gain_ref, out_bias_ref, low, high
-):
-    core = lax.axis_index("c")
+    own_ref, other_ref, w_in_ref, w_gate_ref, w_out_ref, in_gain_ref, in_bias_ref, out_gain_ref, out_bias_ref,
+    low, high,
+):
+    first = first_half()
     own, other = own_ref[...].astype(F32), other_ref[...].astype(F32)
-    low[...] = jnp.where(core == 0, own, other)
-    high[...] = jnp.where(core == 0, other, own)
+    low[...] = jnp.where(first, own, other)
+    high[...] = jnp.where(first, other, own)
     channels = w_in_ref.shape[0]
     for t in range(3):
         w_in_ref[:, t * LANES : (t + 1) * LANES] = low[every(t, channels, 4), :]
@@ -409,14 +414,15 @@
     keep, give, grad_normed = call(
         rear, [(quarter, F32), (quarter, F32), (grid, F32)], [quarter] * 4
     )(grad_edges, factors, normed_t, hat_t, w_in, gate_term, w_out_part, w_gate_part, vectors)
-    got = swap(give)
+    (parts,) = call(add, [(quarter, BF16)], [quarter])(keep, swap(give))
+    (share,) = call(reduce_share, [((8, LANES), F32)])(to_chips(parts))
+    share, grad_normed = lax.optimization_barrier((share, grad_normed))
+    got = lax.ppermute(share, ("X", "c"), [(0, 3), (1, 2), (2, 1), (3, 0)])
     (pair_grad,) = call(beside_rear, [((cells, channels), BF16)], work=1 << 28)(
         grad_normed, hat_t, scale, in_gain_row
     )
     got, pair_grad = lax.optimization_barrier((got, pair_grad))
-    (parts,) = call(add, [(quarter, BF16)])(keep, got)
-    (share,) = call(reduce_share, [((8, LANES), F32)])(to_chips(parts))
-    (copies,) = call(spread, [(quarter, BF16)])(share, lax.ppermute(share, "X", SWAP))
+    (copies,) = call(spread, [(quarter, BF16)], [(8, LANES)])(share, got)
     mine = to_chips(copies)
     w_in_total, w_gate_total, w_out_total, *vectors = call(
         finish,

time: 125 us -> 124 us (level)
    ppermute x1, starting transfers between devices: 2.53 us -> 4.4 us  [on_device(): got = lax.ppermute(share, ('X', 'c'), [(0, 3), (1, 2), (2, 1), (3, 0)])]
    ppermute x4, starting transfers between devices: 12.4 us -> 11 us  [on_device(): swap = lambda a: lax.ppermute(a, 'c', SWAP)]
  transfers between devices with their start and end apart: 5 -> 5, of which waited for: 2 -> 3; matrix products, arithmetic and copies ran while one was open for 0% -> 0% of each run, Pallas kernels for 2% -> 2%
where the time goes in v6:
time: 124 us
  blocking collectives  96.9 us (78%)
  starting transfers between devices  15.4 us (12%)
  Pallas kernels  6.7 us (5%)
  waiting for transfers between devices  2.49 us (2%)
  local copies, waits for them, and re-layouts  1.32 us (1%)
    all_to_all x6, blocking collectives, on_device(): to_chips = lambda a: lax.all_to_all(a, CHIPS, 0, 0, tiled=True)  96.9 us
    ppermute x4, starting transfers between devices, on_device(): swap = lambda a: lax.ppermute(a, 'c', SWAP)  11 us
    pallas_call x13, Pallas kernels, run(): pl.pallas_call(body, out_shape=[jax.ShapeDtypeStruct(shape, dtype) for sh...  6.7 us
    ppermute x1, starting transfers between devices, on_device(): got = lax.ppermute(share, ('X', 'c'), [(0, 3), (1, 2), (2, 1), (3, 0)])  4.4 us
  transfers between devices with their start and end apart: 5, of which 3 were waited for; matrix products, arithmetic and copies ran while one was open for 0% of the time, Pallas kernels for 2%

profile of v6, /device:TPU:1, one launch (start us, length us, event | category | flops | bytes accessed | tf_op | source)
XLA Modules:
  0.0 123.6 jit_solution(15544747814825335587)
XLA Ops:
  0.6 1.6 %shard_map.152 = (bf16[1024,128]{1,0:T(8,128)(2,1)S(1)}, bf16[512,128]{1,0:T(8,128)(2,1)S(1)}, bf16[512,128]{1,0:T(8,128)(2,1)S(1)}) custom-call(bf16[512,128]{1,0:T(8,128)(2,1)} %bitcast.37, f32[1,128]{1,0:T(1,128)} %bitcast.43, f32[1,128]{1,0:T(1,128)} %bitcast.46, bf16[128,512]{1,0:T(8,128)(2,1)} %w_in_ref.1), custom_call_target="tpu_custom_call" | custom-call | bytes 1048576 | tf_op jit(solution)/shard_map/pallas_call | solution.py:20
  2.2 0.0 copy-start.1
  2.2 0.0 copy-start.2
  2.2 0.0 copy-start.3
  2.3 0.0 copy-start.7
  2.3 24.3 %all_to_all.67 = bf16[64,16,128]{2,1,0:T(8,128)(2,1)S(1)} all-to-all(bf16[64,16,128]{2,1,0:T(8,128)(2,1)S(1)} %bitcast.36), channel_id=1, replica_groups=mesh['X'=2,'x'=2,'z'=8,'y'=4,'c'=2] {'x','z','y'}, dimensions={0} | all-to-all | bytes 524288 | tf_op jit(solution)/shard_map/all_to_all | solution.py:369
  26.6 3.4 %collective-permute-start = (bf16[1024,128]{1,0:T(8,128)(2,1)S(1)}, bf16[1024,128]{1,0:T(8,128)(2,1)S(1)}, u32[]{:S(2)}, u32[]{:S(2)}) collective-permute-start(bf16[1024,128]{1,0:T(8,128)(2,1)S(1)} %bitcast.26), channel_id=1, source_target_pairs={{0,1},{1,0},{2,3},{3,2},{4,5},{5,4},{6,7},{7,6},{8,9},{9,8},{10,11... | collective-permute-start | bytes 786440 | tf_op jit(solution)/shard_map/ppermute | solution.py:371
  30.0 0.0 copy-start.4
  30.0 0.0 copy-done.1
  30.0 0.0 copy-done.2
  30.0 0.0 copy-done.3
  30.0 0.0 copy-done.7
  30.0 0.6 copy-done.4
  30.6 0.6 shard_map.153
  31.2 0.0 collective-permute-done.other_ref
  31.2 0.5 shard_map.154
  31.7 14.3 %all_to_all.68 = bf16[64,8,128]{2,1,0:T(8,128)(2,1)S(1)} all-to-all(bf16[64,8,128]{2,1,0:T(8,128)(2,1)S(1)} %bitcast.39), channel_id=1, replica_groups=mesh['X'=2,'x'=2,'z'=8,'y'=4,'c'=2] {'x','z','y'}, dimensions={0} | all-to-all | bytes 262144 | tf_op jit(solution)/shard_map/all_to_all | solution.py:369
  46.0 0.2 shard_map.155
  46.2 14.7 %all_to_all.69 = bf16[64,8,128]{2,1,0:T(8,128)(2,1)S(1)} all-to-all(bf16[64,8,128]{2,1,0:T(8,128)(2,1)S(1)} %bitcast.35), channel_id=1, replica_groups=mesh['X'=2,'x'=2,'z'=8,'y'=4,'c'=2] {'x','z','y'}, dimensions={0} | all-to-all | bytes 262144 | tf_op jit(solution)/shard_map/all_to_all | solution.py:369
  60.9 0.4 shard_map.156
  61.3 2.6 %collective-permute-start.1 = (f32[512,128]{1,0:T(8,128)S(1)}, f32[512,128]{1,0:T(8,128)S(1)}, u32[]{:S(2)}, u32[]{:S(2)}) collective-permute-start(f32[512,128]{1,0:T(8,128)S(1)} %get-tuple-element.68), channel_id=1, source_target_pairs={{0,1},{1,0},{2,3},{3,2},{4,5},{5,4},{6,7},{7,6},{8,9},{9,8},{10,11... | collective-permute-start | bytes 786440 | tf_op jit(solution)/shard_map/ppermute | solution.py:371
  63.9 0.0 copy-start.5
  63.9 0.7 copy-done.5
  64.6 0.6 shard_map.157
  65.2 0.0 collective-permute-done.1.got_ref
  65.2 0.1 shard_map.158
  65.2 0.0 copy-start
  65.2 15.3 %all_to_all.70 = bf16[64,16,128]{2,1,0:T(8,128)(2,1)S(1)} all-to-all(bf16[64,16,128]{2,1,0:T(8,128)(2,1)S(1)} %bitcast.28), channel_id=1, replica_groups=mesh['X'=2,'x'=2,'z'=8,'y'=4,'c'=2] {'x','z','y'}, dimensions={0} | all-to-all | bytes 524288 | tf_op jit(solution)/shard_map/all_to_all | solution.py:369
  80.6 0.0 copy-done
  80.6 0.6 shard_map.159
  81.1 2.6 %collective-permute-start.2 = (f32[512,128]{1,0:T(8,128)S(1)}, f32[512,128]{1,0:T(8,128)S(1)}, u32[]{:S(2)}, u32[]{:S(2)}) collective-permute-start(f32[512,128]{1,0:T(8,128)S(1)} %get-tuple-element.84), channel_id=1, source_target_pairs={{0,1},{1,0},{2,3},{3,2},{4,5},{5,4},{6,7},{7,6},{8,9},{9,8},{10,11... | collective-permute-start | bytes 786440 | tf_op jit(solution)/shard_map/ppermute | solution.py:371
  83.8 1.2 collective-permute-done.2.got_ref
  84.9 0.2 shard_map.160
  85.2 14.5 %all_to_all.71 = bf16[64,8,128]{2,1,0:T(8,128)(2,1)S(1)} all-to-all(bf16[64,8,128]{2,1,0:T(8,128)(2,1)S(1)} %bitcast.29), channel_id=1, replica_groups=mesh['X'=2,'x'=2,'z'=8,'y'=4,'c'=2] {'x','z','y'}, dimensions={0} | all-to-all | bytes 262144 | tf_op jit(solution)/shard_map/all_to_all | solution.py:369
  99.7 0.1 shard_map.161.share_ref
  99.8 0.0 copy-start.6
  99.8 4.4 %collective-permute-start.3 = (f32[8,128]{1,0:T(8,128)S(1)}, f32[8,128]{1,0:T(8,128)S(1)}, u32[]{:S(2)}, u32[]{:S(2)}) collective-permute-start(f32[8,128]{1,0:T(8,128)S(1)} %shard_map.161.share_ref), channel_id=1, source_target_pairs={{0,129},{1,128},{128,1},{129,0},{2,131},{3,130},{130,3},{131,2},{4... | collective-permute-start | bytes 12296 | tf_op jit(solution)/shard_map/ppermute | solution.py:420
  104.2 0.0 copy-done.6
  104.2 1.0 shard_map.162
  105.1 0.3 collective-permute-done.3.got_ref
  105.5 0.2 shard_map.163
  105.6 13.8 %all_to_all.72 = bf16[64,8,128]{2,1,0:T(8,128)(2,1)S(1)} all-to-all(bf16[64,8,128]{2,1,0:T(8,128)(2,1)S(1)} %bitcast.32), channel_id=1, replica_groups=mesh['X'=2,'x'=2,'z'=8,'y'=4,'c'=2] {'x','z','y'}, dimensions={0} | all-to-all | bytes 262144 | tf_op jit(solution)/shard_map/all_to_all | solution.py:369
  119.4 2.4 %collective-permute-start.4 = (bf16[512,128]{1,0:T(8,128)(2,1)S(1)}, bf16[512,128]{1,0:T(8,128)(2,1)S(1)}, u32[]{:S(2)}, u32[]{:S(2)}) collective-permute-start(bf16[512,128]{1,0:T(8,128)(2,1)S(1)} %bitcast.30), channel_id=1, source_target_pairs={{0,1},{1,0},{2,3},{3,2},{4,5},{5,4},{6,7},{7,6},{8,9},{9,8},{10,11... | collective-permute-start | bytes 393224 | tf_op jit(solution)/shard_map/ppermute | solution.py:371
  121.8 1.0 collective-permute-done.4.other_ref
  122.8 0.8 shard_map.164
Async XLA Ops:
  2.2 27.8 %copy-start.1 = (bf16[1,2,256,128]{3,2,1,0:T(8,128)(2,1)S(1)}, bf16[1,2,256,128]{3,2,1,0:T(8,128)(2,1)}, u32[]{:S(2)}) copy-start(bf16[1,2,256,128]{3,2,1,0:T(8,128)(2,1)} %param.9) | copy-start | bytes 393220
  2.2 27.8 %copy-start.2 = (bf16[128,128]{1,0:T(8,128)(2,1)S(1)}, bf16[128,128]{1,0:T(8,128)(2,1)}, u32[]{:S(2)}) copy-start(bf16[128,128]{1,0:T(8,128)(2,1)} %w_gate_ref.3) | copy-start | bytes 98308
  2.2 27.8 %copy-start.3 = (bf16[128,128]{1,0:T(8,128)(2,1)S(1)}, bf16[128,128]{1,0:T(8,128)(2,1)}, u32[]{:S(2)}) copy-start(bf16[128,128]{1,0:T(8,128)(2,1)} %w_out_ref.3) | copy-start | bytes 98308
  2.3 27.8 %copy-start.7 = (bf16[1,2,256,128]{3,2,1,0:T(8,128)(2,1)S(1)}, bf16[1,2,256,128]{3,2,1,0:T(8,128)(2,1)}, u32[]{:S(2)}) copy-start(bf16[1,2,256,128]{3,2,1,0:T(8,128)(2,1)} %param.10) | copy-start | bytes 393220
  26.6 4.7 %collective-permute-start = (bf16[1024,128]{1,0:T(8,128)(2,1)S(1)}, bf16[1024,128]{1,0:T(8,128)(2,1)S(1)}, u32[]{:S(2)}, u32[]{:S(2)}) collective-permute-start(bf16[1024,128]{1,0:T(8,128)(2,1)S(1)} %bitcast.26), channel_id=1, source_target_pairs={{0,1},{1,0},{2,3},{3,2},{4,5},{5,4},{6,7},{7,6},{8,9},{9,8},{10,11... | collective-permute-start | bytes 786440 | tf_op jit(solution)/shard_map/ppermute | solution.py:371
  30.0 0.7 copy-start.4
  61.3 3.9 %collective-permute-start.1 = (f32[512,128]{1,0:T(8,128)S(1)}, f32[512,128]{1,0:T(8,128)S(1)}, u32[]{:S(2)}, u32[]{:S(2)}) collective-permute-start(f32[512,128]{1,0:T(8,128)S(1)} %get-tuple-element.68), channel_id=1, source_target_pairs={{0,1},{1,0},{2,3},{3,2},{4,5},{5,4},{6,7},{7,6},{8,9},{9,8},{10,11... | collective-permute-start | bytes 786440 | tf_op jit(solution)/shard_map/ppermute | solution.py:371
  63.9 0.7 copy-start.5
  65.2 15.3 %copy-start = (bf16[128,512]{1,0:T(8,128)(2,1)S(1)}, bf16[128,512]{1,0:T(8,128)(2,1)}, u32[]{:S(2)}) copy-start(bf16[128,512]{1,0:T(8,128)(2,1)} %w_in_ref.1) | copy-start | bytes 393220
  81.1 3.8 %collective-permute-start.2 = (f32[512,128]{1,0:T(8,128)S(1)}, f32[512,128]{1,0:T(8,128)S(1)}, u32[]{:S(2)}, u32[]{:S(2)}) collective-permute-start(f32[512,128]{1,0:T(8,128)S(1)} %get-tuple-element.84), channel_id=1, source_target_pairs={{0,1},{1,0},{2,3},{3,2},{4,5},{5,4},{6,7},{7,6},{8,9},{9,8},{10,11... | collective-permute-start | bytes 786440 | tf_op jit(solution)/shard_map/ppermute | solution.py:371
  99.8 4.4 %copy-start.6 = (f32[128]{0:T(128)S(1)}, f32[128]{0:T(128)}, u32[]{:S(2)}) copy-start(f32[128]{0:T(128)} %param.14) | copy-start | bytes 1540
  99.8 5.7 %collective-permute-start.3 = (f32[8,128]{1,0:T(8,128)S(1)}, f32[8,128]{1,0:T(8,128)S(1)}, u32[]{:S(2)}, u32[]{:S(2)}) collective-permute-start(f32[8,128]{1,0:T(8,128)S(1)} %shard_map.161.share_ref), channel_id=1, source_target_pairs={{0,129},{1,128},{128,1},{129,0},{2,131},{3,130},{130,3},{131,2},{4... | collective-permute-start | bytes 12296 | tf_op jit(solution)/shard_map/ppermute | solution.py:420
  119.4 3.3 %collective-permute-start.4 = (bf16[512,128]{1,0:T(8,128)(2,1)S(1)}, bf16[512,128]{1,0:T(8,128)(2,1)S(1)}, u32[]{:S(2)}, u32[]{:S(2)}) collective-permute-start(bf16[512,128]{1,0:T(8,128)(2,1)S(1)} %bitcast.30), channel_id=1, source_target_pairs={{0,1},{1,0},{2,3},{3,2},{4,5},{5,4},{6,7},{7,6},{8,9},{9,8},{10,11... | collective-permute-start | bytes 393224 | tf_op jit(solution)/shard_map/ppermute | solution.py:371

commit v7 on v6

v7 whole, which is shorter than its diff:
```python
import functools

import jax
import jax.numpy as jnp
from jax import lax
from jax.experimental import pallas as pl
from jax.experimental.pallas import tpu as pltpu
from jax.sharding import Mesh, PartitionSpec as P

EPSILON = 1e-05
CHIPS = ("x", "z", "y")
SWAP = [(0, 1), (1, 0)]
LANES = 128
F32 = jnp.float32
BF16 = jnp.bfloat16


def call(body, outs, scratch=(), work=0, far=0):
    def run(*operands):
        return pl.pallas_call(
            body,
            out_shape=[jax.ShapeDtypeStruct(shape, dtype) for shape, dtype in outs],
            in_specs=[pl.BlockSpec(memory_space=pltpu.HBM)] * far
            + [pl.BlockSpec(memory_space=pltpu.VMEM)] * (len(operands) - far),
            out_specs=[pl.BlockSpec(memory_space=pltpu.VMEM)] * len(outs),
            scratch_shapes=[pltpu.VMEM(s, F32) if isinstance(s, tuple) else s for s in scratch],
            compiler_params=pltpu.CompilerParams(vmem_limit_bytes=8 * 1024 * 1024),
            cost_estimate=pl.CostEstimate(
                flops=work, bytes_accessed=1 << 20, transcendentals=0
            ),
        )(*operands)

    return run


def dot_nt(a, b):
    return lax.dot_general(a, b, (((1,), (1,)), ((), ())), preferred_element_type=F32)


def dot_nn(a, b):
    return lax.dot_general(a, b, (((1,), (0,)), ((), ())), preferred_element_type=F32)


def sigmoid(x):
    return jax.nn.sigmoid(x)


def first_half():
    return lax.axis_index("c") == lax.axis_index("X")


def every(start, count, stride):
    return pl.ds(start, count, stride=stride)


def column(row):
    return jnp.transpose(jnp.broadcast_to(row, (LANES, row.shape[1])))[:, :1]


def front(
    pair_far, gain_far, bias_far, w_in_far, out_gain_far, out_bias_far, edges_ref, normed_ref, w_in_t_ref, norms_ref,
    rows, pair_ref, w_in_ref, gain_ref, bias_ref, out_gain_ref, out_bias_ref, arrived,
):
    copies = [
        pltpu.make_async_copy(source, target, arrived.at[n])
        for n, (source, target) in enumerate(
            [(pair_far, pair_ref), (gain_far, gain_ref), (bias_far, bias_ref), (w_in_far, w_in_ref),
             (out_gain_far, out_gain_ref), (out_bias_far, out_bias_ref)]
        )
    ]
    for copy in copies:
        copy.start()
    for copy in copies[:3]:
        copy.wait()
    values = pair_ref[...].astype(F32)
    center = values - jnp.mean(values, axis=1, keepdims=True)
    scale = lax.rsqrt(jnp.mean(center * center, axis=1, keepdims=True) + EPSILON)
    normed = (center * scale * gain_ref[...] + bias_ref[...]).astype(BF16)
    normed_ref[...] = normed
    for copy in copies[3:]:
        copy.wait()
    norms = [gain_ref[...], bias_ref[...], out_gain_ref[...], out_bias_ref[...]]
    norms_ref[...] = jnp.concatenate(norms + norms, axis=0)
    w_in_t = jnp.transpose(w_in_ref[...].astype(F32)).astype(BF16)
    w_in_t_ref[...] = w_in_t
    hidden = w_in_t.shape[0] // 4
    for side in range(2):
        proj = dot_nt(w_in_t[2 * side * hidden : (2 * side + 1) * hidden], normed)
        gate = dot_nt(w_in_t[(2 * side + 1) * hidden : (2 * side + 2) * hidden], normed)
        value = sigmoid(gate) * proj
        for u in range(4):
            rows[every(4 * side + u, hidden, 8), :] = value[:, u * LANES : (u + 1) * LANES]
    edges_ref[...] = rows[...].astype(BF16)


def beside_front(
    normed_ref, pair_ref, grad_ref, w_in_t_ref, w_gate_ref, w_out_ref, norms_ref,
    normed_t_ref, hat_t_ref, scale_ref, factors_ref, grad_t_ref, gate_t_ref, grad_lin_ref,
    grad_out_normed_ref, scaled_ref, mean_ref,
):
    hidden = w_out_ref.shape[0]
    normed = normed_ref[...]
    normed_t_ref[...] = jnp.transpose(normed.astype(F32)).astype(BF16)
    values = jnp.transpose(pair_ref[...].astype(F32))
    center = values - jnp.mean(values, axis=0, keepdims=True)
    scale = lax.rsqrt(jnp.mean(center * center, axis=0, keepdims=True) + EPSILON)
    hat_t_ref[...] = center * scale
    scale_ref[...] = jnp.broadcast_to(scale, scale_ref.shape)
    grad_t = jnp.transpose(grad_ref[...].astype(F32))
    grad_t_ref[...] = grad_t
    w_gate_t = jnp.transpose(w_gate_ref[...].astype(F32)).astype(BF16)
    gate = sigmoid(dot_nt(w_gate_t, normed))
    gate_t_ref[...] = gate
    grad_lin = (grad_t * gate).astype(BF16)
    grad_lin_ref[...] = grad_lin
    grad_out_normed = dot_nn(w_out_ref[...], grad_lin)
    grad_out_normed_ref[...] = grad_out_normed
    scaled = grad_out_normed * column(norms_ref[2:3, :])
    scaled_ref[...] = scaled
    mean_ref[...] = jnp.broadcast_to(jnp.mean(scaled, axis=0, keepdims=True), mean_ref.shape)
    factors_ref[...] = factors_of(w_in_t_ref, normed)


def factors_of(w_in_t_ref, normed):
    hidden = w_in_t_ref.shape[0] // 4
    at = pl.multiple_of(jnp.where(first_half(), 0, 2 * hidden), LANES)
    proj = dot_nt(w_in_t_ref[pl.ds(at, hidden), :], normed)
    sig = sigmoid(dot_nt(w_in_t_ref[pl.ds(at + hidden, hidden), :], normed))
    return jnp.concatenate([sig, proj * sig * (1.0 - sig)], axis=0)


def beside_back(
    pair_ref, norms_ref, w_in_t_ref, normed_t_ref, hat_t_ref, factors_ref,
    both_normed_ref, both_hat_ref, both_factors_ref,
):
    core = lax.axis_index("c")
    cells = pair_ref.shape[0]
    values = pair_ref[...].astype(F32)
    center = values - jnp.mean(values, axis=1, keepdims=True)
    hat = center * lax.rsqrt(jnp.mean(center * center, axis=1, keepdims=True) + EPSILON)
    normed = (hat * norms_ref[:1, :] + norms_ref[1:2, :]).astype(BF16)
    for both_ref, own, other in [
        (both_normed_ref, normed_t_ref[...].astype(F32), jnp.transpose(normed.astype(F32))),
        (both_hat_ref, hat_t_ref[...], jnp.transpose(hat)),
        (both_factors_ref, factors_ref[...], factors_of(w_in_t_ref, normed)),
    ]:
        both_ref[:, :cells] = jnp.where(core == 0, own, other).astype(both_ref.dtype)
        both_ref[:, cells:] = jnp.where(core == 0, other, own).astype(both_ref.dtype)


def contract(own_ref, other_ref, product_ref, left_ref, right_ref, own, other, natural, rows):
    core = lax.axis_index("c")
    own[...] = own_ref[...].astype(F32)
    other[...] = other_ref[...].astype(F32)
    chips = own.shape[0] // 16
    for ch in range(2):
        halves = []
        for kh in range(2):
            halves.append(
                jnp.concatenate([own[every(ch * 8 + 2 * r + kh, chips, 16), :] for r in range(2)], axis=0)
            )
            for r in range(2):
                at = every(ch * 8 + 4 + 2 * r + kh, chips, 16)
                mine, theirs = own[at, :], other[at, :]
                base = kh * 4 * chips + r
                natural[every(base, chips, 4), :] = jnp.where(core == 0, mine, theirs)
                natural[every(base + 2, chips, 4), :] = jnp.where(core == 0, theirs, mine)
        left = jnp.concatenate(halves, axis=1).astype(BF16)
        right = jnp.concatenate([natural[: 4 * chips, :], natural[4 * chips :, :]], axis=1).astype(BF16)
        left_ref[ch, : 2 * chips] = left
        theirs = [
            jnp.concatenate([other[every(ch * 8 + 2 * r + kh, chips, 16), :] for r in range(2)], axis=0)
            for kh in range(2)
        ]
        left_ref[ch, 2 * chips :] = jnp.concatenate(theirs, axis=1).astype(BF16)
        right_ref[ch] = right
        product = dot_nt(left, right)
        for r in range(2):
            for jh in range(2):
                rows[every(ch * 4 + 2 * r + jh, chips, 8), :] = product[
                    r * chips : (r + 1) * chips, jh * LANES : (jh + 1) * LANES
                ]
    product_ref[...] = rows[...].astype(BF16)


def out_norm(values):
    center = values - jnp.mean(values, axis=0, keepdims=True)
    scale = lax.rsqrt(jnp.mean(center * center, axis=0, keepdims=True) + EPSILON)
    return center * scale, scale


def middle(product_ref, scaled_ref, mean_ref, grad_ref, rows, grads):
    hidden = scaled_ref.shape[0]
    rows[...] = product_ref[...].astype(F32)
    for u in range(4):
        hat, scale = out_norm(rows[every(u, hidden, 4), :])
        at = slice(u * LANES, (u + 1) * LANES)
        scaled = scaled_ref[:, at]
        both = jnp.mean(scaled * hat, axis=0, keepdims=True)
        grads[every(u, hidden, 4), :] = scale * (scaled - mean_ref[:1, at] - hat * both)
    grad_ref[...] = grads[...].astype(BF16)


def beside_middle(
    product_ref, grad_out_normed_ref, grad_lin_ref, grad_t_ref, gate_t_ref, normed_t_ref,
    w_out_ref, w_gate_ref, norms_ref, keep_ref, give_ref, vectors_ref, gate_term_ref,
    rows,
):
    hidden = w_out_ref.shape[0]
    rows[...] = product_ref[...].astype(F32)
    hats, normed = [], []
    gain, bias = column(norms_ref[2:3, :]), column(norms_ref[3:4, :])
    for u in range(4):
        hat, _ = out_norm(rows[every(u, hidden, 4), :])
        hats.append(hat)
        normed.append((hat * gain + bias).astype(BF16))
    hat = jnp.concatenate(hats, axis=1)
    out_normed = jnp.concatenate(normed, axis=1)
    w_out_t = jnp.transpose(w_out_ref[...].astype(F32)).astype(BF16)
    outlin = dot_nn(w_out_t, out_normed)
    gate = gate_t_ref[...]
    grad_gate = (grad_t_ref[...] * outlin * gate * (1.0 - gate)).astype(BF16)
    first = first_half()
    w_out_part = dot_nt(out_normed, grad_lin_ref[...])
    w_gate_part = dot_nt(normed_t_ref[...], grad_gate)
    keep_ref[...] = jnp.where(first, w_gate_part, w_out_part)
    give_ref[...] = jnp.where(first, w_out_part, w_gate_part)
    gate_term_ref[...] = dot_nn(w_gate_ref[...], grad_gate)
    grad_out_normed = grad_out_normed_ref[...]
    lane = lax.broadcasted_iota(jnp.int32, vectors_ref.shape, 1)
    vectors_ref[...] = jnp.where(
        lane == 0,
        jnp.sum(grad_out_normed * hat, axis=1, keepdims=True),
        jnp.sum(grad_out_normed, axis=1, keepdims=True),
    )


def columns(*sums):
    lane = lax.broadcasted_iota(jnp.int32, (sums[0].shape[0], LANES), 1)
    high = [value.astype(BF16).astype(F32) for value in sums]
    out = jnp.zeros(lane.shape, F32)
    for n, value in enumerate(high + [value - top for value, top in zip(sums, high)]):
        out = jnp.where(lane == n, value, out)
    return out


def contract_back(grad_ref, other_ref, left_ref, right_ref, edges_ref, own, other, natural, edges):
    core, first = lax.axis_index("c"), first_half()
    own[...] = grad_ref[...].astype(F32)
    other[...] = other_ref[...].astype(F32)
    chips = own.shape[0] // 8
    for ch in range(2):
        halves = []
        for jh in range(2):
            halves.append(
                jnp.concatenate(
                    [rows[every(ch * 4 + 2 * r + jh, chips, 8), :] for rows in (own, other) for r in range(2)], axis=0
                )
            )
        grad = jnp.concatenate(halves, axis=1)
        grad_right = dot_nn(jnp.transpose(grad).astype(BF16), left_ref[ch])
        grad_left = dot_nn(grad.astype(BF16), right_ref[ch])
        natural[: 4 * chips, :] = grad_right[:, :LANES]
        natural[4 * chips :, :] = grad_right[:, LANES:]
        for c in range(2):
            for r in range(2):
                for kh in range(2):
                    at = slice(kh * LANES, (kh + 1) * LANES)
                    mine = grad_left[r * chips : (r + 1) * chips, at]
                    theirs = grad_left[(2 + r) * chips : (3 + r) * chips, at]
                    edges[every(ch * 8 + 4 * c + 2 * r + kh, chips, 16), :] = jnp.where(
                        first,
                        jnp.where(core == c, mine, theirs),
                        natural[every(kh * 4 * chips + 2 * c + r, chips, 4), :],
                    )
    edges_ref[...] = edges[...].astype(BF16)


def rear(
    edges_ref, factors_ref, normed_t_ref, hat_t_ref, w_in_ref, gate_term_ref, keep_ref, got_ref, vectors_ref,
    parts_ref, grad_normed_ref, give_ref, rows, parts,
):
    core, first = lax.axis_index("c"), first_half()
    hidden = w_in_ref.shape[1] // 4
    cells = gate_term_ref.shape[1]
    rows[...] = edges_ref[...].astype(F32)
    pieces = []
    for u in range(8):
        at = slice(u * LANES, (u + 1) * LANES)
        grad = rows[every(u, hidden, 8), :]
        pieces.append(
            jnp.concatenate([grad * factors_ref[:hidden, at], grad * factors_ref[hidden:, at]], axis=0).astype(BF16)
        )
    grad_projected = jnp.concatenate(pieces, axis=1)
    w_in_part = dot_nt(normed_t_ref[...], grad_projected)
    w_in = w_in_ref[...].astype(F32)
    w_in = jnp.where(first, w_in[:, : 2 * hidden], w_in[:, 2 * hidden :]).astype(BF16)
    grad_normed = dot_nn(w_in, grad_projected)
    low, high = grad_normed[:, :cells], grad_normed[:, cells:]
    gate_term = gate_term_ref[...]
    low = low + jnp.where(core == 0, gate_term, 0.0)
    high = high + jnp.where(core == 0, 0.0, gate_term)
    grad_normed_ref[...] = jnp.where(core == 0, low, high)
    give_ref[...] = jnp.where(core == 0, high, low)
    channels = w_in_part.shape[0]
    for t in range(2):
        parts[every(t, channels, 4), :] = w_in_part[:, t * LANES : (t + 1) * LANES]
    parts[every(2, channels, 4), :] = keep_ref[...] + got_ref[...]
    gain = jnp.sum(low * hat_t_ref[:, :cells] + high * hat_t_ref[:, cells:], axis=1, keepdims=True)
    parts[every(3, channels, 4), :] = columns(
        gain, jnp.sum(low + high, axis=1, keepdims=True), vectors_ref[:, :1], vectors_ref[:, 1:2]
    )
    parts_ref[...] = parts[...].astype(BF16)


def beside_rear(grad_normed_ref, got_ref, hat_t_ref, scale_ref, norms_ref, pair_grad_ref):
    hat = hat_t_ref[...]
    scaled = (grad_normed_ref[...] + got_ref[...]) * column(norms_ref[:1, :])
    grad = scale_ref[:1, :] * (
        scaled
        - jnp.mean(scaled, axis=0, keepdims=True)
        - hat * jnp.mean(scaled * hat, axis=0, keepdims=True)
    )
    pair_grad_ref[...] = jnp.transpose(grad).astype(BF16)


def split_vectors(sums, count):
    at = every(3, count, 4)
    values = sums[at, :]
    sums[at, :] = columns(*(values[:, n : n + 1] + values[:, n + 4 : n + 5] for n in range(4)))


def reduce_share(parts_ref, share_ref):
    share_ref[...] = jnp.sum(parts_ref[...].astype(F32).reshape(-1, 8, LANES), axis=0)


def spread(share_ref, got_ref, copies_ref, sums):
    sums[...] = share_ref[...] + got_ref[...]
    split_vectors(sums, 2)
    copies_ref[...] = (
        jnp.broadcast_to(sums[...][None], (copies_ref.shape[0] // 8, 8, LANES))
        .reshape(copies_ref.shape)
        .astype(BF16)
    )


def finish(
    own_ref, other_ref, w_in_ref, w_gate_ref, w_out_ref, in_gain_ref, in_bias_ref, out_gain_ref, out_bias_ref,
    low, high,
):
    first = first_half()
    own, other = own_ref[...].astype(F32), other_ref[...].astype(F32)
    low[...] = jnp.where(first, own, other)
    high[...] = jnp.where(first, other, own)
    channels = w_in_ref.shape[0]
    for t in range(2):
        w_in_ref[:, t * LANES : (t + 1) * LANES] = low[every(t, channels, 4), :]
        w_in_ref[:, (2 + t) * LANES : (3 + t) * LANES] = high[every(t, channels, 4), :]
    w_gate_ref[...] = low[every(2, channels, 4), :]
    w_out_ref[...] = high[every(2, channels, 4), :]
    sums = jnp.transpose(low[every(3, channels, 4), :] + high[every(3, channels, 4), :])
    sums = sums[:4] + sums[4:8]
    in_gain_ref[...], in_bias_ref[...] = sums[:1], sums[1:2]
    out_gain_ref[...], out_bias_ref[...] = sums[2:3], sums[3:4]


def on_device(
    pair, grad_out, w_in, w_gate, w_out, ln_in_gain, ln_in_bias, ln_out_gain, ln_out_bias
):
    shape = pair.shape
    channels = shape[3]
    hidden = w_out.shape[0]
    cells = shape[1] * shape[2]
    full_len = shape[2]
    pair2 = pair.reshape(cells, channels)
    grad2 = grad_out.reshape(cells, channels)
    in_gain_row, in_bias_row = ln_in_gain.reshape(1, -1), ln_in_bias.reshape(1, -1)
    out_gain_row, out_bias_row = ln_out_gain.reshape(1, -1), ln_out_bias.reshape(1, -1)
    grid = (hidden, cells)
    quarter = (4 * hidden, LANES)
    whole = (8 * hidden, LANES)
    to_chips = lambda a: lax.all_to_all(a, CHIPS, 0, 0, tiled=True)
    stay = lambda a: pltpu.with_memory_space_constraint(a, pltpu.HBM)
    swap = lambda a: lax.ppermute(a, "c", SWAP)

    edges, normed, w_in_t, norms = call(
        front, [(whole, BF16), ((cells, channels), BF16), ((4 * hidden, channels), BF16), ((8, LANES), F32)],
        [
            whole, pltpu.VMEM((cells, channels), BF16), pltpu.VMEM(w_in.shape, BF16), (1, channels), (1, channels),
            (1, channels), (1, channels),
            pltpu.SemaphoreType.DMA((6,)),
        ],
        far=6,
    )(stay(pair2), stay(in_gain_row), stay(in_bias_row), stay(w_in), stay(out_gain_row), stay(out_bias_row))
    own, normed, pair_again = lax.optimization_barrier((to_chips(edges), normed, pair2))
    other = swap(own)
    pair_other = swap(pair_again)
    normed_t, hat_t, scale, factors, grad_t, gate_t, grad_lin, grad_out_normed, scaled, mean = call(
        beside_front,
        [
            (grid, BF16), (grid, F32), ((8, cells), F32), ((2 * hidden, cells), F32), (grid, F32), (grid, F32),
            (grid, BF16), (grid, F32), (grid, F32), ((8, cells), F32),
        ],
        work=1 << 28,
    )(normed, pair2, grad2, w_in_t, w_gate, w_out, norms)
    other, normed_t, pair_other = lax.optimization_barrier((other, normed_t, pair_other))
    product, left, right = call(
        contract,
        [(quarter, BF16), ((2, full_len, full_len), BF16), ((2, full_len, full_len), BF16)],
        [whole, whole, quarter, quarter],
    )(own, other)
    product = to_chips(product)
    (grad_product,) = call(middle, [(quarter, BF16)], [quarter, quarter])(product, scaled, mean)
    grad_cols = to_chips(grad_product)
    grad_cols, product, pair_other = lax.optimization_barrier((grad_cols, product, pair_other))
    grad_other = swap(grad_cols)
    keep, give, vectors, gate_term = call(
        beside_middle,
        [((hidden, channels), F32), ((channels, channels), F32), ((hidden, LANES), F32), (grid, F32)],
        [quarter],
        work=1 << 28,
    )(product, grad_out_normed, grad_lin, grad_t, gate_t, normed_t, w_out, w_gate, norms)
    both = (channels, 2 * cells)
    both_normed, both_hat, both_factors = call(
        beside_back, [(both, BF16), (both, F32), ((2 * hidden, 2 * cells), F32)], work=1 << 28
    )(pair_other, norms, w_in_t, normed_t, hat_t, factors)
    grad_other, gate_term, both_hat = lax.optimization_barrier((grad_other, gate_term, both_hat))
    got = swap(give)
    (grad_edges,) = call(contract_back, [(whole, BF16)], [quarter, quarter, quarter, whole])(
        grad_cols, grad_other, left, right
    )
    grad_edges, got = lax.optimization_barrier((grad_edges, got))
    grad_edges = to_chips(grad_edges)
    parts, grad_normed, give = call(
        rear, [(quarter, BF16), (grid, F32), (grid, F32)], [whole, quarter]
    )(grad_edges, both_factors, both_normed, both_hat, w_in, gate_term, keep, got, vectors)
    (share,) = call(reduce_share, [((8, LANES), F32)])(to_chips(parts))
    share, give = lax.optimization_barrier((share, give))
    got = lax.ppermute(share, ("X", "c"), [(0, 3), (1, 2), (2, 1), (3, 0)])
    (pair_grad,) = call(beside_rear, [((cells, channels), BF16)], work=1 << 28)(
        grad_normed, swap(give), hat_t, scale, norms
    )
    got, pair_grad = lax.optimization_barrier((got, pair_grad))
    (copies,) = call(spread, [(quarter, BF16)], [(8, LANES)])(share, got)
    mine = to_chips(copies)
    w_in_total, w_gate_total, w_out_total, *vectors = call(
        finish,
        [(w_in.shape, F32), (w_gate.shape, F32), (w_out.shape, F32)] + [((1, LANES), F32)] * 4,
        [quarter, quarter],
    )(mine, swap(mine))
    return (
        pair_grad.reshape(shape),
        w_in_total,
        w_gate_total,
        w_out_total,
        *(vector.reshape(-1) for vector in vectors),
    )


def solution(mesh):
    fine = Mesh(mesh.devices.reshape(2, 2, 8, 4, 2), ("X", "x", "z", "y", "c"))
    cells = P("X", ("x", "z", "y", "c"), None, None)
    in_specs = (cells, cells, P(), P(), P(), P(), P(), P(), P())
    out_specs = (cells, P(), P(), P(), P(), P(), P(), P())
    return jax.shard_map(
        on_device, mesh=fine, in_specs=in_specs, out_specs=out_specs, check_vma=False
    )
```

time: 124 us -> 123 us (level)
  starting transfers between devices: 15.4 us -> 12.9 us
  blocking collectives: 96.9 us -> 98.5 us
  local copies, waits for them, and re-layouts: 1.32 us -> 0.03 us
    ppermute x1, starting transfers between devices: 4.4 us -> 2.44 us  [on_device(): got = lax.ppermute(share, ('X', 'c'), [(0, 3), (1, 2), (2, 1), (3, 0)])]
    all_to_all x6, blocking collectives: 96.9 us -> 98.5 us  [on_device(): to_chips = lambda a: lax.all_to_all(a, CHIPS, 0, 0, tiled=True)]
    unnamed x16 -> x10, local copies, waits for them, and re-layouts: 1.32 us -> 0.03 us
    ppermute x4 -> x6, starting transfers between devices: 11 us -> 10.5 us  [on_device(): swap = lambda a: lax.ppermute(a, 'c', SWAP)]
    pallas_call x13 -> x12, Pallas kernels: 6.7 us -> 7.11 us  [run(): pl.pallas_call(body, out_shape=[jax.ShapeDtypeStruct(shape, dtype) for sh...]
  transfers between devices with their start and end apart: 5 -> 7, of which waited for: 3 -> 4; matrix products, arithmetic and copies ran while one was open for 0% -> 0% of each run, Pallas kernels for 2% -> 3%
where the time goes in v7:
time: 123 us; the launch traced here: 122 us
  blocking collectives  98.5 us (80%)
  starting transfers between devices  12.9 us (10%)
  Pallas kernels  7.11 us (6%)
  waiting for transfers between devices  3.15 us (3%)
    all_to_all x6, blocking collectives, on_device(): to_chips = lambda a: lax.all_to_all(a, CHIPS, 0, 0, tiled=True)  98.5 us
    ppermute x6, starting transfers between devices, on_device(): swap = lambda a: lax.ppermute(a, 'c', SWAP)  10.5 us
    pallas_call x12, Pallas kernels, run(): pl.pallas_call(body, out_shape=[jax.ShapeDtypeStruct(shape, dtype) for sh...  7.11 us
  transfers between devices with their start and end apart: 7, of which 4 were waited for; matrix products, arithmetic and copies ran while one was open for 0% of the time, Pallas kernels for 3%

profile of v7, /device:TPU:1, one launch (start us, length us, event | category | flops | bytes accessed | tf_op | source)
XLA Modules:
  0.0 122.5 jit_solution(13239124992897278660)
XLA Ops:
  0.6 1.6 %shard_map.152 = (bf16[1024,128]{1,0:T(8,128)(2,1)S(1)}, bf16[512,128]{1,0:T(8,128)(2,1)S(1)}, bf16[512,128]{1,0:T(8,128)(2,1)S(1)}, f32[8,128]{1,0:T(8,128)S(1)}) custom-call(bf16[512,128]{1,0:T(8,128)(2,1)} %bitcast.37, f32[1,128]{1,0:T(1,128)} %bitcast.43, f32[1,128]{1,0:T(1,128)} %bitcast.44, bf16[128,512]{1,0:T(8,128)(2,1)} %w_in_ref.1, ...), custom_call_target="tpu_custom_call" | custom-call | bytes 1048576 | tf_op jit(solution)/shard_map/pallas_call | solution.py:20
  2.2 0.0 copy-start.1
  2.3 0.0 copy-start.2
  2.3 0.0 copy-start.3
  2.3 0.0 copy-start.4
  2.3 24.3 %all_to_all.68 = bf16[64,16,128]{2,1,0:T(8,128)(2,1)S(1)} all-to-all(bf16[64,16,128]{2,1,0:T(8,128)(2,1)S(1)} %bitcast.36), channel_id=1, replica_groups=mesh['X'=2,'x'=2,'z'=8,'y'=4,'c'=2] {'x','z','y'}, dimensions={0} | all-to-all | bytes 524288 | tf_op jit(solution)/shard_map/all_to_all | solution.py:382
  26.6 3.4 %collective-permute-start = (bf16[1024,128]{1,0:T(8,128)(2,1)S(1)}, bf16[1024,128]{1,0:T(8,128)(2,1)S(1)}, u32[]{:S(2)}, u32[]{:S(2)}) collective-permute-start(bf16[1024,128]{1,0:T(8,128)(2,1)S(1)} %bitcast.25), channel_id=1, source_target_pairs={{0,1},{1,0},{2,3},{3,2},{4,5},{5,4},{6,7},{7,6},{8,9},{9,8},{10,11... | collective-permute-start | bytes 786440 | tf_op jit(solution)/shard_map/ppermute | solution.py:384
  30.0 0.0 copy-done.1
  30.0 0.0 collective-permute-start.1
  30.0 0.0 copy-done.2
  30.0 0.0 copy-done.3
  30.0 0.0 copy-done.4
  30.0 0.5 shard_map.153
  30.6 0.8 collective-permute-done.1.pair_ref
  31.4 0.0 collective-permute-done.other_ref
  31.4 0.6 shard_map.154
  32.0 14.3 %all_to_all.69 = bf16[64,8,128]{2,1,0:T(8,128)(2,1)S(1)} all-to-all(bf16[64,8,128]{2,1,0:T(8,128)(2,1)S(1)} %bitcast.41), channel_id=1, replica_groups=mesh['X'=2,'x'=2,'z'=8,'y'=4,'c'=2] {'x','z','y'}, dimensions={0} | all-to-all | bytes 262144 | tf_op jit(solution)/shard_map/all_to_all | solution.py:382
  46.2 0.2 shard_map.155
  46.4 14.7 %all_to_all.70 = bf16[64,8,128]{2,1,0:T(8,128)(2,1)S(1)} all-to-all(bf16[64,8,128]{2,1,0:T(8,128)(2,1)S(1)} %bitcast.33), channel_id=1, replica_groups=mesh['X'=2,'x'=2,'z'=8,'y'=4,'c'=2] {'x','z','y'}, dimensions={0} | all-to-all | bytes 262144 | tf_op jit(solution)/shard_map/all_to_all | solution.py:382
  61.1 2.5 %collective-permute-start.2 = (bf16[512,128]{1,0:T(8,128)(2,1)S(1)}, bf16[512,128]{1,0:T(8,128)(2,1)S(1)}, u32[]{:S(2)}, u32[]{:S(2)}) collective-permute-start(bf16[512,128]{1,0:T(8,128)(2,1)S(1)} %bitcast.34), channel_id=1, source_target_pairs={{0,1},{1,0},{2,3},{3,2},{4,5},{5,4},{6,7},{7,6},{8,9},{9,8},{10,11... | collective-permute-start | bytes 393224 | tf_op jit(solution)/shard_map/ppermute | solution.py:384
  63.6 0.6 shard_map.156
  64.2 0.1 collective-permute-start.3
  64.3 0.5 shard_map.157
  64.9 0.0 collective-permute-done.2.other_ref
  64.9 0.5 shard_map.158
  65.4 0.2 collective-permute-done.3.got_ref
  65.6 0.0 copy-start
  65.6 15.2 %all_to_all.71 = bf16[64,16,128]{2,1,0:T(8,128)(2,1)S(1)} all-to-all(bf16[64,16,128]{2,1,0:T(8,128)(2,1)S(1)} %bitcast.27), channel_id=1, replica_groups=mesh['X'=2,'x'=2,'z'=8,'y'=4,'c'=2] {'x','z','y'}, dimensions={0} | all-to-all | bytes 524288 | tf_op jit(solution)/shard_map/all_to_all | solution.py:382
  80.8 0.0 copy-done
  80.8 0.6 shard_map.159
  81.4 16.0 %all_to_all.72 = bf16[64,8,128]{2,1,0:T(8,128)(2,1)S(1)} all-to-all(bf16[64,8,128]{2,1,0:T(8,128)(2,1)S(1)} %bitcast.40), channel_id=1, replica_groups=mesh['X'=2,'x'=2,'z'=8,'y'=4,'c'=2] {'x','z','y'}, dimensions={0} | all-to-all | bytes 262144 | tf_op jit(solution)/shard_map/all_to_all | solution.py:382
  97.4 0.1 shard_map.160.share_ref
  97.5 2.7 %collective-permute-start.5 = (f32[128,512]{1,0:T(8,128)S(1)}, f32[128,512]{1,0:T(8,128)S(1)}, u32[]{:S(2)}, u32[]{:S(2)}) collective-permute-start(f32[128,512]{1,0:T(8,128)S(1)} %get-tuple-element.101), channel_id=1, source_target_pairs={{0,1},{1,0},{2,3},{3,2},{4,5},{5,4},{6,7},{7,6},{8,9},{9,8},{10,11... | collective-permute-start | bytes 786440 | tf_op jit(solution)/shard_map/ppermute | solution.py:384
  100.2 2.4 %collective-permute-start.4 = (f32[8,128]{1,0:T(8,128)S(1)}, f32[8,128]{1,0:T(8,128)S(1)}, u32[]{:S(2)}, u32[]{:S(2)}) collective-permute-start(f32[8,128]{1,0:T(8,128)S(1)} %shard_map.160.share_ref), channel_id=1, source_target_pairs={{0,129},{1,128},{128,1},{129,0},{2,131},{3,130},{130,3},{131,2},{4... | collective-permute-start | bytes 12296 | tf_op jit(solution)/shard_map/ppermute | solution.py:439
  102.7 0.0 collective-permute-done.5.got_ref
  102.7 1.0 shard_map.161
  103.6 1.2 collective-permute-done.4.got_ref
  104.8 0.2 shard_map.162
  104.9 14.0 %all_to_all.73 = bf16[64,8,128]{2,1,0:T(8,128)(2,1)S(1)} all-to-all(bf16[64,8,128]{2,1,0:T(8,128)(2,1)S(1)} %bitcast.31), channel_id=1, replica_groups=mesh['X'=2,'x'=2,'z'=8,'y'=4,'c'=2] {'x','z','y'}, dimensions={0} | all-to-all | bytes 262144 | tf_op jit(solution)/shard_map/all_to_all | solution.py:382
  118.9 1.8 %collective-permute-start.6 = (bf16[512,128]{1,0:T(8,128)(2,1)S(1)}, bf16[512,128]{1,0:T(8,128)(2,1)S(1)}, u32[]{:S(2)}, u32[]{:S(2)}) collective-permute-start(bf16[512,128]{1,0:T(8,128)(2,1)S(1)} %bitcast.29), channel_id=1, source_target_pairs={{0,1},{1,0},{2,3},{3,2},{4,5},{5,4},{6,7},{7,6},{8,9},{9,8},{10,11... | collective-permute-start | bytes 393224 | tf_op jit(solution)/shard_map/ppermute | solution.py:384
  120.7 1.0 collective-permute-done.6.other_ref
  121.7 0.8 shard_map.163
Async XLA Ops:
  2.2 27.8 %copy-start.1 = (bf16[1,2,256,128]{3,2,1,0:T(8,128)(2,1)S(1)}, bf16[1,2,256,128]{3,2,1,0:T(8,128)(2,1)}, u32[]{:S(2)}) copy-start(bf16[1,2,256,128]{3,2,1,0:T(8,128)(2,1)} %param.9) | copy-start | bytes 393220
  2.3 27.8 %copy-start.2 = (bf16[128,128]{1,0:T(8,128)(2,1)S(1)}, bf16[128,128]{1,0:T(8,128)(2,1)}, u32[]{:S(2)}) copy-start(bf16[128,128]{1,0:T(8,128)(2,1)} %w_gate_ref.3) | copy-start | bytes 98308
  2.3 27.8 %copy-start.3 = (bf16[128,128]{1,0:T(8,128)(2,1)S(1)}, bf16[128,128]{1,0:T(8,128)(2,1)}, u32[]{:S(2)}) copy-start(bf16[128,128]{1,0:T(8,128)(2,1)} %w_out_ref.3) | copy-start | bytes 98308
  2.3 27.8 %copy-start.4 = (bf16[1,2,256,128]{3,2,1,0:T(8,128)(2,1)S(1)}, bf16[1,2,256,128]{3,2,1,0:T(8,128)(2,1)}, u32[]{:S(2)}) copy-start(bf16[1,2,256,128]{3,2,1,0:T(8,128)(2,1)} %param.10) | copy-start | bytes 393220
  26.6 4.8 %collective-permute-start = (bf16[1024,128]{1,0:T(8,128)(2,1)S(1)}, bf16[1024,128]{1,0:T(8,128)(2,1)S(1)}, u32[]{:S(2)}, u32[]{:S(2)}) collective-permute-start(bf16[1024,128]{1,0:T(8,128)(2,1)S(1)} %bitcast.25), channel_id=1, source_target_pairs={{0,1},{1,0},{2,3},{3,2},{4,5},{5,4},{6,7},{7,6},{8,9},{9,8},{10,11... | collective-permute-start | bytes 786440 | tf_op jit(solution)/shard_map/ppermute | solution.py:384
  30.0 1.3 %collective-permute-start.1 = (bf16[512,128]{1,0:T(8,128)(2,1)S(1)}, bf16[512,128]{1,0:T(8,128)(2,1)S(1)}, u32[]{:S(2)}, u32[]{:S(2)}) collective-permute-start(bf16[512,128]{1,0:T(8,128)(2,1)S(1)} %bitcast.38), channel_id=1, source_target_pairs={{0,1},{1,0},{2,3},{3,2},{4,5},{5,4},{6,7},{7,6},{8,9},{9,8},{10,11... | collective-permute-start | bytes 393224 | tf_op jit(solution)/shard_map/ppermute | solution.py:384
  61.1 3.7 %collective-permute-start.2 = (bf16[512,128]{1,0:T(8,128)(2,1)S(1)}, bf16[512,128]{1,0:T(8,128)(2,1)S(1)}, u32[]{:S(2)}, u32[]{:S(2)}) collective-permute-start(bf16[512,128]{1,0:T(8,128)(2,1)S(1)} %bitcast.34), channel_id=1, source_target_pairs={{0,1},{1,0},{2,3},{3,2},{4,5},{5,4},{6,7},{7,6},{8,9},{9,8},{10,11... | collective-permute-start | bytes 393224 | tf_op jit(solution)/shard_map/ppermute | solution.py:384
  64.2 1.3 %collective-permute-start.3 = (f32[128,128]{1,0:T(8,128)S(1)}, f32[128,128]{1,0:T(8,128)S(1)}, u32[]{:S(2)}, u32[]{:S(2)}) collective-permute-start(f32[128,128]{1,0:T(8,128)S(1)} %get-tuple-element.88), channel_id=1, source_target_pairs={{0,1},{1,0},{2,3},{3,2},{4,5},{5,4},{6,7},{7,6},{8,9},{9,8},{10,11... | collective-permute-start | bytes 196616 | tf_op jit(solution)/shard_map/ppermute | solution.py:384
  65.6 15.2 %copy-start = (bf16[128,512]{1,0:T(8,128)(2,1)S(1)}, bf16[128,512]{1,0:T(8,128)(2,1)}, u32[]{:S(2)}) copy-start(bf16[128,512]{1,0:T(8,128)(2,1)} %w_in_ref.1) | copy-start | bytes 393220
  97.5 5.2 %collective-permute-start.5 = (f32[128,512]{1,0:T(8,128)S(1)}, f32[128,512]{1,0:T(8,128)S(1)}, u32[]{:S(2)}, u32[]{:S(2)}) collective-permute-start(f32[128,512]{1,0:T(8,128)S(1)} %get-tuple-element.101), channel_id=1, source_target_pairs={{0,1},{1,0},{2,3},{3,2},{4,5},{5,4},{6,7},{7,6},{8,9},{9,8},{10,11... | collective-permute-start | bytes 786440 | tf_op jit(solution)/shard_map/ppermute | solution.py:384
  100.2 4.6 %collective-permute-start.4 = (f32[8,128]{1,0:T(8,128)S(1)}, f32[8,128]{1,0:T(8,128)S(1)}, u32[]{:S(2)}, u32[]{:S(2)}) collective-permute-start(f32[8,128]{1,0:T(8,128)S(1)} %shard_map.160.share_ref), channel_id=1, source_target_pairs={{0,129},{1,128},{128,1},{129,0},{2,131},{3,130},{130,3},{131,2},{4... | collective-permute-start | bytes 12296 | tf_op jit(solution)/shard_map/ppermute | solution.py:439
  118.9 2.7 %collective-permute-start.6 = (bf16[512,128]{1,0:T(8,128)(2,1)S(1)}, bf16[512,128]{1,0:T(8,128)(2,1)S(1)}, u32[]{:S(2)}, u32[]{:S(2)}) collective-permute-start(bf16[512,128]{1,0:T(8,128)(2,1)S(1)} %bitcast.29), channel_id=1, source_target_pairs={{0,1},{1,0},{2,3},{3,2},{4,5},{5,4},{6,7},{7,6},{8,9},{9,8},{10,11... | collective-permute-start | bytes 393224 | tf_op jit(solution)/shard_map/ppermute | solution.py:384

commit v8 on v7

--- a/solution.py
+++ b/solution.py
@@ -435,19 +435,22 @@
         rear, [(quarter, BF16), (grid, F32), (grid, F32)], [whole, quarter]
     )(grad_edges, both_factors, both_normed, both_hat, w_in, gate_term, keep, got, vectors)
     (share,) = call(reduce_share, [((8, LANES), F32)])(to_chips(parts))
-    share, give = lax.optimization_barrier((share, give))
     got = lax.ppermute(share, ("X", "c"), [(0, 3), (1, 2), (2, 1), (3, 0)])
+    (copies,) = call(spread, [(quarter, BF16)], [(8, LANES)])(share, got)
+    copies, give = lax.optimization_barrier((copies, give))
+    part = swap(give)
+    mine = to_chips(copies)
+    mine, part, grad_normed = lax.optimization_barrier((mine, part, grad_normed))
+    theirs = swap(mine)
     (pair_grad,) = call(beside_rear, [((cells, channels), BF16)], work=1 << 28)(
-        grad_normed, swap(give), hat_t, scale, norms
-    )
-    got, pair_grad = lax.optimization_barrier((got, pair_grad))
-    (copies,) = call(spread, [(quarter, BF16)], [(8, LANES)])(share, got)
-    mine = to_chips(copies)
+        grad_normed, part, hat_t, scale, norms
+    )
+    theirs, pair_grad = lax.optimization_barrier((theirs, pair_grad))
     w_in_total, w_gate_total, w_out_total, *vectors = call(
         finish,
         [(w_in.shape, F32), (w_gate.shape, F32), (w_out.shape, F32)] + [((1, LANES), F32)] * 4,
         [quarter, quarter],
-    )(mine, swap(mine))
+    )(mine, theirs)
     return (
         pair_grad.reshape(shape),
         w_in_total,

time: 123 us -> 123 us (level)
    ppermute x1, starting transfers between devices: 2.44 us -> 5.08 us  [on_device(): got = lax.ppermute(share, ('X', 'c'), [(0, 3), (1, 2), (2, 1), (3, 0)])]
    ppermute x6, starting transfers between devices: 10.5 us -> 8.81 us  [on_device(): swap = lambda a: lax.ppermute(a, 'c', SWAP)]
  transfers between devices with their start and end apart: 7 -> 7, of which waited for: 4 -> 3; matrix products, arithmetic and copies ran while one was open for 0% -> 0% of each run, Pallas kernels for 3% -> 3%
where the time goes in v8:
time: 123 us
  blocking collectives  98.4 us (80%)
  starting transfers between devices  13.9 us (11%)
  Pallas kernels  7.11 us (6%)
  waiting for transfers between devices  2.33 us (2%)
    all_to_all x6, blocking collectives, on_device(): to_chips = lambda a: lax.all_to_all(a, CHIPS, 0, 0, tiled=True)  98.4 us
    ppermute x6, starting transfers between devices, on_device(): swap = lambda a: lax.ppermute(a, 'c', SWAP)  8.81 us
    pallas_call x12, Pallas kernels, run(): pl.pallas_call(body, out_shape=[jax.ShapeDtypeStruct(shape, dtype) for sh...  7.11 us
    ppermute x1, starting transfers between devices, on_device(): got = lax.ppermute(share, ('X', 'c'), [(0, 3), (1, 2), (2, 1), (3, 0)])  5.08 us
  transfers between devices with their start and end apart: 7, of which 3 were waited for; matrix products, arithmetic and copies ran while one was open for 0% of the time, Pallas kernels for 3%

profile of v8, /device:TPU:1, one launch (start us, length us, event | category | flops | bytes accessed | tf_op | source)
XLA Modules:
  0.0 122.6 jit_solution(5396010922824470001)
XLA Ops:
  0.6 1.6 %shard_map.152 = (bf16[1024,128]{1,0:T(8,128)(2,1)S(1)}, bf16[512,128]{1,0:T(8,128)(2,1)S(1)}, bf16[512,128]{1,0:T(8,128)(2,1)S(1)}, f32[8,128]{1,0:T(8,128)S(1)}) custom-call(bf16[512,128]{1,0:T(8,128)(2,1)} %bitcast.37, f32[1,128]{1,0:T(1,128)} %bitcast.43, f32[1,128]{1,0:T(1,128)} %bitcast.44, bf16[128,512]{1,0:T(8,128)(2,1)} %w_in_ref.1, ...), custom_call_target="tpu_custom_call" | custom-call | bytes 1048576 | tf_op jit(solution)/shard_map/pallas_call | solution.py:20
  2.2 0.0 copy-start.1
  2.3 0.0 copy-start.2
  2.3 0.0 copy-start.3
  2.3 0.0 copy-start.4
  2.3 24.3 %all_to_all.69 = bf16[64,16,128]{2,1,0:T(8,128)(2,1)S(1)} all-to-all(bf16[64,16,128]{2,1,0:T(8,128)(2,1)S(1)} %bitcast.36), channel_id=1, replica_groups=mesh['X'=2,'x'=2,'z'=8,'y'=4,'c'=2] {'x','z','y'}, dimensions={0} | all-to-all | bytes 524288 | tf_op jit(solution)/shard_map/all_to_all | solution.py:382
  26.6 3.4 %collective-permute-start = (bf16[1024,128]{1,0:T(8,128)(2,1)S(1)}, bf16[1024,128]{1,0:T(8,128)(2,1)S(1)}, u32[]{:S(2)}, u32[]{:S(2)}) collective-permute-start(bf16[1024,128]{1,0:T(8,128)(2,1)S(1)} %bitcast.25), channel_id=1, source_target_pairs={{0,1},{1,0},{2,3},{3,2},{4,5},{5,4},{6,7},{7,6},{8,9},{9,8},{10,11... | collective-permute-start | bytes 786440 | tf_op jit(solution)/shard_map/ppermute | solution.py:384
  30.0 0.0 copy-done.1
  30.0 0.0 collective-permute-start.1
  30.0 0.0 copy-done.2
  30.0 0.0 copy-done.3
  30.0 0.0 copy-done.4
  30.0 0.5 shard_map.153
  30.6 0.8 collective-permute-done.1.pair_ref
  31.4 0.0 collective-permute-done.other_ref
  31.4 0.6 shard_map.154
  32.0 14.3 %all_to_all.70 = bf16[64,8,128]{2,1,0:T(8,128)(2,1)S(1)} all-to-all(bf16[64,8,128]{2,1,0:T(8,128)(2,1)S(1)} %bitcast.41), channel_id=1, replica_groups=mesh['X'=2,'x'=2,'z'=8,'y'=4,'c'=2] {'x','z','y'}, dimensions={0} | all-to-all | bytes 262144 | tf_op jit(solution)/shard_map/all_to_all | solution.py:382
  46.2 0.2 shard_map.155
  46.4 14.7 %all_to_all.71 = bf16[64,8,128]{2,1,0:T(8,128)(2,1)S(1)} all-to-all(bf16[64,8,128]{2,1,0:T(8,128)(2,1)S(1)} %bitcast.33), channel_id=1, replica_groups=mesh['X'=2,'x'=2,'z'=8,'y'=4,'c'=2] {'x','z','y'}, dimensions={0} | all-to-all | bytes 262144 | tf_op jit(solution)/shard_map/all_to_all | solution.py:382
  61.1 2.5 %collective-permute-start.2 = (bf16[512,128]{1,0:T(8,128)(2,1)S(1)}, bf16[512,128]{1,0:T(8,128)(2,1)S(1)}, u32[]{:S(2)}, u32[]{:S(2)}) collective-permute-start(bf16[512,128]{1,0:T(8,128)(2,1)S(1)} %bitcast.34), channel_id=1, source_target_pairs={{0,1},{1,0},{2,3},{3,2},{4,5},{5,4},{6,7},{7,6},{8,9},{9,8},{10,11... | collective-permute-start | bytes 393224 | tf_op jit(solution)/shard_map/ppermute | solution.py:384
  63.6 0.6 shard_map.156
  64.2 0.1 collective-permute-start.3
  64.3 0.5 shard_map.157
  64.9 0.0 collective-permute-done.2.other_ref
  64.9 0.5 shard_map.158
  65.4 0.2 collective-permute-done.3.got_ref
  65.6 0.0 copy-start
  65.6 15.2 %all_to_all.72 = bf16[64,16,128]{2,1,0:T(8,128)(2,1)S(1)} all-to-all(bf16[64,16,128]{2,1,0:T(8,128)(2,1)S(1)} %bitcast.27), channel_id=1, replica_groups=mesh['X'=2,'x'=2,'z'=8,'y'=4,'c'=2] {'x','z','y'}, dimensions={0} | all-to-all | bytes 524288 | tf_op jit(solution)/shard_map/all_to_all | solution.py:382
  80.8 0.0 copy-done
  80.8 0.6 shard_map.159
  81.4 16.0 %all_to_all.73 = bf16[64,8,128]{2,1,0:T(8,128)(2,1)S(1)} all-to-all(bf16[64,8,128]{2,1,0:T(8,128)(2,1)S(1)} %bitcast.40), channel_id=1, replica_groups=mesh['X'=2,'x'=2,'z'=8,'y'=4,'c'=2] {'x','z','y'}, dimensions={0} | all-to-all | bytes 262144 | tf_op jit(solution)/shard_map/all_to_all | solution.py:382
  97.4 0.1 shard_map.160.share_ref
  97.5 5.1 %collective-permute-start.4 = (f32[8,128]{1,0:T(8,128)S(1)}, f32[8,128]{1,0:T(8,128)S(1)}, u32[]{:S(2)}, u32[]{:S(2)}) collective-permute-start(f32[8,128]{1,0:T(8,128)S(1)} %shard_map.160.share_ref), channel_id=1, source_target_pairs={{0,129},{1,128},{128,1},{129,0},{2,131},{3,130},{130,3},{131,2},{4... | collective-permute-start | bytes 12296 | tf_op jit(solution)/shard_map/ppermute | solution.py:438
  102.6 1.3 %collective-permute-done.4.got_ref = f32[8,128]{1,0:T(8,128)S(1)} collective-permute-done((f32[8,128]{1,0:T(8,128)S(1)}, f32[8,128]{1,0:T(8,128)S(1)}, u32[]{:S(2)}, u32[]{:S(2)}) %collective-permute-start.4) | collective-permute-done | bytes 4128 | tf_op jit(solution)/shard_map/ppermute | solution.py:438
  103.8 0.2 shard_map.161
  104.0 1.0 collective-permute-start.5
  105.0 13.9 %all_to_all.74 = bf16[64,8,128]{2,1,0:T(8,128)(2,1)S(1)} all-to-all(bf16[64,8,128]{2,1,0:T(8,128)(2,1)S(1)} %bitcast.31), channel_id=1, replica_groups=mesh['X'=2,'x'=2,'z'=8,'y'=4,'c'=2] {'x','z','y'}, dimensions={0} | all-to-all | bytes 262144 | tf_op jit(solution)/shard_map/all_to_all | solution.py:382
  118.9 0.0 collective-permute-done.5.got_ref
  118.9 1.8 %collective-permute-start.6 = (bf16[512,128]{1,0:T(8,128)(2,1)S(1)}, bf16[512,128]{1,0:T(8,128)(2,1)S(1)}, u32[]{:S(2)}, u32[]{:S(2)}) collective-permute-start(bf16[512,128]{1,0:T(8,128)(2,1)S(1)} %bitcast.29), channel_id=1, source_target_pairs={{0,1},{1,0},{2,3},{3,2},{4,5},{5,4},{6,7},{7,6},{8,9},{9,8},{10,11... | collective-permute-start | bytes 393224 | tf_op jit(solution)/shard_map/ppermute | solution.py:384
  120.8 1.0 shard_map.162
  121.7 0.0 collective-permute-done.6.other_ref
  121.7 0.8 shard_map.163
Async XLA Ops:
  2.2 27.8 %copy-start.1 = (bf16[1,2,256,128]{3,2,1,0:T(8,128)(2,1)S(1)}, bf16[1,2,256,128]{3,2,1,0:T(8,128)(2,1)}, u32[]{:S(2)}) copy-start(bf16[1,2,256,128]{3,2,1,0:T(8,128)(2,1)} %param.9) | copy-start | bytes 393220
  2.3 27.8 %copy-start.2 = (bf16[128,128]{1,0:T(8,128)(2,1)S(1)}, bf16[128,128]{1,0:T(8,128)(2,1)}, u32[]{:S(2)}) copy-start(bf16[128,128]{1,0:T(8,128)(2,1)} %w_gate_ref.3) | copy-start | bytes 98308
  2.3 27.8 %copy-start.3 = (bf16[128,128]{1,0:T(8,128)(2,1)S(1)}, bf16[128,128]{1,0:T(8,128)(2,1)}, u32[]{:S(2)}) copy-start(bf16[128,128]{1,0:T(8,128)(2,1)} %w_out_ref.3) | copy-start | bytes 98308
  2.3 27.8 %copy-start.4 = (bf16[1,2,256,128]{3,2,1,0:T(8,128)(2,1)S(1)}, bf16[1,2,256,128]{3,2,1,0:T(8,128)(2,1)}, u32[]{:S(2)}) copy-start(bf16[1,2,256,128]{3,2,1,0:T(8,128)(2,1)} %param.10) | copy-start | bytes 393220
  26.6 4.8 %collective-permute-start = (bf16[1024,128]{1,0:T(8,128)(2,1)S(1)}, bf16[1024,128]{1,0:T(8,128)(2,1)S(1)}, u32[]{:S(2)}, u32[]{:S(2)}) collective-permute-start(bf16[1024,128]{1,0:T(8,128)(2,1)S(1)} %bitcast.25), channel_id=1, source_target_pairs={{0,1},{1,0},{2,3},{3,2},{4,5},{5,4},{6,7},{7,6},{8,9},{9,8},{10,11... | collective-permute-start | bytes 786440 | tf_op jit(solution)/shard_map/ppermute | solution.py:384
  30.0 1.3 %collective-permute-start.1 = (bf16[512,128]{1,0:T(8,128)(2,1)S(1)}, bf16[512,128]{1,0:T(8,128)(2,1)S(1)}, u32[]{:S(2)}, u32[]{:S(2)}) collective-permute-start(bf16[512,128]{1,0:T(8,128)(2,1)S(1)} %bitcast.38), channel_id=1, source_target_pairs={{0,1},{1,0},{2,3},{3,2},{4,5},{5,4},{6,7},{7,6},{8,9},{9,8},{10,11... | collective-permute-start | bytes 393224 | tf_op jit(solution)/shard_map/ppermute | solution.py:384
  61.1 3.7 %collective-permute-start.2 = (bf16[512,128]{1,0:T(8,128)(2,1)S(1)}, bf16[512,128]{1,0:T(8,128)(2,1)S(1)}, u32[]{:S(2)}, u32[]{:S(2)}) collective-permute-start(bf16[512,128]{1,0:T(8,128)(2,1)S(1)} %bitcast.34), channel_id=1, source_target_pairs={{0,1},{1,0},{2,3},{3,2},{4,5},{5,4},{6,7},{7,6},{8,9},{9,8},{10,11... | collective-permute-start | bytes 393224 | tf_op jit(solution)/shard_map/ppermute | solution.py:384
  64.2 1.3 %collective-permute-start.3 = (f32[128,128]{1,0:T(8,128)S(1)}, f32[128,128]{1,0:T(8,128)S(1)}, u32[]{:S(2)}, u32[]{:S(2)}) collective-permute-start(f32[128,128]{1,0:T(8,128)S(1)} %get-tuple-element.91), channel_id=1, source_target_pairs={{0,1},{1,0},{2,3},{3,2},{4,5},{5,4},{6,7},{7,6},{8,9},{9,8},{10,11... | collective-permute-start | bytes 196616 | tf_op jit(solution)/shard_map/ppermute | solution.py:384
  65.6 15.2 %copy-start = (bf16[128,512]{1,0:T(8,128)(2,1)S(1)}, bf16[128,512]{1,0:T(8,128)(2,1)}, u32[]{:S(2)}) copy-start(bf16[128,512]{1,0:T(8,128)(2,1)} %w_in_ref.1) | copy-start | bytes 393220
  97.5 6.4 %collective-permute-start.4 = (f32[8,128]{1,0:T(8,128)S(1)}, f32[8,128]{1,0:T(8,128)S(1)}, u32[]{:S(2)}, u32[]{:S(2)}) collective-permute-start(f32[8,128]{1,0:T(8,128)S(1)} %shard_map.160.share_ref), channel_id=1, source_target_pairs={{0,129},{1,128},{128,1},{129,0},{2,131},{3,130},{130,3},{131,2},{4... | collective-permute-start | bytes 12296 | tf_op jit(solution)/shard_map/ppermute | solution.py:438
  104.0 14.9 %collective-permute-start.5 = (f32[128,512]{1,0:T(8,128)S(1)}, f32[128,512]{1,0:T(8,128)S(1)}, u32[]{:S(2)}, u32[]{:S(2)}) collective-permute-start(f32[128,512]{1,0:T(8,128)S(1)} %get-tuple-element.103), channel_id=1, source_target_pairs={{0,1},{1,0},{2,3},{3,2},{4,5},{5,4},{6,7},{7,6},{8,9},{9,8},{10,11... | collective-permute-start | bytes 786440 | tf_op jit(solution)/shard_map/ppermute | solution.py:384
  118.9 2.8 %collective-permute-start.6 = (bf16[512,128]{1,0:T(8,128)(2,1)S(1)}, bf16[512,128]{1,0:T(8,128)(2,1)S(1)}, u32[]{:S(2)}, u32[]{:S(2)}) collective-permute-start(bf16[512,128]{1,0:T(8,128)(2,1)S(1)} %bitcast.29), channel_id=1, source_target_pairs={{0,1},{1,0},{2,3},{3,2},{4,5},{5,4},{6,7},{7,6},{8,9},{9,8},{10,11... | collective-permute-start | bytes 393224 | tf_op jit(solution)/shard_map/ppermute | solution.py:384

commit v9 on v7

--- a/solution.py
+++ b/solution.py
@@ -258,21 +258,27 @@
                 )
             )
         grad = jnp.concatenate(halves, axis=1)
-        grad_right = dot_nn(jnp.transpose(grad).astype(BF16), left_ref[ch])
-        grad_left = dot_nn(grad.astype(BF16), right_ref[ch])
-        natural[: 4 * chips, :] = grad_right[:, :LANES]
-        natural[4 * chips :, :] = grad_right[:, LANES:]
-        for c in range(2):
-            for r in range(2):
-                for kh in range(2):
-                    at = slice(kh * LANES, (kh + 1) * LANES)
-                    mine = grad_left[r * chips : (r + 1) * chips, at]
-                    theirs = grad_left[(2 + r) * chips : (3 + r) * chips, at]
-                    edges[every(ch * 8 + 4 * c + 2 * r + kh, chips, 16), :] = jnp.where(
-                        first,
-                        jnp.where(core == c, mine, theirs),
-                        natural[every(kh * 4 * chips + 2 * c + r, chips, 4), :],
-                    )
+        places = [(c, r, kh) for c in range(2) for r in range(2) for kh in range(2)]
+
+        @pl.when(first)
+        def _():
+            grad_left = dot_nn(grad.astype(BF16), right_ref[ch])
+            for c, r, kh in places:
+                at = slice(kh * LANES, (kh + 1) * LANES)
+                mine = grad_left[r * chips : (r + 1) * chips, at]
+                theirs = grad_left[(2 + r) * chips : (3 + r) * chips, at]
+                edges[every(ch * 8 + 4 * c + 2 * r + kh, chips, 16), :] = jnp.where(core == c, mine, theirs)
+
+        @pl.when(jnp.logical_not(first))
+        def _():
+            grad_right = dot_nn(jnp.transpose(grad).astype(BF16), left_ref[ch])
+            natural[: 4 * chips, :] = grad_right[:, :LANES]
+            natural[4 * chips :, :] = grad_right[:, LANES:]
+            for c, r, kh in places:
+                edges[every(ch * 8 + 4 * c + 2 * r + kh, chips, 16), :] = natural[
+                    every(kh * 4 * chips + 2 * c + r, chips, 4), :
+                ]
+
     edges_ref[...] = edges[...].astype(BF16)
 
 

time: 123 us -> 123 us (level)
  transfers between devices with their start and end apart: 7 -> 7, of which waited for: 4 -> 3; matrix products, arithmetic and copies ran while one was open for 0% -> 0% of each run, Pallas kernels for 3% -> 3%
where the time goes in v9:
time: 123 us
  blocking collectives  98.5 us (80%)
  starting transfers between devices  12.9 us (10%)
  Pallas kernels  7.32 us (6%)
  waiting for transfers between devices  2.99 us (2%)
    all_to_all x6, blocking collectives, on_device(): to_chips = lambda a: lax.all_to_all(a, CHIPS, 0, 0, tiled=True)  98.5 us
    ppermute x6, starting transfers between devices, on_device(): swap = lambda a: lax.ppermute(a, 'c', SWAP)  10.5 us
    pallas_call x12, Pallas kernels, run(): pl.pallas_call(body, out_shape=[jax.ShapeDtypeStruct(shape, dtype) for sh...  7.32 us
  transfers between devices with their start and end apart: 7, of which 3 were waited for; matrix products, arithmetic and copies ran while one was open for 0% of the time, Pallas kernels for 3%

profile of v9, /device:TPU:1, one launch (start us, length us, event | category | flops | bytes accessed | tf_op | source)
XLA Modules:
  0.0 122.5 jit_solution(11678945567807321480)
XLA Ops:
  0.6 1.6 %shard_map.152 = (bf16[1024,128]{1,0:T(8,128)(2,1)S(1)}, bf16[512,128]{1,0:T(8,128)(2,1)S(1)}, bf16[512,128]{1,0:T(8,128)(2,1)S(1)}, f32[8,128]{1,0:T(8,128)S(1)}) custom-call(bf16[512,128]{1,0:T(8,128)(2,1)} %bitcast.37, f32[1,128]{1,0:T(1,128)} %bitcast.43, f32[1,128]{1,0:T(1,128)} %bitcast.44, bf16[128,512]{1,0:T(8,128)(2,1)} %w_in_ref.1, ...), custom_call_target="tpu_custom_call" | custom-call | bytes 1048576 | tf_op jit(solution)/shard_map/pallas_call | solution.py:20
  2.2 0.0 copy-start.1
  2.3 0.0 copy-start.2
  2.3 0.0 copy-start.3
  2.3 0.0 copy-start.4
  2.3 24.3 %all_to_all.68 = bf16[64,16,128]{2,1,0:T(8,128)(2,1)S(1)} all-to-all(bf16[64,16,128]{2,1,0:T(8,128)(2,1)S(1)} %bitcast.36), channel_id=1, replica_groups=mesh['X'=2,'x'=2,'z'=8,'y'=4,'c'=2] {'x','z','y'}, dimensions={0} | all-to-all | bytes 524288 | tf_op jit(solution)/shard_map/all_to_all | solution.py:388
  26.6 3.4 %collective-permute-start = (bf16[1024,128]{1,0:T(8,128)(2,1)S(1)}, bf16[1024,128]{1,0:T(8,128)(2,1)S(1)}, u32[]{:S(2)}, u32[]{:S(2)}) collective-permute-start(bf16[1024,128]{1,0:T(8,128)(2,1)S(1)} %bitcast.25), channel_id=1, source_target_pairs={{0,1},{1,0},{2,3},{3,2},{4,5},{5,4},{6,7},{7,6},{8,9},{9,8},{10,11... | collective-permute-start | bytes 786440 | tf_op jit(solution)/shard_map/ppermute | solution.py:390
  30.0 0.0 copy-done.1
  30.0 0.0 collective-permute-start.1
  30.0 0.0 copy-done.2
  30.0 0.0 copy-done.3
  30.0 0.0 copy-done.4
  30.0 0.5 shard_map.153
  30.6 0.8 collective-permute-done.1.pair_ref
  31.4 0.0 collective-permute-done.other_ref
  31.4 0.6 shard_map.154
  32.0 14.3 %all_to_all.69 = bf16[64,8,128]{2,1,0:T(8,128)(2,1)S(1)} all-to-all(bf16[64,8,128]{2,1,0:T(8,128)(2,1)S(1)} %bitcast.41), channel_id=1, replica_groups=mesh['X'=2,'x'=2,'z'=8,'y'=4,'c'=2] {'x','z','y'}, dimensions={0} | all-to-all | bytes 262144 | tf_op jit(solution)/shard_map/all_to_all | solution.py:388
  46.2 0.2 shard_map.155
  46.4 14.7 %all_to_all.70 = bf16[64,8,128]{2,1,0:T(8,128)(2,1)S(1)} all-to-all(bf16[64,8,128]{2,1,0:T(8,128)(2,1)S(1)} %bitcast.33), channel_id=1, replica_groups=mesh['X'=2,'x'=2,'z'=8,'y'=4,'c'=2] {'x','z','y'}, dimensions={0} | all-to-all | bytes 262144 | tf_op jit(solution)/shard_map/all_to_all | solution.py:388
  61.1 2.5 %collective-permute-start.2 = (bf16[512,128]{1,0:T(8,128)(2,1)S(1)}, bf16[512,128]{1,0:T(8,128)(2,1)S(1)}, u32[]{:S(2)}, u32[]{:S(2)}) collective-permute-start(bf16[512,128]{1,0:T(8,128)(2,1)S(1)} %bitcast.34), channel_id=1, source_target_pairs={{0,1},{1,0},{2,3},{3,2},{4,5},{5,4},{6,7},{7,6},{8,9},{9,8},{10,11... | collective-permute-start | bytes 393224 | tf_op jit(solution)/shard_map/ppermute | solution.py:390
  63.6 0.6 shard_map.156
  64.2 0.1 collective-permute-start.3
  64.3 0.5 shard_map.157
  64.9 0.0 collective-permute-done.2.other_ref
  64.9 0.7 shard_map.158
  65.6 0.0 collective-permute-done.3.got_ref
  65.6 0.0 copy-start
  65.6 15.2 %all_to_all.71 = bf16[64,16,128]{2,1,0:T(8,128)(2,1)S(1)} all-to-all(bf16[64,16,128]{2,1,0:T(8,128)(2,1)S(1)} %bitcast.27), channel_id=1, replica_groups=mesh['X'=2,'x'=2,'z'=8,'y'=4,'c'=2] {'x','z','y'}, dimensions={0} | all-to-all | bytes 524288 | tf_op jit(solution)/shard_map/all_to_all | solution.py:388
  80.8 0.0 copy-done
  80.8 0.6 shard_map.159
  81.4 16.0 %all_to_all.72 = bf16[64,8,128]{2,1,0:T(8,128)(2,1)S(1)} all-to-all(bf16[64,8,128]{2,1,0:T(8,128)(2,1)S(1)} %bitcast.40), channel_id=1, replica_groups=mesh['X'=2,'x'=2,'z'=8,'y'=4,'c'=2] {'x','z','y'}, dimensions={0} | all-to-all | bytes 262144 | tf_op jit(solution)/shard_map/all_to_all | solution.py:388
  97.4 0.1 shard_map.160.share_ref
  97.5 2.8 %collective-permute-start.5 = (f32[128,512]{1,0:T(8,128)S(1)}, f32[128,512]{1,0:T(8,128)S(1)}, u32[]{:S(2)}, u32[]{:S(2)}) collective-permute-start(f32[128,512]{1,0:T(8,128)S(1)} %get-tuple-element.101), channel_id=1, source_target_pairs={{0,1},{1,0},{2,3},{3,2},{4,5},{5,4},{6,7},{7,6},{8,9},{9,8},{10,11... | collective-permute-start | bytes 786440 | tf_op jit(solution)/shard_map/ppermute | solution.py:390
  100.3 2.4 %collective-permute-start.4 = (f32[8,128]{1,0:T(8,128)S(1)}, f32[8,128]{1,0:T(8,128)S(1)}, u32[]{:S(2)}, u32[]{:S(2)}) collective-permute-start(f32[8,128]{1,0:T(8,128)S(1)} %shard_map.160.share_ref), channel_id=1, source_target_pairs={{0,129},{1,128},{128,1},{129,0},{2,131},{3,130},{130,3},{131,2},{4... | collective-permute-start | bytes 12296 | tf_op jit(solution)/shard_map/ppermute | solution.py:445
  102.7 0.0 collective-permute-done.5.got_ref
  102.7 1.0 shard_map.161
  103.6 1.2 collective-permute-done.4.got_ref
  104.8 0.2 shard_map.162
  105.0 14.0 %all_to_all.73 = bf16[64,8,128]{2,1,0:T(8,128)(2,1)S(1)} all-to-all(bf16[64,8,128]{2,1,0:T(8,128)(2,1)S(1)} %bitcast.31), channel_id=1, replica_groups=mesh['X'=2,'x'=2,'z'=8,'y'=4,'c'=2] {'x','z','y'}, dimensions={0} | all-to-all | bytes 262144 | tf_op jit(solution)/shard_map/all_to_all | solution.py:388
  119.0 1.8 %collective-permute-start.6 = (bf16[512,128]{1,0:T(8,128)(2,1)S(1)}, bf16[512,128]{1,0:T(8,128)(2,1)S(1)}, u32[]{:S(2)}, u32[]{:S(2)}) collective-permute-start(bf16[512,128]{1,0:T(8,128)(2,1)S(1)} %bitcast.29), channel_id=1, source_target_pairs={{0,1},{1,0},{2,3},{3,2},{4,5},{5,4},{6,7},{7,6},{8,9},{9,8},{10,11... | collective-permute-start | bytes 393224 | tf_op jit(solution)/shard_map/ppermute | solution.py:390
  120.7 1.0 collective-permute-done.6.other_ref
  121.7 0.8 shard_map.163
Async XLA Ops:
  2.2 27.8 %copy-start.1 = (bf16[1,2,256,128]{3,2,1,0:T(8,128)(2,1)S(1)}, bf16[1,2,256,128]{3,2,1,0:T(8,128)(2,1)}, u32[]{:S(2)}) copy-start(bf16[1,2,256,128]{3,2,1,0:T(8,128)(2,1)} %param.9) | copy-start | bytes 393220
  2.3 27.8 %copy-start.2 = (bf16[128,128]{1,0:T(8,128)(2,1)S(1)}, bf16[128,128]{1,0:T(8,128)(2,1)}, u32[]{:S(2)}) copy-start(bf16[128,128]{1,0:T(8,128)(2,1)} %w_gate_ref.3) | copy-start | bytes 98308
  2.3 27.8 %copy-start.3 = (bf16[128,128]{1,0:T(8,128)(2,1)S(1)}, bf16[128,128]{1,0:T(8,128)(2,1)}, u32[]{:S(2)}) copy-start(bf16[128,128]{1,0:T(8,128)(2,1)} %w_out_ref.3) | copy-start | bytes 98308
  2.3 27.8 %copy-start.4 = (bf16[1,2,256,128]{3,2,1,0:T(8,128)(2,1)S(1)}, bf16[1,2,256,128]{3,2,1,0:T(8,128)(2,1)}, u32[]{:S(2)}) copy-start(bf16[1,2,256,128]{3,2,1,0:T(8,128)(2,1)} %param.10) | copy-start | bytes 393220
  26.6 4.8 %collective-permute-start = (bf16[1024,128]{1,0:T(8,128)(2,1)S(1)}, bf16[1024,128]{1,0:T(8,128)(2,1)S(1)}, u32[]{:S(2)}, u32[]{:S(2)}) collective-permute-start(bf16[1024,128]{1,0:T(8,128)(2,1)S(1)} %bitcast.25), channel_id=1, source_target_pairs={{0,1},{1,0},{2,3},{3,2},{4,5},{5,4},{6,7},{7,6},{8,9},{9,8},{10,11... | collective-permute-start | bytes 786440 | tf_op jit(solution)/shard_map/ppermute | solution.py:390
  30.0 1.3 %collective-permute-start.1 = (bf16[512,128]{1,0:T(8,128)(2,1)S(1)}, bf16[512,128]{1,0:T(8,128)(2,1)S(1)}, u32[]{:S(2)}, u32[]{:S(2)}) collective-permute-start(bf16[512,128]{1,0:T(8,128)(2,1)S(1)} %bitcast.38), channel_id=1, source_target_pairs={{0,1},{1,0},{2,3},{3,2},{4,5},{5,4},{6,7},{7,6},{8,9},{9,8},{10,11... | collective-permute-start | bytes 393224 | tf_op jit(solution)/shard_map/ppermute | solution.py:390
  61.1 3.7 %collective-permute-start.2 = (bf16[512,128]{1,0:T(8,128)(2,1)S(1)}, bf16[512,128]{1,0:T(8,128)(2,1)S(1)}, u32[]{:S(2)}, u32[]{:S(2)}) collective-permute-start(bf16[512,128]{1,0:T(8,128)(2,1)S(1)} %bitcast.34), channel_id=1, source_target_pairs={{0,1},{1,0},{2,3},{3,2},{4,5},{5,4},{6,7},{7,6},{8,9},{9,8},{10,11... | collective-permute-start | bytes 393224 | tf_op jit(solution)/shard_map/ppermute | solution.py:390
  64.2 1.4 %collective-permute-start.3 = (f32[128,128]{1,0:T(8,128)S(1)}, f32[128,128]{1,0:T(8,128)S(1)}, u32[]{:S(2)}, u32[]{:S(2)}) collective-permute-start(f32[128,128]{1,0:T(8,128)S(1)} %get-tuple-element.88), channel_id=1, source_target_pairs={{0,1},{1,0},{2,3},{3,2},{4,5},{5,4},{6,7},{7,6},{8,9},{9,8},{10,11... | collective-permute-start | bytes 196616 | tf_op jit(solution)/shard_map/ppermute | solution.py:390
  65.6 15.2 %copy-start = (bf16[128,512]{1,0:T(8,128)(2,1)S(1)}, bf16[128,512]{1,0:T(8,128)(2,1)}, u32[]{:S(2)}) copy-start(bf16[128,512]{1,0:T(8,128)(2,1)} %w_in_ref.1) | copy-start | bytes 393220
  97.5 5.1 %collective-permute-start.5 = (f32[128,512]{1,0:T(8,128)S(1)}, f32[128,512]{1,0:T(8,128)S(1)}, u32[]{:S(2)}, u32[]{:S(2)}) collective-permute-start(f32[128,512]{1,0:T(8,128)S(1)} %get-tuple-element.101), channel_id=1, source_target_pairs={{0,1},{1,0},{2,3},{3,2},{4,5},{5,4},{6,7},{7,6},{8,9},{9,8},{10,11... | collective-permute-start | bytes 786440 | tf_op jit(solution)/shard_map/ppermute | solution.py:390
  100.3 4.6 %collective-permute-start.4 = (f32[8,128]{1,0:T(8,128)S(1)}, f32[8,128]{1,0:T(8,128)S(1)}, u32[]{:S(2)}, u32[]{:S(2)}) collective-permute-start(f32[8,128]{1,0:T(8,128)S(1)} %shard_map.160.share_ref), channel_id=1, source_target_pairs={{0,129},{1,128},{128,1},{129,0},{2,131},{3,130},{130,3},{131,2},{4... | collective-permute-start | bytes 12296 | tf_op jit(solution)/shard_map/ppermute | solution.py:445
  119.0 2.7 %collective-permute-start.6 = (bf16[512,128]{1,0:T(8,128)(2,1)S(1)}, bf16[512,128]{1,0:T(8,128)(2,1)S(1)}, u32[]{:S(2)}, u32[]{:S(2)}) collective-permute-start(bf16[512,128]{1,0:T(8,128)(2,1)S(1)} %bitcast.29), channel_id=1, source_target_pairs={{0,1},{1,0},{2,3},{3,2},{4,5},{5,4},{6,7},{7,6},{8,9},{9,8},{10,11... | collective-permute-start | bytes 393224 | tf_op jit(solution)/shard_map/ppermute | solution.py:390
